TPU v7x, 32 devices: a whole 2x2x4 slice. The times are simulated.
32 devices in a mesh: dp: 4 (over x, core), expert: 8 (over z, y).
Axes of the slice: x: 2, y: 2, z: 4, core: 2. Of those that a mesh axis runs over, the one named last changes fastest.
Arguments:
- query: bfloat16 [2, 2048, 2560], P(None, ('dp', 'expert')), may hold values from -24 to 24
- keys: bfloat16 [2, 2048, 512], P(None, ('dp', 'expert')), may hold values from -4 to 4
- values: bfloat16 [2, 2048, 512], P(None, ('dp', 'expert')), may hold values from -6 to 6
- lengths: int32 [2, 32, 4], P(None, ('dp', 'expert')), may hold values from 0 to 64, as said below
- routes: int32 [2, 2048, 6], P(None, ('dp', 'expert')), may hold values from 0 to 7, as said below
- gates: float32 [2, 2048, 6], P(None, ('dp', 'expert')), may hold values from 0.05 to 0.4
- norm_gain: float32 [2560], replicated, may hold values from 0.1 to 1.9
- old_holds: int32 [8], replicated, may hold values from 0 to 7, as said below
- dup_experts: int32 [4], replicated, may hold values from 0 to 7, as said below
- w_gate: bfloat16 [8, 2560, 768], P('expert'), may hold values from -0.125 to 0.125
- w_up: bfloat16 [8, 2560, 768], P('expert'), may hold values from -0.125 to 0.125
- w_down: bfloat16 [8, 768, 2560], P('expert'), may hold values from -0.21875 to 0.21875
Outputs:
- layer_out: bfloat16 [2, 2048, 2560], P(None, ('dp', 'expert'))
Inputs may be any that keep to these rules, and one draw needn't show every extreme that they name: Each length is a multiple of 8; the 4 lengths of one device in one batch add up to 64. `routes`: each token names 6 different experts. `dup_experts`: 4 different experts. `old_holds`: each expert stands in exactly one slot.
All inputs are finite; a program needn't handle non-finite values.
Results may differ from a plain program's by a relative error of at most 0.0061.
Values may be sent and summed in bfloat16 or wider, within the bound.
No kernel may reach another device: no remote copies, remote signals or barrier semaphores. Data moves between devices by JAX's collectives and lax.ppermute only.
A program may use at most 128 MiB of HBM per device.

v0:
```python
import jax
import jax.numpy as jnp
from jax import lax
from jax.sharding import PartitionSpec as P

HEAD_WIDTH = 128
CAP = 6


def from_behind(value, axis, steps):
    count = lax.axis_size(axis)
    pairs = [(source, (source + steps) % count) for source in range(count)]
    return lax.ppermute(value, axis, pairs)


def attend(query, key_rows, value_rows, lengths):
    rows = query.shape[0]
    kv_heads = key_rows.shape[1] // HEAD_WIDTH
    query_group = query.shape[1] // HEAD_WIDTH // kv_heads
    ends = jnp.cumsum(lengths)
    position = lax.iota(jnp.int32, rows)
    request = jnp.sum((position[:, None] >= ends[None, :]).astype(jnp.int32), axis=1)
    allowed = (request[:, None] == request[None, :]) & (position[None, :] <= position[:, None])
    query_heads = query.reshape(rows, kv_heads, query_group, HEAD_WIDTH)
    key_heads = key_rows.reshape(rows, kv_heads, HEAD_WIDTH)
    value_heads = value_rows.reshape(rows, kv_heads, HEAD_WIDTH)
    router_logits = jnp.einsum(
        "qhgd,khd->hgqk", query_heads, key_heads, preferred_element_type=jnp.float32
    ) * HEAD_WIDTH ** (-0.5)
    router_logits = jnp.where(allowed[None, None], router_logits, -1e30)
    highest = jnp.max(router_logits, axis=-1, keepdims=True)
    weights = jnp.exp(router_logits - highest)
    probs = (weights / jnp.sum(weights, axis=-1, keepdims=True)).astype(jnp.bfloat16)
    mixed = jnp.einsum("hgqk,khd->qhgd", probs, value_heads, preferred_element_type=jnp.float32)
    return mixed.reshape(rows, kv_heads * query_group * HEAD_WIDTH)


def normalize(attn, gain):
    meansq = jnp.mean(attn * attn, axis=-1, keepdims=True)
    return (attn * lax.rsqrt(meansq + 1e-05) * gain).astype(jnp.bfloat16)


def expert_rows(rows, gate_mat, up_mat, down_mat):
    gate_val = jnp.dot(rows, gate_mat, preferred_element_type=jnp.float32)
    up_val = jnp.dot(rows, up_mat, preferred_element_type=jnp.float32)
    hidden = (jax.nn.silu(gate_val) * up_val).astype(jnp.bfloat16)
    return jnp.dot(hidden, down_mat, preferred_element_type=jnp.float32).astype(jnp.bfloat16)


def routing(routes, copies_of, first_target, second_target, regions):
    expert_list = lax.iota(jnp.int32, copies_of.shape[0])
    hit = (routes[:, :, None] == expert_list[None, None, :]).astype(jnp.int32)
    named = jnp.sum(hit, axis=1)
    before = jnp.cumsum(named, axis=0) - named
    place = jnp.sum(hit * before[:, None, :], axis=2)
    limit = jnp.sum(hit * copies_of[None, None, :], axis=2)
    kept = place < limit * CAP
    which = place // CAP
    target = jnp.where(
        which == 0,
        jnp.sum(hit * first_target[None, None, :], axis=2),
        jnp.sum(hit * second_target[None, None, :], axis=2),
    )
    flat = (target * regions + which) * CAP + place % CAP
    return (flat, kept)


def pack(normed, flat, kept, slots):
    tok_rows = normed.shape[0]
    token = jnp.broadcast_to(lax.iota(jnp.int32, tok_rows)[:, None], flat.shape)
    spot = jnp.where(kept, flat, slots)
    source_row = jnp.full((slots,), tok_rows, jnp.int32).at[spot].set(token, mode="drop")
    padded = jnp.concatenate([normed, jnp.zeros((1, normed.shape[1]), normed.dtype)], axis=0)
    return (padded[source_row], spot)


def combine(attn, returned, spot, kept, gates):
    picked = returned[jnp.minimum(spot, returned.shape[0] - 1)]
    weight = jnp.where(kept, gates, 0.0)
    mixed = jnp.einsum("tk,tkd->td", weight, picked.astype(jnp.float32))
    return (attn + mixed).astype(jnp.bfloat16)


def shards(
    query,
    keys,
    values,
    lengths,
    routes,
    gates,
    norm_gain,
    old_holds,
    dup_experts,
    w_gate,
    w_up,
    w_down,
):
    width = lax.axis_size("expert")
    half = width // 2
    features = norm_gain.shape[0]
    expert_list = lax.iota(jnp.int32, old_holds.shape[0])
    holder = jnp.sum(
        expert_list[:, None] * (old_holds[:, None] == expert_list[None, :]).astype(jnp.int32),
        axis=0,
    )
    doubled = jnp.sum((dup_experts[:, None] == expert_list[None, :]).astype(jnp.int32), axis=0)
    own_gate, own_up, own_down = (w_gate[0], w_up[0], w_down[0])
    moved = from_behind((w_gate, w_up, w_down), "expert", half)
    extra_gate, extra_up, extra_down = (moved[0][0], moved[1][0], moved[2][0])
    spare = (holder + half) % width
    position_now = lax.axis_index("expert")
    serving = jnp.sum(doubled * (spare == position_now).astype(jnp.int32)) > 0
    attn_one = attend(query[0], keys[0], values[0], lengths[0, 0])
    normed_one = normalize(attn_one, norm_gain)
    flat_one, kept_one = routing(routes[0], jnp.ones_like(doubled), holder, holder, 1)
    packed_one, spot_one = pack(normed_one, flat_one, kept_one, width * CAP)
    received = lax.all_to_all(
        packed_one.reshape(width, 1, CAP, features),
        "expert",
        split_axis=0,
        concat_axis=0,
        tiled=True,
    )
    result = expert_rows(received.reshape(-1, features), own_gate, own_up, own_down)
    back_one = lax.all_to_all(
        result.reshape(received.shape), "expert", split_axis=0, concat_axis=0, tiled=True
    )
    out_one = combine(attn_one, back_one.reshape(-1, features), spot_one, kept_one, gates[0])
    attn_two = attend(query[1], keys[1], values[1], lengths[1, 0])
    normed_two = normalize(attn_two, norm_gain)
    flat_two, kept_two = routing(routes[1], 1 + doubled, holder, spare, 2)
    packed_two, spot_two = pack(normed_two, flat_two, kept_two, width * 2 * CAP)
    received = lax.all_to_all(
        packed_two.reshape(width, 2, CAP, features),
        "expert",
        split_axis=0,
        concat_axis=0,
        tiled=True,
    )
    first_rows = received[:, 0]
    second_rows = received[:, 1]
    first_out = expert_rows(first_rows.reshape(-1, features), own_gate, own_up, own_down)
    second_flat = second_rows.reshape(-1, features)
    second_out = lax.cond(
        serving,
        lambda rows_in: expert_rows(rows_in, extra_gate, extra_up, extra_down),
        lambda rows_in: jnp.zeros_like(rows_in),
        second_flat,
    )
    result = jnp.stack(
        [first_out.reshape(first_rows.shape), second_out.reshape(second_rows.shape)], axis=1
    )
    back_two = lax.all_to_all(result, "expert", split_axis=0, concat_axis=0, tiled=True)
    out_two = combine(attn_two, back_two.reshape(-1, features), spot_two, kept_two, gates[1])
    return jnp.stack([out_one, out_two])


def solution(mesh):
    placed = (
        P(None, ("dp", "expert"), None),
        P(None, ("dp", "expert"), None),
        P(None, ("dp", "expert"), None),
        P(None, ("dp", "expert"), None),
        P(None, ("dp", "expert"), None),
        P(None, ("dp", "expert"), None),
        P(),
        P(),
        P(),
        P("expert", None, None),
        P("expert", None, None),
        P("expert", None, None),
    )
    return jax.shard_map(
        shards,
        mesh=mesh,
        in_specs=placed,
        out_specs=P(None, ("dp", "expert"), None),
        check_vma=False,
    )
```

profile of v0, /device:TPU:0, one launch (start us, length us, event | category | flops | bytes accessed | tf_op | source)
XLA Modules:
  0.0 611.1 jit_solution(16484302962209181392)
XLA Ops:
  0.0 4.0 collective-permute-start
  4.1 2.9 collective-permute-start.2
  7.0 1.1 fusion.136
  17.2 2.9 scatter_custom_fusion
  21.9 3.8 all-to-all-start
  25.8 491.8 %all-to-all-done = bf16[8,1,6,2560]{3,2,1,0:T(8,128)(2,1)S(1)} async-done(((bf16[8,1,6,2560]{3,2,1,0:T(8,128)(2,1)}), bf16[8,1,6,2560]{3,2,1,0:T(8,128)(2,1)S(1)}, u32[]{:S(2)}, u32[]{:S(2)}) %all-to-all-start) | async-done | bytes 245792 | tf_op jit(solution)/shard_map/all_to_all | solution.py:117
  517.6 2.9 fusion.36
  520.5 5.0 fusion.38
  526.4 5.8 all-to-all-start.1
  532.6 2.9 scatter_custom_fusion.1
  536.7 1.2 copy.92
  537.8 4.8 all-to-all-done.1
  542.6 4.3 all-to-all-start.2
  548.1 2.6 gather_fusion.1
  550.8 2.3 reshape.468
  553.1 7.2 %all-to-all-done.2 = bf16[8,2,6,2560]{3,1,2,0:T(2,128)(2,1)} async-done(((bf16[8,2,6,2560]{3,1,2,0:T(2,128)(2,1)}), bf16[8,2,6,2560]{3,1,2,0:T(2,128)(2,1)}, u32[]{:S(2)}, u32[]{:S(2)}) %all-to-all-start.2) | async-done | bytes 491552 | tf_op jit(solution)/shard_map/all_to_all | solution.py:133
  560.2 2.3 slice_reduce_fusion
  562.7 2.9 fusion.34
  565.6 5.0 fusion.41
  571.4 10.0 %conditional.1 = (bf16[8,1,6,2560]{3,2,0,1:T(8,128)(2,1)}) conditional(s32[]{:T(128)} %convert_element_type.72, () %tuple.13, (bf16[8,2,6,2560]{3,1,2,0:T(2,128)(2,1)}, bf16[1,2560,768]{2,1,0:T(8,128)(2,1)}, bf16[1,2560,768]{2,1,0:T(8,128)(2,1)}, bf16[1,768,2560]{2,1,0:T(8,128)(2,1)}) %tuple.14), branch_computations={%region_26.27_spmd, %region_27.28_spmd} | conditional | flops 566575104 | bytes 15286280 | solution.py:144
  571.5 1.1 copy.93
  572.7 2.9 fusion.4
  575.6 5.0 fusion.6
  581.4 1.4 pad_maximum_fusion
  582.8 1.3 copy.94
  584.1 4.1 all-to-all-start.3
  589.1 1.9 fusion.70
  591.0 10.4 %all-to-all-done.3 = bf16[8,2,6,2560]{3,1,2,0:T(2,128)(2,1)} async-done(((bf16[8,2,6,2560]{3,1,2,0:T(2,128)(2,1)}), bf16[8,2,6,2560]{3,1,2,0:T(2,128)(2,1)}, u32[]{:S(2)}, u32[]{:S(2)}) %all-to-all-start.3) | async-done | bytes 491552 | tf_op jit(solution)/shard_map/all_to_all | solution.py:153
  601.4 1.1 copy.95
  602.6 2.6 gather_fusion.3
  605.3 2.3 reshape.484
  607.5 2.6 fusion.152
  (108 shorter events, 17.6 us)
Async XLA Ops:
  0.0 571.4 %collective-permute-start = (bf16[1,2560,768]{2,1,0:T(8,128)(2,1)}, bf16[1,2560,768]{2,1,0:T(8,128)(2,1)}, u32[]{:S(2)}, u32[]{:S(2)}) collective-permute-start(bf16[1,2560,768]{2,1,0:T(8,128)(2,1)} %param.23), channel_id=1, source_target_pairs={{0,4},{1,5},{2,6},{3,7},{4,0},{5,1},{6,2},{7,3},{8,12},{9,13},{10,... | collective-permute-start | bytes 11796488 | tf_op jit(solution)/shard_map/ppermute | solution.py:13
  4.0 567.4 %collective-permute-start.1 = (bf16[1,2560,768]{2,1,0:T(8,128)(2,1)}, bf16[1,2560,768]{2,1,0:T(8,128)(2,1)}, u32[]{:S(2)}, u32[]{:S(2)}) collective-permute-start(bf16[1,2560,768]{2,1,0:T(8,128)(2,1)} %param.24), channel_id=1, source_target_pairs={{0,4},{1,5},{2,6},{3,7},{4,0},{5,1},{6,2},{7,3},{8,12},{9,13},{10,... | collective-permute-start | bytes 11796488 | tf_op jit(solution)/shard_map/ppermute | solution.py:13
  4.1 567.4 %collective-permute-start.2 = (bf16[1,768,2560]{2,1,0:T(8,128)(2,1)}, bf16[1,768,2560]{2,1,0:T(8,128)(2,1)}, u32[]{:S(2)}, u32[]{:S(2)}) collective-permute-start(bf16[1,768,2560]{2,1,0:T(8,128)(2,1)} %param.25), channel_id=1, source_target_pairs={{0,4},{1,5},{2,6},{3,7},{4,0},{5,1},{6,2},{7,3},{8,12},{9,13},{10,... | collective-permute-start | bytes 11796488 | tf_op jit(solution)/shard_map/ppermute | solution.py:13
  8.1 5.0 copy-start.5
  8.1 5.5 copy-start.7
  8.1 5.6 copy-start.8
  8.5 6.5 %copy-start.3 = (bf16[2,64,512]{2,1,0:T(8,128)(2,1)S(1)}, bf16[2,64,512]{2,1,0:T(8,128)(2,1)}, u32[]{:S(2)}) copy-start(bf16[2,64,512]{2,1,0:T(8,128)(2,1)} %param.16) | copy-start | bytes 393220
  15.9 4.2 copy-start.4
  16.1 4.2 copy-start.1
  21.9 495.6 %all-to-all-start = ((bf16[8,1,6,2560]{3,2,1,0:T(8,128)(2,1)}), bf16[8,1,6,2560]{3,2,1,0:T(8,128)(2,1)S(1)}, u32[]{:S(2)}, u32[]{:S(2)}) async-start(bf16[8,1,6,2560]{3,2,1,0:T(8,128)(2,1)} %bitcast.17), calls=%async_computation | async-start | bytes 655360 | tf_op jit(solution)/shard_map/all_to_all | solution.py:117
  526.4 16.2 %all-to-all-start.1 = ((bf16[8,1,6,2560]{3,2,1,0:T(8,128)(2,1)}), bf16[8,1,6,2560]{3,2,1,0:T(8,128)(2,1)S(1)}, u32[]{:S(2)}, u32[]{:S(2)}) async-start(bf16[8,1,6,2560]{3,2,1,0:T(8,128)(2,1)} %bitcast.21), calls=%async_computation.1 | async-start | bytes 655360 | tf_op jit(solution)/shard_map/all_to_all | solution.py:125
  535.6 11.3 %copy-start.6 = (f32[2,64,6]{1,0,2:T(2,128)S(1)}, f32[2,64,6]{1,0,2:T(2,128)}, u32[]{:S(2)}) copy-start(f32[2,64,6]{1,0,2:T(2,128)} %param.19) | copy-start | bytes 9220
  542.6 17.6 %all-to-all-start.2 = ((bf16[8,2,6,2560]{3,1,2,0:T(2,128)(2,1)}), bf16[8,2,6,2560]{3,1,2,0:T(2,128)(2,1)}, u32[]{:S(2)}, u32[]{:S(2)}) async-start(bf16[8,2,6,2560]{3,1,2,0:T(2,128)(2,1)} %copy.92), calls=%async_computation.2 | async-start | bytes 983040 | tf_op jit(solution)/shard_map/all_to_all | solution.py:133
  581.4 6.8 %copy-start = (bf16[64,6,2560]{2,1,0:T(8,128)(2,1)S(1)}, bf16[64,6,2560]{2,1,0:T(8,128)(2,1)}, u32[]{:S(2)}) copy-start(bf16[64,6,2560]{2,1,0:T(8,128)(2,1)} %reshape.468) | copy-start | bytes 5898244
  584.1 17.2 %all-to-all-start.3 = ((bf16[8,2,6,2560]{3,1,2,0:T(2,128)(2,1)}), bf16[8,2,6,2560]{3,1,2,0:T(2,128)(2,1)}, u32[]{:S(2)}, u32[]{:S(2)}) async-start(bf16[8,2,6,2560]{3,1,2,0:T(2,128)(2,1)} %copy.94), calls=%async_computation.3 | async-start | bytes 983040 | tf_op jit(solution)/shard_map/all_to_all | solution.py:153
  605.3 4.9 copy-start.2
where the time goes:
time: 612 us; the launch traced here: 611 us
  waiting for transfers between devices  514 us (84%)
  local copies, waits for them, and re-layouts  34.7 us (6%)
  matrix products  29.7 us (5%)
  starting transfers between devices  25 us (4%)
  other arithmetic  6.36 us (1%)
    all_to_all x1, waiting for transfers between devices, shards(): lax.all_to_all(packed_one.reshape(width, 1, CAP, features), 'expert', spl...  492 us
    dot_general x3, matrix products, expert_rows(): jnp.dot(hidden, down_mat, preferred_element_type=jnp.float32)  15 us
  transfers between devices with their start and end apart: 7, of which 4 were waited for; matrix products, arithmetic and copies ran while one was open for 8% of the time, Pallas kernels for 0%

commit v1 on v0

v1 whole, which is shorter than its diff:
```python
import functools

import jax
import jax.numpy as jnp
from jax import lax
from jax.experimental import pallas as pl
from jax.experimental.pallas import tpu as pltpu
from jax.sharding import PartitionSpec as P

HEAD_WIDTH = 128
CAP = 6
PACK = 8
SPLIT = CAP // (PACK - CAP)
GROUPS = 3
VMEM_LIMIT = 56 * 1024 * 1024

F32 = jnp.float32
BF16 = jnp.bfloat16


def dot(a, b, dims=((1,), (0,))):
    return lax.dot_general(a, b, (dims, ((), ())), preferred_element_type=F32)


def row_iota(shape, axis):
    return lax.broadcasted_iota(jnp.int32, shape, axis)


def count_steps(value, step, upto):
    total = jnp.zeros_like(value)
    for at in range(1, upto):
        total = total + (value >= step * at).astype(jnp.int32)
    return total


def slot_picks(width, holds_ref, dup_ref, routes_ref):
    _, batches, tokens = routes_ref.shape
    lanes = batches * tokens
    rows = width * GROUPS * PACK
    shape = (rows, lanes)
    row = row_iota(shape, 0)
    lane = row_iota(shape, 1)
    slot = count_steps(row, GROUPS * PACK, width)
    within = row - slot * (GROUPS * PACK)
    group = count_steps(within, PACK, GROUPS)
    place = within - group * PACK
    expert = jnp.zeros(shape, jnp.int32)
    for at in range(width):
        expert = jnp.where(slot == at, holds_ref[at], expert)
    doubled = jnp.zeros(shape, jnp.bool_)
    for at in range(dup_ref.shape[0]):
        doubled = doubled | (expert == dup_ref[at])
    batch = (lane >= tokens).astype(jnp.int32)
    allowed = (batch == (group >= 1).astype(jnp.int32)) & (doubled | (group < 2))
    routes = routes_ref[...]
    routes = jnp.concatenate([routes[:, at, :] for at in range(batches)], axis=1)
    named = [routes[k : k + 1, :] == expert for k in range(routes.shape[0])]
    hit = functools.reduce(jnp.logical_or, named)
    earlier = row_iota((lanes, lanes), 0)
    later = row_iota((lanes, lanes), 1)
    same = (earlier >= tokens) == (later >= tokens)
    before_mat = jnp.where((earlier < later) & same, 1.0, 0.0).astype(BF16)
    before = dot(jnp.where(hit, 1.0, 0.0).astype(BF16), before_mat).astype(jnp.int32)
    before = before - jnp.where(group == 2, CAP, 0)
    live = hit & allowed
    lead = live & (place < CAP) & (before == place)
    trail = [
        live & (place >= CAP) & (before == (place - CAP) * SPLIT + piece) for piece in range(SPLIT)
    ]
    return lead, trail, named


def attend(query_ref, key_ref, value_ref, lengths_ref, batch, attn_ref):
    tokens = query_ref.shape[1]
    kv_heads = key_ref.shape[2] // HEAD_WIDTH
    group = query_ref.shape[2] // HEAD_WIDTH // kv_heads
    at_row = row_iota((tokens, tokens), 0)
    at_col = row_iota((tokens, tokens), 1)
    row_request = jnp.zeros((tokens, tokens), jnp.int32)
    col_request = jnp.zeros((tokens, tokens), jnp.int32)
    end = jnp.int32(0)
    for r in range(lengths_ref.shape[2]):
        end = end + lengths_ref[batch, 0, r]
        row_request = row_request + (at_row >= end).astype(jnp.int32)
        col_request = col_request + (at_col >= end).astype(jnp.int32)
    allowed = (row_request == col_request) & (at_col <= at_row)
    squares = jnp.zeros((tokens, HEAD_WIDTH), F32)
    for h in range(kv_heads):
        kv = slice(h * HEAD_WIDTH, (h + 1) * HEAD_WIDTH)
        heads = [
            slice((h * group + g) * HEAD_WIDTH, (h * group + g + 1) * HEAD_WIDTH)
            for g in range(group)
        ]
        q = jnp.concatenate([query_ref[batch, :, cols] for cols in heads], axis=0)
        scores = dot(q, key_ref[batch, :, kv], ((1,), (1,))) * HEAD_WIDTH ** (-0.5)
        scores = scores.reshape(group, tokens, tokens)
        scores = jnp.where(allowed[None], scores, -1e30)
        weights = jnp.exp(scores - jnp.max(scores, axis=-1, keepdims=True))
        probs = (weights / jnp.sum(weights, axis=-1, keepdims=True)).astype(BF16)
        mixed = dot(probs.reshape(group * tokens, tokens), value_ref[batch, :, kv])
        for g, cols in enumerate(heads):
            part = mixed[g * tokens : (g + 1) * tokens]
            attn_ref[batch, :, cols] = part
            squares = squares + part * part
    meansq = jnp.sum(squares, axis=-1, keepdims=True) / query_ref.shape[2]
    return lax.rsqrt(meansq + 1e-05)


def front_kernel(
    lengths_ref,
    holds_ref,
    dup_ref,
    query_ref,
    key_ref,
    value_ref,
    routes_ref,
    gain_ref,
    attn_ref,
    send_ref,
    normed_ref,
):
    batches, tokens, features = query_ref.shape
    cols = send_ref.shape[1]
    step = cols // SPLIT
    for b in range(batches):
        scale = attend(query_ref, key_ref, value_ref, lengths_ref, b, attn_ref)
        normed_ref[b * tokens : (b + 1) * tokens, :] = (
            attn_ref[b] * scale * gain_ref[...]
        ).astype(BF16)
    width = send_ref.shape[0] // (GROUPS * PACK)
    lead, trail, _ = slot_picks(width, holds_ref, dup_ref, routes_ref)
    tail = normed_ref[:, cols:features]
    for j in range(SPLIT):
        at = slice(j * step, (j + 1) * step)
        picks = jnp.concatenate([lead, trail[j]], axis=1)
        picks = jnp.where(picks, 1.0, 0.0).astype(BF16)
        source = jnp.concatenate([normed_ref[:, at], tail], axis=0)
        send_ref[:, at] = dot(picks, source).astype(BF16)


def weights_kernel(holds_ref, dup_ref, routes_ref, gates_ref, mix_ref):
    width = mix_ref.shape[1] // (GROUPS * PACK)
    lead, trail, named = slot_picks(width, holds_ref, dup_ref, routes_ref)
    gates = gates_ref[...]
    gates = jnp.concatenate([gates[:, at, :] for at in range(gates.shape[1])], axis=1)
    gate = jnp.zeros(lead.shape, F32)
    for k, match in enumerate(named):
        gate = gate + jnp.where(match, gates[k : k + 1, :], 0.0)
    lanes = lead.shape[1]
    for j in range(SPLIT):
        for part, pick in enumerate((lead, trail[j])):
            weight = jnp.where(pick, gate, 0.0)
            high = weight.astype(BF16)
            low = (weight - high.astype(F32)).astype(BF16)
            mix_ref[j, :, (2 * part) * lanes : (2 * part + 1) * lanes] = high
            mix_ref[j, :, (2 * part + 1) * lanes : (2 * part + 2) * lanes] = low


def expert_kernel(got_ref, gate_ref, up_ref, down_ref, back_ref, rows_ref, total_ref):
    rows, cols = got_ref.shape
    features = rows_ref.shape[1]
    step = cols // SPLIT
    chunk = pl.program_id(1)
    shape = (rows, rows)
    row = row_iota(shape, 0)
    other = row_iota(shape, 1)
    tile = row - lax.rem(row, PACK)
    place = row - tile

    def trails(j):
        picked = jnp.zeros(shape, jnp.bool_)
        for a in range(PACK - CAP):
            picked = picked | ((place == a * SPLIT + j) & (other == tile + CAP + a))
        return jnp.where(picked, 1.0, 0.0).astype(BF16)

    @pl.when(chunk == 0)
    def _():
        rows_ref[:, :cols] = got_ref[...]
        tail = jnp.zeros((rows, features - cols), F32)
        for j in range(SPLIT):
            tail = tail + dot(trails(j), got_ref[:, j * step : (j + 1) * step])
        rows_ref[:, cols:] = tail.astype(BF16)
        total_ref[...] = jnp.zeros_like(total_ref)

    gate_val = dot(rows_ref[...], gate_ref[0])
    up_val = dot(rows_ref[...], up_ref[0])
    hidden = (gate_val / (1.0 + jnp.exp(-gate_val)) * up_val).astype(BF16)
    total_ref[...] += dot(hidden, down_ref[0])

    @pl.when(chunk == pl.num_programs(1) - 1)
    def _():
        tail = total_ref[:, cols:].astype(BF16)
        leading = lax.rem(row_iota((rows, step), 0), PACK) < CAP
        for j in range(SPLIT):
            at = slice(j * step, (j + 1) * step)
            moved = dot(trails(j), tail, ((0,), (0,)))
            back_ref[:, at] = jnp.where(leading, total_ref[:, at], moved).astype(BF16)


def combine_kernel(attn_ref, mix_ref, back_ref, out_ref):
    batches, tokens, features = attn_ref.shape
    lanes = batches * tokens
    cols = back_ref.shape[1]
    step = cols // SPLIT
    tail = jnp.zeros((lanes, features - cols), F32)
    for j in range(SPLIT):
        at = slice(j * step, (j + 1) * step)
        mixed = dot(mix_ref[j], back_ref[:, at], ((0,), (0,)))
        lead = mixed[:lanes] + mixed[lanes : 2 * lanes]
        tail = tail + (mixed[2 * lanes : 3 * lanes] + mixed[3 * lanes :])
        for b in range(batches):
            out_ref[b, :, at] = (attn_ref[b, :, at] + lead[b * tokens : (b + 1) * tokens]).astype(
                BF16
            )
    for b in range(batches):
        out_ref[b, :, cols:] = (
            attn_ref[b, :, cols:] + tail[b * tokens : (b + 1) * tokens]
        ).astype(BF16)


def in_vmem(count):
    return [pl.BlockSpec(memory_space=pltpu.VMEM)] * count


def in_smem(count):
    return [pl.BlockSpec(memory_space=pltpu.SMEM)] * count


def exchange(value):
    return lax.all_to_all(value, "expert", split_axis=0, concat_axis=0, tiled=True)


def shards(
    query,
    keys,
    values,
    lengths,
    routes,
    gates,
    norm_gain,
    old_holds,
    dup_experts,
    w_gate,
    w_up,
    w_down,
):
    width = lax.axis_size("expert")
    batches, tokens, features = query.shape
    cols = features * CAP // PACK
    rows = width * GROUPS * PACK
    hidden = w_gate.shape[2]
    params = pltpu.CompilerParams(vmem_limit_bytes=VMEM_LIMIT)
    routes = jnp.transpose(routes, (2, 0, 1))
    gates = jnp.transpose(gates, (2, 0, 1))

    attn, send = pl.pallas_call(
        front_kernel,
        name="attend_and_pack",
        out_shape=(
            jax.ShapeDtypeStruct((batches, tokens, features), F32),
            jax.ShapeDtypeStruct((rows, cols), BF16),
        ),
        in_specs=in_smem(3) + in_vmem(5),
        out_specs=tuple(in_vmem(2)),
        scratch_shapes=[pltpu.VMEM((batches * tokens, features), BF16)],
        compiler_params=params,
    )(lengths, old_holds, dup_experts, query, keys, values, routes, norm_gain.reshape(1, features))

    got = exchange(send)

    mix = pl.pallas_call(
        weights_kernel,
        name="gate_weights",
        out_shape=jax.ShapeDtypeStruct((SPLIT, rows, 4 * batches * tokens), BF16),
        in_specs=in_smem(2) + in_vmem(2),
        out_specs=in_vmem(1)[0],
        compiler_params=params,
    )(old_holds, dup_experts, routes, gates)

    block = GROUPS * PACK * min(width, 8)
    chunk = 256 if hidden % 256 == 0 else hidden
    back = pl.pallas_call(
        expert_kernel,
        name="expert_ffn",
        out_shape=jax.ShapeDtypeStruct((rows, cols), BF16),
        grid=(rows // block, hidden // chunk),
        in_specs=[
            pl.BlockSpec((block, cols), lambda i, j: (i, 0)),
            pl.BlockSpec((1, features, chunk), lambda i, j: (0, 0, j)),
            pl.BlockSpec((1, features, chunk), lambda i, j: (0, 0, j)),
            pl.BlockSpec((1, chunk, features), lambda i, j: (0, j, 0)),
        ],
        out_specs=pl.BlockSpec((block, cols), lambda i, j: (i, 0)),
        scratch_shapes=[
            pltpu.VMEM((block, features), BF16),
            pltpu.VMEM((block, features), F32),
        ],
        compiler_params=params,
    )(got, w_gate, w_up, w_down)

    returned = exchange(back)

    return pl.pallas_call(
        combine_kernel,
        name="combine",
        out_shape=jax.ShapeDtypeStruct((batches, tokens, features), BF16),
        in_specs=in_vmem(3),
        out_specs=in_vmem(1)[0],
        compiler_params=params,
    )(attn, mix, returned)


def solution(mesh):
    placed = (
        P(None, ("dp", "expert"), None),
        P(None, ("dp", "expert"), None),
        P(None, ("dp", "expert"), None),
        P(None, ("dp", "expert"), None),
        P(None, ("dp", "expert"), None),
        P(None, ("dp", "expert"), None),
        P(),
        P(),
        P(),
        P("expert", None, None),
        P("expert", None, None),
        P("expert", None, None),
    )
    return jax.shard_map(
        shards,
        mesh=mesh,
        in_specs=placed,
        out_specs=P(None, ("dp", "expert"), None),
        check_vma=False,
    )
```

time: 612 us -> 67.9 us (0.11)
  waiting for transfers between devices: 514 us -> 17 us
  local copies, waits for them, and re-layouts: 34.7 us -> 2.22 us
  matrix products: 29.7 us -> 0 us
  blocking collectives: 0 us -> 26.5 us
  starting transfers between devices: 25 us -> 3.55 us
  Pallas kernels: 0 us -> 18.2 us
  other arithmetic: 6.36 us -> 0 us
    all_to_all x4 -> x1, waiting for transfers between devices: 514 us -> 17 us  [exchange(): lax.all_to_all(value, 'expert', split_axis=0, concat_axis=0, tiled=True)]
    dot_general x12 -> x0, matrix products: 28.8 us -> none  [the longest x3 15 us: expert_rows(): jnp.dot(hidden, down_mat, preferred_element_type=jnp.float32)]
    all_to_all x0 -> x1, blocking collectives: none -> 26.5 us  [exchange(): lax.all_to_all(value, 'expert', split_axis=0, concat_axis=0, tiled=True)]
    pallas_call x0 -> x4, Pallas kernels: none -> 18.2 us  [the longest x1 9.11 us: shards(): pl.pallas_call(expert_kernel, name='expert_ffn', out_shape=jax.ShapeDtype...]
    all_to_all x4 -> x1, starting transfers between devices: 18 us -> 3.55 us  [exchange(): lax.all_to_all(value, 'expert', split_axis=0, concat_axis=0, tiled=True)]
    gather x6 -> x0, local copies, waits for them, and re-layouts: 11.4 us -> none  [the longest x4 9.81 us: combine(): picked = returned[jnp.minimum(spot, returned.shape[0] - 1)]]
    ppermute x3 -> x0, starting transfers between devices: 6.96 us -> none  [from_behind(): return lax.ppermute(value, axis, pairs)]
  transfers between devices with their start and end apart: 7 -> 1, of which waited for: 4 -> 1; matrix products, arithmetic and copies ran while one was open for 8% -> 0% of each run, Pallas kernels for 0% -> 3%
where the time goes in v1:
time: 67.9 us; the launch traced here: 67.5 us
  blocking collectives  26.5 us (39%)
  Pallas kernels  18.2 us (27%)
  waiting for transfers between devices  17 us (25%)
  starting transfers between devices  3.55 us (5%)
  local copies, waits for them, and re-layouts  2.22 us (3%)
    all_to_all x1, blocking collectives, exchange(): lax.all_to_all(value, 'expert', split_axis=0, concat_axis=0, tiled=True)  26.5 us
    all_to_all x1, waiting for transfers between devices, exchange(): lax.all_to_all(value, 'expert', split_axis=0, concat_axis=0, tiled=True)  17 us
    pallas_call x1, Pallas kernels, shards(): pl.pallas_call(expert_kernel, name='expert_ffn', out_shape=jax.ShapeDtype...  9.11 us
    pallas_call x1, Pallas kernels, shards(): pl.pallas_call(front_kernel, name='attend_and_pack', out_shape=(jax.Shape...  3.91 us
    all_to_all x1, starting transfers between devices, exchange(): lax.all_to_all(value, 'expert', split_axis=0, concat_axis=0, tiled=True)  3.55 us
    pallas_call x1, Pallas kernels, shards(): pl.pallas_call(combine_kernel, name='combine', out_shape=jax.ShapeDtypeSt...  3.35 us
    pallas_call x1, Pallas kernels, shards(): pl.pallas_call(weights_kernel, name='gate_weights', out_shape=jax.ShapeDt...  1.85 us
  transfers between devices with their start and end apart: 1, of which 1 were waited for; matrix products, arithmetic and copies ran while one was open for 0% of the time, Pallas kernels for 3%

profile of v1, /device:TPU:0, one launch (start us, length us, event | category | flops | bytes accessed | tf_op | source)
XLA Modules:
  0.0 67.5 jit_solution(10413204804945196992)
XLA Ops:
  0.0 1.3 %reshape.7.gain_ref = f32[1,2560]{1,0:T(1,128)} reshape(f32[2560]{0:T(1024)} %param.18) | data formatting | bytes 20480 | tf_op jit(solution)/shard_map/reshape | solution.py:267
  1.3 3.9 %attend_and_pack.1 = (f32[2,64,2560]{2,1,0:T(8,128)}, bf16[192,1920]{1,0:T(8,128)(2,1)}) custom-call(s32[2,1,4]{2,1,0:T(1,128)} %lengths_ref.1, s32[8]{0:T(128)} %holds_ref.3, s32[4]{0:T(128)} %dup_ref.3, bf16[2,64,2560]{2,1,0:T(8,128)(2,1)} %query_ref.1, bf16[2,64,512]{2,1,0:T(8,128)(2,1)} %key_ref.1, bf16[2,64,512]{2,1,0:T(8,128)(2,1)} %value_ref.1, ...), custom_call_target="tpu_custom_call" | custom-call | tf_op jit(solution)/shard_map/attend_and_pack/pallas_call | solution.py:256
  5.2 26.5 %all_to_all.22 = bf16[8,24,1920]{2,1,0:T(8,128)(2,1)} all-to-all(bf16[8,24,1920]{2,1,0:T(8,128)(2,1)} %bitcast.9), channel_id=1, replica_groups=mesh['dp'=4,'expert'=8] {'expert'}, dimensions={0} | all-to-all | bytes 1474560 | tf_op jit(solution)/shard_map/all_to_all | solution.py:230
  31.8 9.1 %expert_ffn.1 = bf16[192,1920]{1,0:T(8,128)(2,1)} custom-call(bf16[192,1920]{1,0:T(8,128)(2,1)} %bitcast.8, bf16[1,2560,768]{2,1,0:T(8,128)(2,1)} %gate_ref.1, bf16[1,2560,768]{2,1,0:T(8,128)(2,1)} %up_ref.1, bf16[1,768,2560]{2,1,0:T(8,128)(2,1)} %down_ref.1), custom_call_target="tpu_custom_call" | custom-call | tf_op jit(solution)/shard_map/expert_ffn/pallas_call | solution.py:282
  40.9 3.5 %all-to-all-start.1 = ((bf16[8,24,1920]{2,1,0:T(8,128)(2,1)}), bf16[8,24,1920]{2,1,0:T(8,128)(2,1)S(1)}, u32[]{:S(2)}, u32[]{:S(2)}) async-start(bf16[8,24,1920]{2,1,0:T(8,128)(2,1)} %bitcast.7), calls=%async_computation.1 | async-start | bytes 1474560 | tf_op jit(solution)/shard_map/all_to_all | solution.py:230
  44.4 1.9 %gate_weights.1.mix_ref = bf16[3,192,512]{2,1,0:T(8,128)(2,1)} custom-call(s32[8]{0:T(128)} %holds_ref.3, s32[4]{0:T(128)} %dup_ref.3, s32[6,2,64]{2,1,0:T(2,128)} %bitcast.11, f32[6,2,64]{2,1,0:T(2,128)} %bitcast.12), custom_call_target="tpu_custom_call" | custom-call | tf_op jit(solution)/shard_map/gate_weights/pallas_call | solution.py:271
  46.3 17.0 %all-to-all-done.1 = bf16[8,24,1920]{2,1,0:T(8,128)(2,1)S(1)} async-done(((bf16[8,24,1920]{2,1,0:T(8,128)(2,1)}), bf16[8,24,1920]{2,1,0:T(8,128)(2,1)S(1)}, u32[]{:S(2)}, u32[]{:S(2)}) %all-to-all-start.1) | async-done | bytes 737312 | tf_op jit(solution)/shard_map/all_to_all | solution.py:230
  63.3 0.0 copy-start
  63.3 0.9 %copy-done = bf16[8,24,1920]{2,1,0:T(8,128)(2,1)} copy-done((bf16[8,24,1920]{2,1,0:T(8,128)(2,1)}, bf16[8,24,1920]{2,1,0:T(8,128)(2,1)S(1)}, u32[]{:S(2)}) %copy-start) | copy-done | bytes 737304
  64.2 3.3 %combine.1 = bf16[2,64,2560]{2,1,0:T(8,128)(2,1)} custom-call(f32[2,64,2560]{2,1,0:T(8,128)} %get-tuple-element.7.attn_ref, bf16[3,192,512]{2,1,0:T(8,128)(2,1)} %gate_weights.1.mix_ref, bf16[192,1920]{1,0:T(8,128)(2,1)} %bitcast.6), custom_call_target="tpu_custom_call" | custom-call | tf_op jit(solution)/shard_map/combine/pallas_call | solution.py:303
Async XLA Ops:
  40.9 22.4 %all-to-all-start.1 = ((bf16[8,24,1920]{2,1,0:T(8,128)(2,1)}), bf16[8,24,1920]{2,1,0:T(8,128)(2,1)S(1)}, u32[]{:S(2)}, u32[]{:S(2)}) async-start(bf16[8,24,1920]{2,1,0:T(8,128)(2,1)} %bitcast.7), calls=%async_computation.1 | async-start | bytes 1474560 | tf_op jit(solution)/shard_map/all_to_all | solution.py:230
  63.3 0.9 %copy-start = (bf16[8,24,1920]{2,1,0:T(8,128)(2,1)}, bf16[8,24,1920]{2,1,0:T(8,128)(2,1)S(1)}, u32[]{:S(2)}) copy-start(bf16[8,24,1920]{2,1,0:T(8,128)(2,1)S(1)} %all-to-all-done.1) | copy-start | bytes 2211844

commit v2 on v1

v2 whole, which is shorter than its diff:
```python
import functools

import jax
import jax.numpy as jnp
from jax import lax
from jax.experimental import pallas as pl
from jax.experimental.pallas import tpu as pltpu
from jax.sharding import PartitionSpec as P

HEAD_WIDTH = 128
CAP = 6
PACK = 8
SPLIT = CAP // (PACK - CAP)
GROUPS = 3
PERMUTED_WIDTH = 8
MIB = 1024 * 1024

F32 = jnp.float32
BF16 = jnp.bfloat16


def dot(a, b, dims=((1,), (0,))):
    return lax.dot_general(a, b, (dims, ((), ())), preferred_element_type=F32)


def row_iota(shape, axis):
    return lax.broadcasted_iota(jnp.int32, shape, axis)


def count_steps(value, step, upto):
    total = jnp.zeros_like(value)
    for at in range(1, upto):
        total = total + (value >= step * at).astype(jnp.int32)
    return total


def slot_picks(order, relative, holds_ref, dup_ref, routes_ref):
    _, batches, tokens = routes_ref.shape
    lanes = batches * tokens
    rows = len(order) * GROUPS * PACK
    shape = (rows, lanes)
    row = row_iota(shape, 0)
    lane = row_iota(shape, 1)
    block = count_steps(row, GROUPS * PACK, len(order))
    within = row - block * (GROUPS * PACK)
    group = count_steps(within, PACK, GROUPS)
    place = within - group * PACK
    me = lax.axis_index("expert") if relative else 0
    expert = jnp.zeros(shape, jnp.int32)
    for at, slot in enumerate(order):
        expert = jnp.where(block == at, holds_ref[me ^ slot], expert)
    doubled = jnp.zeros(shape, jnp.bool_)
    for at in range(dup_ref.shape[0]):
        doubled = doubled | (expert == dup_ref[at])
    batch = (lane >= tokens).astype(jnp.int32)
    allowed = (batch == (group >= 1).astype(jnp.int32)) & (doubled | (group < 2))
    routes = routes_ref[...]
    routes = jnp.concatenate([routes[:, at, :] for at in range(batches)], axis=1)
    named = [routes[k : k + 1, :] == expert for k in range(routes.shape[0])]
    hit = functools.reduce(jnp.logical_or, named)
    earlier = row_iota((lanes, lanes), 0)
    later = row_iota((lanes, lanes), 1)
    same = (earlier >= tokens) == (later >= tokens)
    before_mat = jnp.where((earlier < later) & same, 1.0, 0.0).astype(BF16)
    before = dot(jnp.where(hit, 1.0, 0.0).astype(BF16), before_mat).astype(jnp.int32)
    before = before - jnp.where(group == 2, CAP, 0)
    live = hit & allowed
    lead = live & (place < CAP) & (before == place)
    trail = [
        live & (place >= CAP) & (before == (place - CAP) * SPLIT + piece) for piece in range(SPLIT)
    ]
    return lead, trail, named


def attend(query_ref, key_ref, value_ref, lengths_ref, batch, attn_ref):
    tokens = query_ref.shape[1]
    kv_heads = key_ref.shape[2] // HEAD_WIDTH
    group = query_ref.shape[2] // HEAD_WIDTH // kv_heads
    at_row = row_iota((tokens, tokens), 0)
    at_col = row_iota((tokens, tokens), 1)
    row_request = jnp.zeros((tokens, tokens), jnp.int32)
    col_request = jnp.zeros((tokens, tokens), jnp.int32)
    end = jnp.int32(0)
    for r in range(lengths_ref.shape[2]):
        end = end + lengths_ref[batch, 0, r]
        row_request = row_request + (at_row >= end).astype(jnp.int32)
        col_request = col_request + (at_col >= end).astype(jnp.int32)
    allowed = (row_request == col_request) & (at_col <= at_row)
    squares = jnp.zeros((tokens, HEAD_WIDTH), F32)
    for h in range(kv_heads):
        kv = slice(h * HEAD_WIDTH, (h + 1) * HEAD_WIDTH)
        heads = [
            slice((h * group + g) * HEAD_WIDTH, (h * group + g + 1) * HEAD_WIDTH)
            for g in range(group)
        ]
        q = jnp.concatenate([query_ref[batch, :, cols] for cols in heads], axis=0)
        scores = dot(q, key_ref[batch, :, kv], ((1,), (1,))) * HEAD_WIDTH ** (-0.5)
        scores = scores.reshape(group, tokens, tokens)
        scores = jnp.where(allowed[None], scores, -1e30)
        weights = jnp.exp(scores - jnp.max(scores, axis=-1, keepdims=True))
        probs = (weights / jnp.sum(weights, axis=-1, keepdims=True)).astype(BF16)
        mixed = dot(probs.reshape(group * tokens, tokens), value_ref[batch, :, kv])
        for g, cols in enumerate(heads):
            part = mixed[g * tokens : (g + 1) * tokens]
            attn_ref[batch, :, cols] = part
            squares = squares + part * part
    meansq = jnp.sum(squares, axis=-1, keepdims=True) / query_ref.shape[2]
    return lax.rsqrt(meansq + 1e-05)


def front_kernel(
    order,
    relative,
    lengths_ref,
    holds_ref,
    dup_ref,
    query_ref,
    key_ref,
    value_ref,
    routes_ref,
    gain_ref,
    attn_ref,
    *rest,
):
    *send_refs, normed_ref = rest
    batches, tokens, features = query_ref.shape
    piece, cols = send_refs[0].shape
    step = cols // SPLIT
    for b in range(batches):
        scale = attend(query_ref, key_ref, value_ref, lengths_ref, b, attn_ref)
        normed_ref[b * tokens : (b + 1) * tokens, :] = (
            attn_ref[b] * scale * gain_ref[...]
        ).astype(BF16)
    lead, trail, _ = slot_picks(order, relative, holds_ref, dup_ref, routes_ref)
    tail = normed_ref[:, cols:features]
    for j in range(SPLIT):
        at = slice(j * step, (j + 1) * step)
        picks = jnp.concatenate([lead, trail[j]], axis=1)
        picks = jnp.where(picks, 1.0, 0.0).astype(BF16)
        source = jnp.concatenate([normed_ref[:, at], tail], axis=0)
        packed = dot(picks, source)
        for i, send_ref in enumerate(send_refs):
            send_ref[:, at] = packed[i * piece : (i + 1) * piece].astype(BF16)


def prepare_kernel(
    order,
    relative,
    holds_ref,
    dup_ref,
    routes_ref,
    gates_ref,
    gate_hbm,
    up_hbm,
    down_hbm,
    gate_ref,
    up_ref,
    down_ref,
    *rest,
):
    *mix_refs, sems = rest
    pairs = ((gate_hbm, gate_ref), (up_hbm, up_ref), (down_hbm, down_ref))
    loads = [pltpu.make_async_copy(a, b, sems.at[i]) for i, (a, b) in enumerate(pairs)]
    for load in loads:
        load.start()
    lead, trail, named = slot_picks(order, relative, holds_ref, dup_ref, routes_ref)
    gates = gates_ref[...]
    gates = jnp.concatenate([gates[:, at, :] for at in range(gates.shape[1])], axis=1)
    gate = jnp.zeros(lead.shape, F32)
    for k, match in enumerate(named):
        gate = gate + jnp.where(match, gates[k : k + 1, :], 0.0)
    lanes = lead.shape[1]
    rows = mix_refs[0].shape[2]
    for j in range(SPLIT):
        for part, pick in enumerate((lead, trail[j])):
            weight = jnp.where(pick, gate, 0.0)
            for i, mix_ref in enumerate(mix_refs):
                mine = weight[i * rows : (i + 1) * rows].T
                high = mine.astype(BF16)
                low = (mine - high.astype(F32)).astype(BF16)
                mix_ref[j, (2 * part) * lanes : (2 * part + 1) * lanes, :] = high
                mix_ref[j, (2 * part + 1) * lanes : (2 * part + 2) * lanes, :] = low
    for load in loads:
        load.wait()


def expert_kernel(count, gate_ref, up_ref, down_ref, *rest):
    got_refs, back_refs = rest[:count], rest[count : 2 * count]
    rows_ref, hidden_ref = rest[2 * count :]
    piece, cols = got_refs[0].shape
    features = rows_ref.shape[1]
    step = cols // SPLIT
    block, hidden = hidden_ref.shape
    shape = (block, block)
    row = row_iota(shape, 0)
    other = row_iota(shape, 1)
    place = lax.rem(row, PACK)
    tile = row - place

    def trails(j):
        picked = jnp.zeros(shape, jnp.bool_)
        for a in range(PACK - CAP):
            picked = picked | ((place == a * SPLIT + j) & (other == tile + CAP + a))
        return jnp.where(picked, 1.0, 0.0).astype(BF16)

    take = min(piece, block)
    for start in range(0, piece * count, block):
        spots = [
            (at // piece, slice(at % piece, at % piece + take), slice(at - start, at - start + take))
            for at in range(start, start + block, take)
        ]
        for i, theirs, mine in spots:
            rows_ref[mine, :cols] = got_refs[i][theirs, :]
        tail = jnp.zeros((block, features - cols), F32)
        for j in range(SPLIT):
            tail = tail + dot(trails(j), rows_ref[:, j * step : (j + 1) * step])
        rows_ref[:, cols:] = tail.astype(BF16)
        chunk = 256 if hidden % 256 == 0 else hidden
        for c in range(0, hidden, chunk):
            gate_val = dot(rows_ref[...], gate_ref[0, :, c : c + chunk])
            up_val = dot(rows_ref[...], up_ref[0, :, c : c + chunk])
            hidden_ref[:, c : c + chunk] = (
                gate_val / (1.0 + jnp.exp(-gate_val)) * up_val
            ).astype(BF16)
        tail = dot(hidden_ref[...], down_ref[0, :, cols:]).astype(BF16)
        leading = lax.rem(row_iota((block, step), 0), PACK) < CAP
        for j in range(SPLIT):
            at = slice(j * step, (j + 1) * step)
            moved = dot(trails(j), tail, ((0,), (0,)))
            result = jnp.where(leading, dot(hidden_ref[...], down_ref[0, :, at]), moved)
            for i, theirs, mine in spots:
                back_refs[i][theirs, at] = result[mine].astype(BF16)


def combine_kernel(base_ref, mix_ref, *rest):
    *back_refs, out_ref = rest
    batches, tokens, features = base_ref.shape
    lanes = batches * tokens
    piece, cols = back_refs[0].shape
    step = cols // SPLIT
    tail = jnp.zeros((lanes, features - cols), F32)

    def put(part, at):
        for b in range(batches):
            out_ref[b, :, at] = (base_ref[b, :, at] + part[b * tokens : (b + 1) * tokens]).astype(
                out_ref.dtype
            )

    for j in range(SPLIT):
        at = slice(j * step, (j + 1) * step)
        back = jnp.concatenate([back_ref[:, at] for back_ref in back_refs], axis=0)
        mixed = dot(mix_ref[j], back)
        put(mixed[:lanes] + mixed[lanes : 2 * lanes], at)
        tail = tail + (mixed[2 * lanes : 3 * lanes] + mixed[3 * lanes :])
    put(tail, slice(cols, features))


def results(in_vmem, *shapes):
    kind = pltpu.VMEM if in_vmem else jax.ShapeDtypeStruct
    return [kind(shape, dtype) for shape, dtype in shapes]


def from_hbm(*values):
    return [pltpu.with_memory_space_constraint(value, pltpu.HBM) for value in values]


def in_vmem(count):
    return [pl.BlockSpec(memory_space=pltpu.VMEM)] * count


def in_smem(count):
    return [pl.BlockSpec(memory_space=pltpu.SMEM)] * count


def peer_groups(width):
    half = width // 2
    far, near = list(range(half, width)), [1, 0] + list(range(2, half))
    return [far[: half // 2] + near[: half // 2], far[half // 2 :] + near[half // 2 :]]


def swap(value, peer):
    if peer == 0:
        return value
    pairs = [(source, source ^ peer) for source in range(lax.axis_size("expert"))]
    return lax.ppermute(value, "expert", pairs)


def exchange_all(value):
    return lax.all_to_all(value, "expert", split_axis=0, concat_axis=0, tiled=True)


def shards(
    query,
    keys,
    values,
    lengths,
    routes,
    gates,
    norm_gain,
    old_holds,
    dup_experts,
    w_gate,
    w_up,
    w_down,
):
    width = lax.axis_size("expert")
    batches, tokens, features = query.shape
    lanes = batches * tokens
    cols = features * CAP // PACK
    hidden = w_gate.shape[2]
    relative = width == PERMUTED_WIDTH
    groups = peer_groups(width) if relative else [list(range(width))]
    order = [peer for group in groups for peer in group]
    block = GROUPS * PACK
    piece = block if relative else block * width
    counts = [len(group) * block // piece for group in groups]
    params = pltpu.CompilerParams(vmem_limit_bytes=24 * MIB if relative else 56 * MIB)
    routes = jnp.transpose(routes, (2, 0, 1))
    gates = jnp.transpose(gates, (2, 0, 1))
    gain = norm_gain.reshape(1, features)

    attn, *send = pl.pallas_call(
        functools.partial(front_kernel, order, relative),
        name="attend_and_pack",
        out_shape=results(
            relative, ((batches, tokens, features), F32), *[((piece, cols), BF16)] * sum(counts)
        ),
        in_specs=in_smem(3) + in_vmem(5),
        out_specs=in_vmem(1 + sum(counts)),
        scratch_shapes=[pltpu.VMEM((lanes, features), BF16)],
        compiler_params=params,
    )(*from_hbm(lengths, old_holds, dup_experts, query, keys, values, routes, gain))

    def travel(parts, group):
        if relative:
            return [swap(part, peer) for part, peer in zip(parts, group)]
        return [exchange_all(part) for part in parts]

    arrived, at = [], 0
    for group, count in zip(groups, counts):
        arrived.append(travel(send[at : at + count], group))
        at += count

    big = [w_gate, w_up, w_down]
    gate_mat, up_mat, down_mat, *mixes = pl.pallas_call(
        functools.partial(prepare_kernel, order, relative),
        name="prepare",
        out_shape=results(
            relative,
            *[(w.shape, w.dtype) for w in big],
            *[((SPLIT, 4 * lanes, len(group) * block), BF16) for group in groups],
        ),
        in_specs=in_smem(2) + in_vmem(2) + [pl.BlockSpec(memory_space=pltpu.HBM)] * 3,
        out_specs=in_vmem(3 + len(groups)),
        scratch_shapes=[pltpu.SemaphoreType.DMA((3,))],
        cost_estimate=pl.CostEstimate(
            flops=0, bytes_accessed=sum(2 * w.size * 2 for w in big), transcendentals=0
        ),
        compiler_params=params,
    )(*from_hbm(old_holds, dup_experts, routes, gates, *big))

    returned = []
    for group, count, got in zip(groups, counts, arrived):
        rows = min(count * piece, block * 8)
        back = pl.pallas_call(
            functools.partial(expert_kernel, count),
            name="expert_ffn",
            out_shape=[jax.ShapeDtypeStruct((piece, cols), BF16)] * count,
            in_specs=in_vmem(3 + count),
            out_specs=in_vmem(count),
            scratch_shapes=[pltpu.VMEM((rows, features), BF16), pltpu.VMEM((rows, hidden), BF16)],
            cost_estimate=pl.CostEstimate(
                flops=count * piece * features * hidden * 6,
                bytes_accessed=sum(w.size * 2 for w in big),
                transcendentals=0,
            ),
            compiler_params=params,
        )(gate_mat, up_mat, down_mat, *got)
        returned.append(travel(back, group))

    base = attn
    for at, (mix, back) in enumerate(zip(mixes, returned)):
        last = at == len(groups) - 1
        base = pl.pallas_call(
            combine_kernel,
            name="combine",
            out_shape=jax.ShapeDtypeStruct(attn.shape, BF16 if last else F32),
            in_specs=in_vmem(2 + len(back)),
            out_specs=in_vmem(1)[0],
            cost_estimate=pl.CostEstimate(
                flops=2 * mix.size * features // SPLIT,
                bytes_accessed=attn.size * 8,
                transcendentals=0,
            ),
            compiler_params=params,
        )(base, mix, *back)
    return base


def solution(mesh):
    placed = (
        P(None, ("dp", "expert"), None),
        P(None, ("dp", "expert"), None),
        P(None, ("dp", "expert"), None),
        P(None, ("dp", "expert"), None),
        P(None, ("dp", "expert"), None),
        P(None, ("dp", "expert"), None),
        P(),
        P(),
        P(),
        P("expert", None, None),
        P("expert", None, None),
        P("expert", None, None),
    )
    return jax.shard_map(
        shards,
        mesh=mesh,
        in_specs=placed,
        out_specs=P(None, ("dp", "expert"), None),
        check_vma=False,
    )
```

time: 67.9 us -> 46.8 us (0.69)
  blocking collectives: 26.5 us -> 0 us
  starting transfers between devices: 3.55 us -> 22.6 us
  waiting for transfers between devices: 17 us -> 7.8 us
  Pallas kernels: 18.2 us -> 14.7 us
  local copies, waits for them, and re-layouts: 2.22 us -> 1.31 us
    all_to_all x1 -> x0, blocking collectives: 26.5 us -> none  [exchange(): lax.all_to_all(value, 'expert', split_axis=0, concat_axis=0, tiled=True)]
    ppermute x0 -> x14, starting transfers between devices: none -> 22.6 us  [swap(): return lax.ppermute(value, 'expert', pairs)]
    all_to_all x1 -> x0, waiting for transfers between devices: 17 us -> none  [exchange(): lax.all_to_all(value, 'expert', split_axis=0, concat_axis=0, tiled=True)]
    ppermute x0 -> x14, waiting for transfers between devices: none -> 7.8 us  [swap(): return lax.ppermute(value, 'expert', pairs)]
    all_to_all x1 -> x0, starting transfers between devices: 3.55 us -> none  [exchange(): lax.all_to_all(value, 'expert', split_axis=0, concat_axis=0, tiled=True)]
    pallas_call x3 -> x4, Pallas kernels: 14.9 us -> 12.6 us  [the longest x1 5.19 us: shards(): pl.pallas_call(functools.partial(prepare_kernel, order, relative), name='...]
    pallas_call x1 -> x2, Pallas kernels: 3.35 us -> 2.16 us  [shards(): pl.pallas_call(combine_kernel, name='combine', out_shape=jax.ShapeDtypeSt...]
    unnamed x2 -> x0, local copies, waits for them, and re-layouts: 0.91 us -> none
  transfers between devices with their start and end apart: 1 -> 14, of which waited for: 1 -> 5; matrix products, arithmetic and copies ran while one was open for 0% -> 0% of each run, Pallas kernels for 3% -> 22%
where the time goes in v2:
time: 46.8 us; the launch traced here: 46.5 us
  starting transfers between devices  22.6 us (48%)
  Pallas kernels  14.7 us (31%)
  waiting for transfers between devices  7.8 us (17%)
  local copies, waits for them, and re-layouts  1.31 us (3%)
    ppermute x14, starting transfers between devices, swap(): return lax.ppermute(value, 'expert', pairs)  22.6 us
    ppermute x14, waiting for transfers between devices, swap(): return lax.ppermute(value, 'expert', pairs)  7.8 us
    pallas_call x1, Pallas kernels, shards(): pl.pallas_call(functools.partial(prepare_kernel, order, relative), name='...  5.19 us
    pallas_call x2, Pallas kernels, shards(): pl.pallas_call(functools.partial(expert_kernel, count), name='expert_ffn'...  4.38 us
    pallas_call x1, Pallas kernels, shards(): pl.pallas_call(functools.partial(front_kernel, order, relative), name='at...  3 us
    pallas_call x2, Pallas kernels, shards(): pl.pallas_call(combine_kernel, name='combine', out_shape=jax.ShapeDtypeSt...  2.16 us
    reshape x1, local copies, waits for them, and re-layouts, shards(): gain = norm_gain.reshape(1, features)  1.31 us
  transfers between devices with their start and end apart: 14, of which 5 were waited for; matrix products, arithmetic and copies ran while one was open for 0% of the time, Pallas kernels for 22%

profile of v2, /device:TPU:0, one launch (start us, length us, event | category | flops | bytes accessed | tf_op | source)
XLA Modules:
  0.0 46.5 jit_solution(5834487134496740555)
XLA Ops:
  0.0 1.3 %reshape.3.gain_ref = f32[1,2560]{1,0:T(1,128)} reshape(f32[2560]{0:T(1024)} %param.18) | data formatting | bytes 20480 | tf_op jit(solution)/shard_map/reshape | solution.py:320
  1.3 3.0 %attend_and_pack.1 = (f32[2,64,2560]{2,1,0:T(8,128)S(1)}, bf16[24,1920]{1,0:T(8,128)(2,1)S(1)}, bf16[24,1920]{1,0:T(8,128)(2,1)S(1)}, bf16[24,1920]{1,0:T(8,128)...) custom-call(s32[2,1,4]{2,1,0:T(1,128)} %lengths_ref.1, ...), custom_call_target="tpu_custom_call" | custom-call | tf_op jit(solution)/shard_map/attend_and_pack/pallas_call | solution.py:322
  4.3 4.1 %collective-permute-start = (bf16[24,1920]{1,0:T(8,128)(2,1)S(1)}, bf16[24,1920]{1,0:T(8,128)(2,1)S(1)}, u32[]{:S(2)}, u32[]{:S(2)}) collective-permute-start(bf16[24,1920]{1,0:T(8,128)(2,1)S(1)} %get-tuple-element.32), channel_id=1, source_target_pairs={{0,4},{1,5},{2,6},{3,7},{4,0},{5,1},{6,2},{7,3},{8,12},{9,13},{10,... | collective-permute-start | bytes 276488 | tf_op jit(solution)/shard_map/ppermute | solution.py:285
  8.4 1.3 %collective-permute-start.1 = (bf16[24,1920]{1,0:T(8,128)(2,1)S(1)}, bf16[24,1920]{1,0:T(8,128)(2,1)S(1)}, u32[]{:S(2)}, u32[]{:S(2)}) collective-permute-start(bf16[24,1920]{1,0:T(8,128)(2,1)S(1)} %get-tuple-element.33), channel_id=1, source_target_pairs={{0,5},{1,4},{2,7},{3,6},{4,1},{5,0},{6,3},{7,2},{8,13},{9,12},{10,... | collective-permute-start | bytes 276488 | tf_op jit(solution)/shard_map/ppermute | solution.py:285
  9.7 0.3 collective-permute-start.2
  10.0 3.9 %collective-permute-start.6 = (bf16[24,1920]{1,0:T(8,128)(2,1)S(1)}, bf16[24,1920]{1,0:T(8,128)(2,1)S(1)}, u32[]{:S(2)}, u32[]{:S(2)}) collective-permute-start(bf16[24,1920]{1,0:T(8,128)(2,1)S(1)} %get-tuple-element.41), channel_id=1, source_target_pairs={{0,6},{1,7},{2,4},{3,5},{4,2},{5,3},{6,0},{7,1},{8,14},{9,15},{10,... | collective-permute-start | bytes 276488 | tf_op jit(solution)/shard_map/ppermute | solution.py:285
  13.8 1.2 %collective-permute-start.7 = (bf16[24,1920]{1,0:T(8,128)(2,1)S(1)}, bf16[24,1920]{1,0:T(8,128)(2,1)S(1)}, u32[]{:S(2)}, u32[]{:S(2)}) collective-permute-start(bf16[24,1920]{1,0:T(8,128)(2,1)S(1)} %get-tuple-element.42), channel_id=1, source_target_pairs={{0,7},{1,6},{2,5},{3,4},{4,3},{5,2},{6,1},{7,0},{8,15},{9,14},{10,... | collective-permute-start | bytes 276488 | tf_op jit(solution)/shard_map/ppermute | solution.py:285
  15.0 5.2 %prepare.1 = (bf16[1,2560,768]{2,1,0:T(8,128)(2,1)S(1)}, bf16[1,2560,768]{2,1,0:T(8,128)(2,1)S(1)}, bf16[1,768,2560]{2,1,0:T(8,128)(2,1)S(1)}, bf16[3,512,96]{2,1,0:T(8,128)(2,1)S(1)}, bf16[3,512,96]{2,1,0:T(8,128)(2,1)S(1)}) custom-call(s32[8]{0:T(128)} %holds_ref.3, s32[4]{0:T(128)} %dup_ref.3, s32[6,2,64]{2,1,0:T(2,128)} %bitcast.3, f32[6,2,64]{2,1,0:T(2,128)} %bitcast.4, ...), custom_call_target="tpu_custom_call" | custom-call | bytes 23592960 | tf_op jit(solution)/shard_map/prepare/pallas_call | solution.py:345
  20.2 0.0 collective-permute-done.rest_0_
  20.2 0.1 collective-permute-start.8
  20.3 2.6 %collective-permute-done.1.rest_1_ = bf16[24,1920]{1,0:T(8,128)(2,1)S(1)} collective-permute-done((bf16[24,1920]{1,0:T(8,128)(2,1)S(1)}, bf16[24,1920]{1,0:T(8,128)(2,1)S(1)}, u32[]{:S(2)}, u32[]{:S(2)}) %collective-permute-start.1) | collective-permute-done | bytes 92192 | tf_op jit(solution)/shard_map/ppermute | solution.py:285
  22.9 0.0 collective-permute-start.9
  22.9 0.0 collective-permute-done.2.rest_2_
  22.9 2.2 %expert_ffn.2 = (bf16[24,1920]{1,0:T(8,128)(2,1)S(1)}, bf16[24,1920]{1,0:T(8,128)(2,1)S(1)}, bf16[24,1920]{1,0:T(8,128)(2,1)S(1)}, bf16[24,1920]{1,0:T(8,128)(2,1)S(1)}) custom-call(bf16[1,2560,768]{2,1,0:T(8,128)(2,1)S(1)} %get-tuple-element.29.gate_ref, bf16[1,2560,768]{2,1,0:T(8,128)(2,1)S(1)} %get-tuple-element.30.up_ref, ...), custom_call_target="tpu_custom_call" | custom-call | flops 1132462080 | bytes 11796480 | tf_op jit(solution)/shard_map/expert_ffn/pallas_call | solution.py:365
  25.1 3.3 %collective-permute-start.3 = (bf16[24,1920]{1,0:T(8,128)(2,1)S(1)}, bf16[24,1920]{1,0:T(8,128)(2,1)S(1)}, u32[]{:S(2)}, u32[]{:S(2)}) collective-permute-start(bf16[24,1920]{1,0:T(8,128)(2,1)S(1)} %get-tuple-element.36), channel_id=1, source_target_pairs={{0,4},{1,5},{2,6},{3,7},{4,0},{5,1},{6,2},{7,3},{8,12},{9,13},{10,... | collective-permute-start | bytes 276488 | tf_op jit(solution)/shard_map/ppermute | solution.py:285
  28.3 1.1 %collective-permute-start.4 = (bf16[24,1920]{1,0:T(8,128)(2,1)S(1)}, bf16[24,1920]{1,0:T(8,128)(2,1)S(1)}, u32[]{:S(2)}, u32[]{:S(2)}) collective-permute-start(bf16[24,1920]{1,0:T(8,128)(2,1)S(1)} %get-tuple-element.37), channel_id=1, source_target_pairs={{0,5},{1,4},{2,7},{3,6},{4,1},{5,0},{6,3},{7,2},{8,13},{9,12},{10,... | collective-permute-start | bytes 276488 | tf_op jit(solution)/shard_map/ppermute | solution.py:285
  29.4 0.0 collective-permute-done.7.rest_1_
  29.4 0.5 %collective-permute-start.5 = (bf16[24,1920]{1,0:T(8,128)(2,1)S(1)}, bf16[24,1920]{1,0:T(8,128)(2,1)S(1)}, u32[]{:S(2)}, u32[]{:S(2)}) collective-permute-start(bf16[24,1920]{1,0:T(8,128)(2,1)S(1)} %get-tuple-element.38), channel_id=1, source_target_pairs={{0,1},{1,0},{2,3},{3,2},{4,5},{5,4},{6,7},{7,6},{8,9},{9,8},{10,11... | collective-permute-start | bytes 276488 | tf_op jit(solution)/shard_map/ppermute | solution.py:285
  29.9 0.0 collective-permute-done.8.rest_2_
  29.9 0.0 collective-permute-done.9.rest_3_
  29.9 2.2 %expert_ffn.3 = (bf16[24,1920]{1,0:T(8,128)(2,1)S(1)}, bf16[24,1920]{1,0:T(8,128)(2,1)S(1)}, bf16[24,1920]{1,0:T(8,128)(2,1)S(1)}, bf16[24,1920]{1,0:T(8,128)(2,1)S(1)}) custom-call(bf16[1,2560,768]{2,1,0:T(8,128)(2,1)S(1)} %get-tuple-element.29.gate_ref, bf16[1,2560,768]{2,1,0:T(8,128)(2,1)S(1)} %get-tuple-element.30.up_ref, ...), custom_call_target="tpu_custom_call" | custom-call | flops 1132462080 | bytes 11796480 | tf_op jit(solution)/shard_map/expert_ffn/pallas_call | solution.py:365
  32.1 2.7 %collective-permute-start.10 = (bf16[24,1920]{1,0:T(8,128)(2,1)S(1)}, bf16[24,1920]{1,0:T(8,128)(2,1)S(1)}, u32[]{:S(2)}, u32[]{:S(2)}) collective-permute-start(bf16[24,1920]{1,0:T(8,128)(2,1)S(1)} %get-tuple-element.45), channel_id=1, source_target_pairs={{0,6},{1,7},{2,4},{3,5},{4,2},{5,3},{6,0},{7,1},{8,14},{9,15},{10,... | collective-permute-start | bytes 276488 | tf_op jit(solution)/shard_map/ppermute | solution.py:285
  34.8 2.1 %collective-permute-start.11 = (bf16[24,1920]{1,0:T(8,128)(2,1)S(1)}, bf16[24,1920]{1,0:T(8,128)(2,1)S(1)}, u32[]{:S(2)}, u32[]{:S(2)}) collective-permute-start(bf16[24,1920]{1,0:T(8,128)(2,1)S(1)} %get-tuple-element.46), channel_id=1, source_target_pairs={{0,7},{1,6},{2,5},{3,4},{4,3},{5,2},{6,1},{7,0},{8,15},{9,14},{10,... | collective-permute-start | bytes 276488 | tf_op jit(solution)/shard_map/ppermute | solution.py:285
  36.9 1.2 %collective-permute-done.4.rest_1_ = bf16[24,1920]{1,0:T(8,128)(2,1)S(1)} collective-permute-done((bf16[24,1920]{1,0:T(8,128)(2,1)S(1)}, bf16[24,1920]{1,0:T(8,128)(2,1)S(1)}, u32[]{:S(2)}, u32[]{:S(2)}) %collective-permute-start.4) | collective-permute-done | bytes 92192 | tf_op jit(solution)/shard_map/ppermute | solution.py:285
  38.2 2.2 %collective-permute-start.13 = (bf16[24,1920]{1,0:T(8,128)(2,1)S(1)}, bf16[24,1920]{1,0:T(8,128)(2,1)S(1)}, u32[]{:S(2)}, u32[]{:S(2)}) collective-permute-start(bf16[24,1920]{1,0:T(8,128)(2,1)S(1)} %get-tuple-element.48), channel_id=1, source_target_pairs={{0,3},{1,2},{2,1},{3,0},{4,7},{5,6},{6,5},{7,4},{8,11},{9,10},{10,... | collective-permute-start | bytes 276488 | tf_op jit(solution)/shard_map/ppermute | solution.py:285
  40.4 0.0 collective-permute-done.5.rest_2_
  40.4 0.7 %combine.2.base_ref = f32[2,64,2560]{2,1,0:T(8,128)S(1)} custom-call(f32[2,64,2560]{2,1,0:T(8,128)S(1)} %get-tuple-element.27.base_ref, bf16[3,512,96]{2,1,0:T(8,128)(2,1)S(1)} %get-tuple-element.28.mix_ref, bf16[24,1920]{1,0:T(8,128)(2,1)S(1)} %collective-permute-done.3.rest_0_, bf16[24,1920]{1,0:T(8,128)(2,1)S(1)} %collective-permute-done.4.rest_1_, ...), custom_call_target="tpu_custom_call" | custom-call | flops 251658240 | bytes 2621440 | tf_op jit(solution)/shard_map/combine/pallas_call | solution.py:384
  41.0 0.0 collective-permute-done.10.rest_0_
  41.0 2.1 %collective-permute-done.11.rest_1_ = bf16[24,1920]{1,0:T(8,128)(2,1)S(1)} collective-permute-done((bf16[24,1920]{1,0:T(8,128)(2,1)S(1)}, bf16[24,1920]{1,0:T(8,128)(2,1)S(1)}, u32[]{:S(2)}, u32[]{:S(2)}) %collective-permute-start.11) | collective-permute-done | bytes 92192 | tf_op jit(solution)/shard_map/ppermute | solution.py:285
  43.1 0.4 collective-permute-done.12.rest_2_
  43.5 1.5 %collective-permute-done.13.rest_3_ = bf16[24,1920]{1,0:T(8,128)(2,1)S(1)} collective-permute-done((bf16[24,1920]{1,0:T(8,128)(2,1)S(1)}, bf16[24,1920]{1,0:T(8,128)(2,1)S(1)}, u32[]{:S(2)}, u32[]{:S(2)}) %collective-permute-start.13) | collective-permute-done | bytes 92192 | tf_op jit(solution)/shard_map/ppermute | solution.py:285
  45.0 1.5 %combine.3 = bf16[2,64,2560]{2,1,0:T(8,128)(2,1)} custom-call(f32[2,64,2560]{2,1,0:T(8,128)S(1)} %combine.2.base_ref, bf16[3,512,96]{2,1,0:T(8,128)(2,1)S(1)} %get-tuple-element.40.mix_ref, bf16[24,1920]{1,0:T(8,128)(2,1)S(1)} %collective-permute-done.10.rest_0_, bf16[24,1920]{1,0:T(8,128)(2,1)S(1)} %collective-permute-done.11.rest_1_, ...), custom_call_target="tpu_custom_call" | custom-call | flops 251658240 | bytes 2621440 | tf_op jit(solution)/shard_map/combine/pallas_call | solution.py:384
  (3 shorter events, 0.0 us)
Async XLA Ops:
  4.3 15.9 %collective-permute-start = (bf16[24,1920]{1,0:T(8,128)(2,1)S(1)}, bf16[24,1920]{1,0:T(8,128)(2,1)S(1)}, u32[]{:S(2)}, u32[]{:S(2)}) collective-permute-start(bf16[24,1920]{1,0:T(8,128)(2,1)S(1)} %get-tuple-element.32), channel_id=1, source_target_pairs={{0,4},{1,5},{2,6},{3,7},{4,0},{5,1},{6,2},{7,3},{8,12},{9,13},{10,... | collective-permute-start | bytes 276488 | tf_op jit(solution)/shard_map/ppermute | solution.py:285
  8.4 14.4 %collective-permute-start.1 = (bf16[24,1920]{1,0:T(8,128)(2,1)S(1)}, bf16[24,1920]{1,0:T(8,128)(2,1)S(1)}, u32[]{:S(2)}, u32[]{:S(2)}) collective-permute-start(bf16[24,1920]{1,0:T(8,128)(2,1)S(1)} %get-tuple-element.33), channel_id=1, source_target_pairs={{0,5},{1,4},{2,7},{3,6},{4,1},{5,0},{6,3},{7,2},{8,13},{9,12},{10,... | collective-permute-start | bytes 276488 | tf_op jit(solution)/shard_map/ppermute | solution.py:285
  9.7 13.1 %collective-permute-start.2 = (bf16[24,1920]{1,0:T(8,128)(2,1)S(1)}, bf16[24,1920]{1,0:T(8,128)(2,1)S(1)}, u32[]{:S(2)}, u32[]{:S(2)}) collective-permute-start(bf16[24,1920]{1,0:T(8,128)(2,1)S(1)} %get-tuple-element.34), channel_id=1, source_target_pairs={{0,1},{1,0},{2,3},{3,2},{4,5},{5,4},{6,7},{7,6},{8,9},{9,8},{10,11... | collective-permute-start | bytes 276488 | tf_op jit(solution)/shard_map/ppermute | solution.py:285
  10.0 18.3 %collective-permute-start.6 = (bf16[24,1920]{1,0:T(8,128)(2,1)S(1)}, bf16[24,1920]{1,0:T(8,128)(2,1)S(1)}, u32[]{:S(2)}, u32[]{:S(2)}) collective-permute-start(bf16[24,1920]{1,0:T(8,128)(2,1)S(1)} %get-tuple-element.41), channel_id=1, source_target_pairs={{0,6},{1,7},{2,4},{3,5},{4,2},{5,3},{6,0},{7,1},{8,14},{9,15},{10,... | collective-permute-start | bytes 276488 | tf_op jit(solution)/shard_map/ppermute | solution.py:285
  13.8 15.5 %collective-permute-start.7 = (bf16[24,1920]{1,0:T(8,128)(2,1)S(1)}, bf16[24,1920]{1,0:T(8,128)(2,1)S(1)}, u32[]{:S(2)}, u32[]{:S(2)}) collective-permute-start(bf16[24,1920]{1,0:T(8,128)(2,1)S(1)} %get-tuple-element.42), channel_id=1, source_target_pairs={{0,7},{1,6},{2,5},{3,4},{4,3},{5,2},{6,1},{7,0},{8,15},{9,14},{10,... | collective-permute-start | bytes 276488 | tf_op jit(solution)/shard_map/ppermute | solution.py:285
  20.2 9.7 %collective-permute-start.8 = (bf16[24,1920]{1,0:T(8,128)(2,1)S(1)}, bf16[24,1920]{1,0:T(8,128)(2,1)S(1)}, u32[]{:S(2)}, u32[]{:S(2)}) collective-permute-start(bf16[24,1920]{1,0:T(8,128)(2,1)S(1)} %get-tuple-element.43), channel_id=1, source_target_pairs={{0,2},{1,3},{2,0},{3,1},{4,6},{5,7},{6,4},{7,5},{8,10},{9,11},{10,... | collective-permute-start | bytes 276488 | tf_op jit(solution)/shard_map/ppermute | solution.py:285
  22.9 7.1 %collective-permute-start.9 = (bf16[24,1920]{1,0:T(8,128)(2,1)S(1)}, bf16[24,1920]{1,0:T(8,128)(2,1)S(1)}, u32[]{:S(2)}, u32[]{:S(2)}) collective-permute-start(bf16[24,1920]{1,0:T(8,128)(2,1)S(1)} %get-tuple-element.44), channel_id=1, source_target_pairs={{0,3},{1,2},{2,1},{3,0},{4,7},{5,6},{6,5},{7,4},{8,11},{9,10},{10,... | collective-permute-start | bytes 276488 | tf_op jit(solution)/shard_map/ppermute | solution.py:285
  25.1 11.9 %collective-permute-start.3 = (bf16[24,1920]{1,0:T(8,128)(2,1)S(1)}, bf16[24,1920]{1,0:T(8,128)(2,1)S(1)}, u32[]{:S(2)}, u32[]{:S(2)}) collective-permute-start(bf16[24,1920]{1,0:T(8,128)(2,1)S(1)} %get-tuple-element.36), channel_id=1, source_target_pairs={{0,4},{1,5},{2,6},{3,7},{4,0},{5,1},{6,2},{7,3},{8,12},{9,13},{10,... | collective-permute-start | bytes 276488 | tf_op jit(solution)/shard_map/ppermute | solution.py:285
  28.3 9.9 %collective-permute-start.4 = (bf16[24,1920]{1,0:T(8,128)(2,1)S(1)}, bf16[24,1920]{1,0:T(8,128)(2,1)S(1)}, u32[]{:S(2)}, u32[]{:S(2)}) collective-permute-start(bf16[24,1920]{1,0:T(8,128)(2,1)S(1)} %get-tuple-element.37), channel_id=1, source_target_pairs={{0,5},{1,4},{2,7},{3,6},{4,1},{5,0},{6,3},{7,2},{8,13},{9,12},{10,... | collective-permute-start | bytes 276488 | tf_op jit(solution)/shard_map/ppermute | solution.py:285
  29.4 11.0 %collective-permute-start.5 = (bf16[24,1920]{1,0:T(8,128)(2,1)S(1)}, bf16[24,1920]{1,0:T(8,128)(2,1)S(1)}, u32[]{:S(2)}, u32[]{:S(2)}) collective-permute-start(bf16[24,1920]{1,0:T(8,128)(2,1)S(1)} %get-tuple-element.38), channel_id=1, source_target_pairs={{0,1},{1,0},{2,3},{3,2},{4,5},{5,4},{6,7},{7,6},{8,9},{9,8},{10,11... | collective-permute-start | bytes 276488 | tf_op jit(solution)/shard_map/ppermute | solution.py:285
  32.1 8.9 %collective-permute-start.10 = (bf16[24,1920]{1,0:T(8,128)(2,1)S(1)}, bf16[24,1920]{1,0:T(8,128)(2,1)S(1)}, u32[]{:S(2)}, u32[]{:S(2)}) collective-permute-start(bf16[24,1920]{1,0:T(8,128)(2,1)S(1)} %get-tuple-element.45), channel_id=1, source_target_pairs={{0,6},{1,7},{2,4},{3,5},{4,2},{5,3},{6,0},{7,1},{8,14},{9,15},{10,... | collective-permute-start | bytes 276488 | tf_op jit(solution)/shard_map/ppermute | solution.py:285
  34.8 8.3 %collective-permute-start.11 = (bf16[24,1920]{1,0:T(8,128)(2,1)S(1)}, bf16[24,1920]{1,0:T(8,128)(2,1)S(1)}, u32[]{:S(2)}, u32[]{:S(2)}) collective-permute-start(bf16[24,1920]{1,0:T(8,128)(2,1)S(1)} %get-tuple-element.46), channel_id=1, source_target_pairs={{0,7},{1,6},{2,5},{3,4},{4,3},{5,2},{6,1},{7,0},{8,15},{9,14},{10,... | collective-permute-start | bytes 276488 | tf_op jit(solution)/shard_map/ppermute | solution.py:285
  36.9 6.6 %collective-permute-start.12 = (bf16[24,1920]{1,0:T(8,128)(2,1)S(1)}, bf16[24,1920]{1,0:T(8,128)(2,1)S(1)}, u32[]{:S(2)}, u32[]{:S(2)}) collective-permute-start(bf16[24,1920]{1,0:T(8,128)(2,1)S(1)} %get-tuple-element.47), channel_id=1, source_target_pairs={{0,2},{1,3},{2,0},{3,1},{4,6},{5,7},{6,4},{7,5},{8,10},{9,11},{10,... | collective-permute-start | bytes 276488 | tf_op jit(solution)/shard_map/ppermute | solution.py:285
  38.2 6.8 %collective-permute-start.13 = (bf16[24,1920]{1,0:T(8,128)(2,1)S(1)}, bf16[24,1920]{1,0:T(8,128)(2,1)S(1)}, u32[]{:S(2)}, u32[]{:S(2)}) collective-permute-start(bf16[24,1920]{1,0:T(8,128)(2,1)S(1)} %get-tuple-element.48), channel_id=1, source_target_pairs={{0,3},{1,2},{2,1},{3,0},{4,7},{5,6},{6,5},{7,4},{8,11},{9,10},{10,... | collective-permute-start | bytes 276488 | tf_op jit(solution)/shard_map/ppermute | solution.py:285

commit v3 on v2

--- a/solution.py
+++ b/solution.py
@@ -1,4 +1,5 @@
 import functools
+import math
 
 import jax
 import jax.numpy as jnp
@@ -37,23 +38,16 @@
 def slot_picks(order, relative, holds_ref, dup_ref, routes_ref):
     _, batches, tokens = routes_ref.shape
     lanes = batches * tokens
-    rows = len(order) * GROUPS * PACK
-    shape = (rows, lanes)
-    row = row_iota(shape, 0)
-    lane = row_iota(shape, 1)
-    block = count_steps(row, GROUPS * PACK, len(order))
-    within = row - block * (GROUPS * PACK)
-    group = count_steps(within, PACK, GROUPS)
-    place = within - group * PACK
+    shape = (len(order), lanes)
+    block = row_iota(shape, 0)
     me = lax.axis_index("expert") if relative else 0
     expert = jnp.zeros(shape, jnp.int32)
     for at, slot in enumerate(order):
         expert = jnp.where(block == at, holds_ref[me ^ slot], expert)
-    doubled = jnp.zeros(shape, jnp.bool_)
+    limit = jnp.full(shape, CAP, jnp.int32)
     for at in range(dup_ref.shape[0]):
-        doubled = doubled | (expert == dup_ref[at])
-    batch = (lane >= tokens).astype(jnp.int32)
-    allowed = (batch == (group >= 1).astype(jnp.int32)) & (doubled | (group < 2))
+        limit = jnp.where(expert == dup_ref[at], 2 * CAP, limit)
+    limit = jnp.where(row_iota(shape, 1) >= tokens, limit, CAP)
     routes = routes_ref[...]
     routes = jnp.concatenate([routes[:, at, :] for at in range(batches)], axis=1)
     named = [routes[k : k + 1, :] == expert for k in range(routes.shape[0])]
@@ -63,13 +57,27 @@
     same = (earlier >= tokens) == (later >= tokens)
     before_mat = jnp.where((earlier < later) & same, 1.0, 0.0).astype(BF16)
     before = dot(jnp.where(hit, 1.0, 0.0).astype(BF16), before_mat).astype(jnp.int32)
-    before = before - jnp.where(group == 2, CAP, 0)
-    live = hit & allowed
-    lead = live & (place < CAP) & (before == place)
-    trail = [
-        live & (place >= CAP) & (before == (place - CAP) * SPLIT + piece) for piece in range(SPLIT)
+    before = jnp.where(hit & (before < limit), before, -1)
+
+    shape = (GROUPS * PACK, lanes)
+    row = row_iota(shape, 0)
+    group = count_steps(row, PACK, GROUPS)
+    place = row - group * PACK
+    mine = (row_iota(shape, 1) >= tokens) == (group >= 1)
+    first = jnp.where(group == 2, CAP, 0)
+    lead_place = jnp.where(mine & (place < CAP), place + first, -2)
+    trail_places = [
+        jnp.where(mine & (place >= CAP), (place - CAP) * SPLIT + piece + first, -2)
+        for piece in range(SPLIT)
     ]
-    return lead, trail, named
+
+    def matches(places):
+        blocks = [
+            jnp.where(before[at : at + 1, :] == places, 1.0, 0.0) for at in range(len(order))
+        ]
+        return jnp.concatenate(blocks, axis=0)
+
+    return matches(lead_place), [matches(places) for places in trail_places], named
 
 
 def attend(query_ref, key_ref, value_ref, lengths_ref, batch, attn_ref):
@@ -86,6 +94,8 @@
         row_request = row_request + (at_row >= end).astype(jnp.int32)
         col_request = col_request + (at_col >= end).astype(jnp.int32)
     allowed = (row_request == col_request) & (at_col <= at_row)
+    bias = jnp.where(allowed, 0.0, -1e30)
+    scale = HEAD_WIDTH ** (-0.5) * math.log2(math.e)
     squares = jnp.zeros((tokens, HEAD_WIDTH), F32)
     for h in range(kv_heads):
         kv = slice(h * HEAD_WIDTH, (h + 1) * HEAD_WIDTH)
@@ -94,11 +104,11 @@
             for g in range(group)
         ]
         q = jnp.concatenate([query_ref[batch, :, cols] for cols in heads], axis=0)
-        scores = dot(q, key_ref[batch, :, kv], ((1,), (1,))) * HEAD_WIDTH ** (-0.5)
-        scores = scores.reshape(group, tokens, tokens)
-        scores = jnp.where(allowed[None], scores, -1e30)
-        weights = jnp.exp(scores - jnp.max(scores, axis=-1, keepdims=True))
-        probs = (weights / jnp.sum(weights, axis=-1, keepdims=True)).astype(BF16)
+        scores = dot(q, key_ref[batch, :, kv], ((1,), (1,)))
+        scores = scores.reshape(group, tokens, tokens) + bias[None]
+        weights = jnp.exp2((scores - jnp.max(scores, axis=-1, keepdims=True)) * scale)
+        share = 1.0 / jnp.sum(weights, axis=-1, keepdims=True)
+        probs = (weights * share).astype(BF16)
         mixed = dot(probs.reshape(group * tokens, tokens), value_ref[batch, :, kv])
         for g, cols in enumerate(heads):
             part = mixed[g * tokens : (g + 1) * tokens]
@@ -129,59 +139,52 @@
     for b in range(batches):
         scale = attend(query_ref, key_ref, value_ref, lengths_ref, b, attn_ref)
         normed_ref[b * tokens : (b + 1) * tokens, :] = (
-            attn_ref[b] * scale * gain_ref[...]
+            attn_ref[b] * scale * gain_ref[...][None, :]
         ).astype(BF16)
     lead, trail, _ = slot_picks(order, relative, holds_ref, dup_ref, routes_ref)
     tail = normed_ref[:, cols:features]
     for j in range(SPLIT):
         at = slice(j * step, (j + 1) * step)
-        picks = jnp.concatenate([lead, trail[j]], axis=1)
-        picks = jnp.where(picks, 1.0, 0.0).astype(BF16)
+        picks = jnp.concatenate([lead, trail[j]], axis=1).astype(BF16)
         source = jnp.concatenate([normed_ref[:, at], tail], axis=0)
         packed = dot(picks, source)
         for i, send_ref in enumerate(send_refs):
             send_ref[:, at] = packed[i * piece : (i + 1) * piece].astype(BF16)
 
 
-def prepare_kernel(
-    order,
-    relative,
-    holds_ref,
-    dup_ref,
-    routes_ref,
-    gates_ref,
-    gate_hbm,
-    up_hbm,
-    down_hbm,
-    gate_ref,
-    up_ref,
-    down_ref,
-    *rest,
-):
-    *mix_refs, sems = rest
-    pairs = ((gate_hbm, gate_ref), (up_hbm, up_ref), (down_hbm, down_ref))
-    loads = [pltpu.make_async_copy(a, b, sems.at[i]) for i, (a, b) in enumerate(pairs)]
+def load_kernel(*refs):
+    *refs, sems = refs
+    half = len(refs) // 2
+    loads = [
+        pltpu.make_async_copy(refs[i], refs[half + i], sems.at[i]) for i in range(half)
+    ]
     for load in loads:
         load.start()
+    for load in loads:
+        load.wait()
+
+
+def weights_kernel(order, relative, holds_ref, dup_ref, routes_ref, gates_ref, *mix_refs):
     lead, trail, named = slot_picks(order, relative, holds_ref, dup_ref, routes_ref)
     gates = gates_ref[...]
     gates = jnp.concatenate([gates[:, at, :] for at in range(gates.shape[1])], axis=1)
-    gate = jnp.zeros(lead.shape, F32)
+    gate = jnp.zeros(named[0].shape, F32)
     for k, match in enumerate(named):
         gate = gate + jnp.where(match, gates[k : k + 1, :], 0.0)
+    high = gate.astype(BF16).astype(F32)
     lanes = lead.shape[1]
-    rows = mix_refs[0].shape[2]
-    for j in range(SPLIT):
-        for part, pick in enumerate((lead, trail[j])):
-            weight = jnp.where(pick, gate, 0.0)
-            for i, mix_ref in enumerate(mix_refs):
-                mine = weight[i * rows : (i + 1) * rows].T
-                high = mine.astype(BF16)
-                low = (mine - high.astype(F32)).astype(BF16)
-                mix_ref[j, (2 * part) * lanes : (2 * part + 1) * lanes, :] = high
-                mix_ref[j, (2 * part + 1) * lanes : (2 * part + 2) * lanes, :] = low
-    for load in loads:
-        load.wait()
+    rows = mix_refs[0].shape[2] // 2
+    block = GROUPS * PACK
+    for k, part in enumerate((high, gate - high)):
+        spread = [jnp.broadcast_to(part[at : at + 1], (block, lanes)) for at in range(len(order))]
+        spread = jnp.concatenate(spread, axis=0)
+        for j in range(SPLIT):
+            for half, pick in enumerate((lead, trail[j])):
+                weight = pick * spread
+                for i, mix_ref in enumerate(mix_refs):
+                    mix_ref[j, half * lanes : (half + 1) * lanes, k * rows : (k + 1) * rows] = (
+                        weight[i * rows : (i + 1) * rows].T.astype(BF16)
+                    )
 
 
 def expert_kernel(count, gate_ref, up_ref, down_ref, *rest):
@@ -248,10 +251,10 @@
 
     for j in range(SPLIT):
         at = slice(j * step, (j + 1) * step)
-        back = jnp.concatenate([back_ref[:, at] for back_ref in back_refs], axis=0)
+        back = jnp.concatenate([back_ref[:, at] for back_ref in back_refs] * 2, axis=0)
         mixed = dot(mix_ref[j], back)
-        put(mixed[:lanes] + mixed[lanes : 2 * lanes], at)
-        tail = tail + (mixed[2 * lanes : 3 * lanes] + mixed[3 * lanes :])
+        put(mixed[:lanes], at)
+        tail = tail + mixed[lanes:]
     put(tail, slice(cols, features))
 
 
@@ -283,6 +286,25 @@
         return value
     pairs = [(source, source ^ peer) for source in range(lax.axis_size("expert"))]
     return lax.ppermute(value, "expert", pairs)
+
+
+def after(value, first):
+    return lax.optimization_barrier((value, first))[0]
+
+
+def load_weights(params, *weights):
+    return pl.pallas_call(
+        load_kernel,
+        name="load_weights",
+        out_shape=results(True, *[(w.shape, w.dtype) for w in weights]),
+        in_specs=[pl.BlockSpec(memory_space=pltpu.HBM)] * len(weights),
+        out_specs=in_vmem(len(weights)),
+        scratch_shapes=[pltpu.SemaphoreType.DMA((len(weights),))],
+        cost_estimate=pl.CostEstimate(
+            flops=0, bytes_accessed=sum(w.size * 4 for w in weights), transcendentals=0
+        ),
+        compiler_params=params,
+    )(*from_hbm(*weights))
 
 
 def exchange_all(value):
@@ -317,7 +339,6 @@
     params = pltpu.CompilerParams(vmem_limit_bytes=24 * MIB if relative else 56 * MIB)
     routes = jnp.transpose(routes, (2, 0, 1))
     gates = jnp.transpose(gates, (2, 0, 1))
-    gain = norm_gain.reshape(1, features)
 
     attn, *send = pl.pallas_call(
         functools.partial(front_kernel, order, relative),
@@ -329,54 +350,61 @@
         out_specs=in_vmem(1 + sum(counts)),
         scratch_shapes=[pltpu.VMEM((lanes, features), BF16)],
         compiler_params=params,
-    )(*from_hbm(lengths, old_holds, dup_experts, query, keys, values, routes, gain))
-
-    def travel(parts, group):
-        if relative:
-            return [swap(part, peer) for part, peer in zip(parts, group)]
-        return [exchange_all(part) for part in parts]
-
-    arrived, at = [], 0
+    )(*from_hbm(lengths, old_holds, dup_experts, query, keys, values, routes, norm_gain))
+
+    sent = dict(zip(order, send))
+    arrived = {}
+    gate_mat, up_mat, down_mat = w_gate, w_up, w_down
+    if relative:
+        half = width // 2
+        for peer in groups[0]:
+            arrived[peer] = swap(sent[peer], peer)
+        gate_mat, up_mat = load_weights(params, w_gate, w_up)
+        for peer in groups[1]:
+            if peer >= half:
+                arrived[peer] = swap(after(sent[peer], up_mat), peer)
+        (down_mat,) = load_weights(params, after(w_down, up_mat))
+        for peer in groups[1]:
+            if peer < half:
+                arrived[peer] = swap(after(sent[peer], down_mat), peer)
+    else:
+        arrived[0] = exchange_all(send[0])
+
+    returned = []
     for group, count in zip(groups, counts):
-        arrived.append(travel(send[at : at + count], group))
-        at += count
-
-    big = [w_gate, w_up, w_down]
-    gate_mat, up_mat, down_mat, *mixes = pl.pallas_call(
-        functools.partial(prepare_kernel, order, relative),
-        name="prepare",
-        out_shape=results(
-            relative,
-            *[(w.shape, w.dtype) for w in big],
-            *[((SPLIT, 4 * lanes, len(group) * block), BF16) for group in groups],
-        ),
-        in_specs=in_smem(2) + in_vmem(2) + [pl.BlockSpec(memory_space=pltpu.HBM)] * 3,
-        out_specs=in_vmem(3 + len(groups)),
-        scratch_shapes=[pltpu.SemaphoreType.DMA((3,))],
-        cost_estimate=pl.CostEstimate(
-            flops=0, bytes_accessed=sum(2 * w.size * 2 for w in big), transcendentals=0
-        ),
-        compiler_params=params,
-    )(*from_hbm(old_holds, dup_experts, routes, gates, *big))
-
-    returned = []
-    for group, count, got in zip(groups, counts, arrived):
+        got = [arrived[peer] for peer in group[:count]]
         rows = min(count * piece, block * 8)
         back = pl.pallas_call(
             functools.partial(expert_kernel, count),
             name="expert_ffn",
-            out_shape=[jax.ShapeDtypeStruct((piece, cols), BF16)] * count,
+            out_shape=results(relative, *[((piece, cols), BF16)] * count),
             in_specs=in_vmem(3 + count),
             out_specs=in_vmem(count),
             scratch_shapes=[pltpu.VMEM((rows, features), BF16), pltpu.VMEM((rows, hidden), BF16)],
             cost_estimate=pl.CostEstimate(
                 flops=count * piece * features * hidden * 6,
-                bytes_accessed=sum(w.size * 2 for w in big),
+                bytes_accessed=w_gate.size * 6,
                 transcendentals=0,
             ),
             compiler_params=params,
         )(gate_mat, up_mat, down_mat, *got)
-        returned.append(travel(back, group))
+        if relative:
+            returned.append([swap(part, peer) for part, peer in zip(back, group)])
+        else:
+            returned.append([exchange_all(part) for part in back])
+
+    mixes = pl.pallas_call(
+        functools.partial(weights_kernel, order, relative),
+        name="gate_weights",
+        out_shape=results(
+            relative,
+            *[((SPLIT, 2 * lanes, 2 * len(group) * block), BF16) for group in groups],
+        ),
+        in_specs=in_smem(2) + in_vmem(2),
+        out_specs=in_vmem(len(groups)),
+        cost_estimate=pl.CostEstimate(flops=0, bytes_accessed=4 * MIB, transcendentals=0),
+        compiler_params=params,
+    )(*from_hbm(old_holds, dup_experts, after(routes, back[0]), gates))
 
     base = attn
     for at, (mix, back) in enumerate(zip(mixes, returned)):

time: 46.8 us -> 44.5 us (0.951)
  waiting for transfers between devices: 7.8 us -> 2.06 us
  starting transfers between devices: 22.6 us -> 26.3 us
  local copies, waits for them, and re-layouts: 1.31 us -> 0 us
  Pallas kernels: 14.7 us -> 15.8 us
    ppermute x14, waiting for transfers between devices: 7.8 us -> 2.06 us  [swap(): return lax.ppermute(value, 'expert', pairs)]
    ppermute x14, starting transfers between devices: 22.6 us -> 26.3 us  [swap(): return lax.ppermute(value, 'expert', pairs)]
    pallas_call x1 -> x3, Pallas kernels: 5.19 us -> 6.75 us  [the longest x2 5.45 us: load_weights(): pl.pallas_call(load_kernel, name='load_weights', out_shape=results(True,...]
    reshape x1 -> x0, local copies, waits for them, and re-layouts: 1.31 us -> none  [shards(): gain = norm_gain.reshape(1, features)]
  transfers between devices with their start and end apart: 14 -> 14, of which waited for: 5 -> 2; matrix products, arithmetic and copies ran while one was open for 0% -> 0% of each run, Pallas kernels for 22% -> 26%
where the time goes in v3:
time: 44.5 us; the launch traced here: 44.3 us
  starting transfers between devices  26.3 us (59%)
  Pallas kernels  15.8 us (36%)
  waiting for transfers between devices  2.06 us (5%)
    ppermute x14, starting transfers between devices, swap(): return lax.ppermute(value, 'expert', pairs)  26.3 us
    pallas_call x2, Pallas kernels, load_weights(): pl.pallas_call(load_kernel, name='load_weights', out_shape=results(True,...  5.45 us
    pallas_call x2, Pallas kernels, shards(): pl.pallas_call(functools.partial(expert_kernel, count), name='expert_ffn'...  4.29 us
    pallas_call x1, Pallas kernels, shards(): pl.pallas_call(functools.partial(front_kernel, order, relative), name='at...  2.99 us
    ppermute x14, waiting for transfers between devices, swap(): return lax.ppermute(value, 'expert', pairs)  2.06 us
    pallas_call x2, Pallas kernels, shards(): pl.pallas_call(combine_kernel, name='combine', out_shape=jax.ShapeDtypeSt...  1.78 us
    pallas_call x1, Pallas kernels, shards(): pl.pallas_call(functools.partial(weights_kernel, order, relative), name='...  1.3 us
  transfers between devices with their start and end apart: 14, of which 2 were waited for; matrix products, arithmetic and copies ran while one was open for 0% of the time, Pallas kernels for 26%

profile of v3, /device:TPU:0, one launch (start us, length us, event | category | flops | bytes accessed | tf_op | source)
XLA Modules:
  0.0 44.3 jit_solution(2524722583612962697)
XLA Ops:
  0.0 3.0 %attend_and_pack.1 = (f32[2,64,2560]{2,1,0:T(8,128)S(1)}, bf16[24,1920]{1,0:T(8,128)(2,1)S(1)}, bf16[24,1920]{1,0:T(8,128)(2,1)S(1)}, bf16[24,1920]{1,0:T(8,128)...) custom-call(s32[2,1,4]{2,1,0:T(1,128)} %lengths_ref.1, ...), custom_call_target="tpu_custom_call" | custom-call | tf_op jit(solution)/shard_map/attend_and_pack/pallas_call | solution.py:343
  3.0 4.1 %collective-permute-start.4 = (bf16[24,1920]{1,0:T(8,128)(2,1)S(1)}, bf16[24,1920]{1,0:T(8,128)(2,1)S(1)}, u32[]{:S(2)}, u32[]{:S(2)}) collective-permute-start(bf16[24,1920]{1,0:T(8,128)(2,1)S(1)} %get-tuple-element.47), channel_id=1, source_target_pairs={{0,4},{1,5},{2,6},{3,7},{4,0},{5,1},{6,2},{7,3},{8,12},{9,13},{10,... | collective-permute-start | bytes 276488 | tf_op jit(solution)/shard_map/ppermute | solution.py:288
  7.1 1.3 %collective-permute-start.5 = (bf16[24,1920]{1,0:T(8,128)(2,1)S(1)}, bf16[24,1920]{1,0:T(8,128)(2,1)S(1)}, u32[]{:S(2)}, u32[]{:S(2)}) collective-permute-start(bf16[24,1920]{1,0:T(8,128)(2,1)S(1)} %get-tuple-element.48), channel_id=1, source_target_pairs={{0,5},{1,4},{2,7},{3,6},{4,1},{5,0},{6,3},{7,2},{8,13},{9,12},{10,... | collective-permute-start | bytes 276488 | tf_op jit(solution)/shard_map/ppermute | solution.py:288
  8.4 0.2 collective-permute-start.6
  8.6 3.3 %load_weights.2 = (bf16[1,2560,768]{2,1,0:T(8,128)(2,1)S(1)}, bf16[1,2560,768]{2,1,0:T(8,128)(2,1)S(1)}) custom-call(bf16[1,2560,768]{2,1,0:T(8,128)(2,1)} %refs_0_.1, bf16[1,2560,768]{2,1,0:T(8,128)(2,1)} %refs_1_.1), custom_call_target="tpu_custom_call" | custom-call | bytes 15728640 | tf_op jit(solution)/shard_map/load_weights/pallas_call | solution.py:296
  12.0 3.9 %collective-permute-start = (bf16[24,1920]{1,0:T(8,128)(2,1)S(1)}, bf16[24,1920]{1,0:T(8,128)(2,1)S(1)}, u32[]{:S(2)}, u32[]{:S(2)}) collective-permute-start(bf16[24,1920]{1,0:T(8,128)(2,1)S(1)} %get-tuple-element.37), channel_id=1, source_target_pairs={{0,6},{1,7},{2,4},{3,5},{4,2},{5,3},{6,0},{7,1},{8,14},{9,15},{10,... | collective-permute-start | bytes 276488 | tf_op jit(solution)/shard_map/ppermute | solution.py:288
  15.9 1.2 %collective-permute-start.1 = (bf16[24,1920]{1,0:T(8,128)(2,1)S(1)}, bf16[24,1920]{1,0:T(8,128)(2,1)S(1)}, u32[]{:S(2)}, u32[]{:S(2)}) collective-permute-start(bf16[24,1920]{1,0:T(8,128)(2,1)S(1)} %get-tuple-element.39), channel_id=1, source_target_pairs={{0,7},{1,6},{2,5},{3,4},{4,3},{5,2},{6,1},{7,0},{8,15},{9,14},{10,... | collective-permute-start | bytes 276488 | tf_op jit(solution)/shard_map/ppermute | solution.py:288
  17.1 2.1 %load_weights.3.down_ref = bf16[1,768,2560]{2,1,0:T(8,128)(2,1)S(1)} custom-call(bf16[1,768,2560]{2,1,0:T(8,128)(2,1)} %refs_0_.2), custom_call_target="tpu_custom_call" | custom-call | bytes 7864320 | tf_op jit(solution)/shard_map/load_weights/pallas_call | solution.py:296
  19.2 0.0 collective-permute-done.4.rest_0_
  19.2 0.1 collective-permute-start.2
  19.3 0.0 collective-permute-done.5.rest_1_
  19.3 1.8 %collective-permute-start.3 = (bf16[24,1920]{1,0:T(8,128)(2,1)S(1)}, bf16[24,1920]{1,0:T(8,128)(2,1)S(1)}, u32[]{:S(2)}, u32[]{:S(2)}) collective-permute-start(bf16[24,1920]{1,0:T(8,128)(2,1)S(1)} %get-tuple-element.43), channel_id=1, source_target_pairs={{0,3},{1,2},{2,1},{3,0},{4,7},{5,6},{6,5},{7,4},{8,11},{9,10},{10,... | collective-permute-start | bytes 276488 | tf_op jit(solution)/shard_map/ppermute | solution.py:288
  21.1 0.0 collective-permute-done.6.rest_2_
  21.1 2.1 %expert_ffn.3 = (bf16[24,1920]{1,0:T(8,128)(2,1)S(1)}, bf16[24,1920]{1,0:T(8,128)(2,1)S(1)}, bf16[24,1920]{1,0:T(8,128)(2,1)S(1)}, bf16[24,1920]{1,0:T(8,128)(2,1)S(1)}) custom-call(bf16[1,2560,768]{2,1,0:T(8,128)(2,1)S(1)} %get-tuple-element.33.gate_ref, bf16[1,2560,768]{2,1,0:T(8,128)(2,1)S(1)} %get-tuple-element.34.up_ref, ...), custom_call_target="tpu_custom_call" | custom-call | flops 1132462080 | bytes 11796480 | tf_op jit(solution)/shard_map/expert_ffn/pallas_call | solution.py:377
  23.3 2.4 %collective-permute-start.7 = (bf16[24,1920]{1,0:T(8,128)(2,1)S(1)}, bf16[24,1920]{1,0:T(8,128)(2,1)S(1)}, u32[]{:S(2)}, u32[]{:S(2)}) collective-permute-start(bf16[24,1920]{1,0:T(8,128)(2,1)S(1)} %get-tuple-element.51), channel_id=1, source_target_pairs={{0,4},{1,5},{2,6},{3,7},{4,0},{5,1},{6,2},{7,3},{8,12},{9,13},{10,... | collective-permute-start | bytes 276488 | tf_op jit(solution)/shard_map/ppermute | solution.py:288
  25.7 0.0 collective-permute-done.rest_0_
  25.7 1.7 %collective-permute-start.8 = (bf16[24,1920]{1,0:T(8,128)(2,1)S(1)}, bf16[24,1920]{1,0:T(8,128)(2,1)S(1)}, u32[]{:S(2)}, u32[]{:S(2)}) collective-permute-start(bf16[24,1920]{1,0:T(8,128)(2,1)S(1)} %get-tuple-element.52), channel_id=1, source_target_pairs={{0,5},{1,4},{2,7},{3,6},{4,1},{5,0},{6,3},{7,2},{8,13},{9,12},{10,... | collective-permute-start | bytes 276488 | tf_op jit(solution)/shard_map/ppermute | solution.py:288
  27.4 0.0 collective-permute-done.1.rest_1_
  27.4 0.4 collective-permute-start.9
  27.7 0.0 collective-permute-done.2.rest_2_
  27.7 0.0 collective-permute-done.3.rest_3_
  27.7 2.1 %expert_ffn.2 = (bf16[24,1920]{1,0:T(8,128)(2,1)S(1)}, bf16[24,1920]{1,0:T(8,128)(2,1)S(1)}, bf16[24,1920]{1,0:T(8,128)(2,1)S(1)}, bf16[24,1920]{1,0:T(8,128)(2,1)S(1)}) custom-call(bf16[1,2560,768]{2,1,0:T(8,128)(2,1)S(1)} %get-tuple-element.33.gate_ref, bf16[1,2560,768]{2,1,0:T(8,128)(2,1)S(1)} %get-tuple-element.34.up_ref, ...), custom_call_target="tpu_custom_call" | custom-call | flops 1132462080 | bytes 11796480 | tf_op jit(solution)/shard_map/expert_ffn/pallas_call | solution.py:377
  29.9 4.8 %collective-permute-start.11 = (bf16[24,1920]{1,0:T(8,128)(2,1)S(1)}, bf16[24,1920]{1,0:T(8,128)(2,1)S(1)}, u32[]{:S(2)}, u32[]{:S(2)}) collective-permute-start(bf16[24,1920]{1,0:T(8,128)(2,1)S(1)} %get-tuple-element.56), channel_id=1, source_target_pairs={{0,7},{1,6},{2,5},{3,4},{4,3},{5,2},{6,1},{7,0},{8,15},{9,14},{10,... | collective-permute-start | bytes 276488 | tf_op jit(solution)/shard_map/ppermute | solution.py:288
  34.6 0.0 collective-permute-start.12
  34.7 2.0 %collective-permute-start.13 = (bf16[24,1920]{1,0:T(8,128)(2,1)S(1)}, bf16[24,1920]{1,0:T(8,128)(2,1)S(1)}, u32[]{:S(2)}, u32[]{:S(2)}) collective-permute-start(bf16[24,1920]{1,0:T(8,128)(2,1)S(1)} %get-tuple-element.58), channel_id=1, source_target_pairs={{0,3},{1,2},{2,1},{3,0},{4,7},{5,6},{6,5},{7,4},{8,11},{9,10},{10,... | collective-permute-start | bytes 276488 | tf_op jit(solution)/shard_map/ppermute | solution.py:288
  36.6 2.5 %collective-permute-start.10 = (bf16[24,1920]{1,0:T(8,128)(2,1)S(1)}, bf16[24,1920]{1,0:T(8,128)(2,1)S(1)}, u32[]{:S(2)}, u32[]{:S(2)}) collective-permute-start(bf16[24,1920]{1,0:T(8,128)(2,1)S(1)} %get-tuple-element.44), channel_id=1, source_target_pairs={{0,6},{1,7},{2,4},{3,5},{4,2},{5,3},{6,0},{7,1},{8,14},{9,15},{10,... | collective-permute-start | bytes 276488 | tf_op jit(solution)/shard_map/ppermute | solution.py:288
  39.1 1.3 %gate_weights.1 = (bf16[3,256,192]{2,1,0:T(8,128)(2,1)S(1)}, bf16[3,256,192]{2,1,0:T(8,128)(2,1)S(1)}) custom-call(s32[8]{0:T(128)} %holds_ref.3, s32[4]{0:T(128)} %dup_ref.3, s32[6,2,64]{2,1,0:T(2,128)} %bitcast.3, f32[6,2,64]{2,1,0:T(2,128)} %bitcast.4), custom_call_target="tpu_custom_call" | custom-call | bytes 4194304 | tf_op jit(solution)/shard_map/gate_weights/pallas_call | solution.py:396
  40.4 0.0 collective-permute-done.9.rest_2_
  40.4 0.5 %combine.2.base_ref = f32[2,64,2560]{2,1,0:T(8,128)S(1)} custom-call(f32[2,64,2560]{2,1,0:T(8,128)S(1)} %get-tuple-element.32.base_ref, bf16[3,256,192]{2,1,0:T(8,128)(2,1)S(1)} %get-tuple-element.46.mix_ref, bf16[24,1920]{1,0:T(8,128)(2,1)S(1)} %collective-permute-done.7.rest_0_, bf16[24,1920]{1,0:T(8,128)(2,1)S(1)} %collective-permute-done.8.rest_1_, ...), custom_call_target="tpu_custom_call" | custom-call | flops 251658240 | bytes 2621440 | tf_op jit(solution)/shard_map/combine/pallas_call | solution.py:412
  40.9 0.2 collective-permute-done.13.rest_3_
  41.1 1.9 %collective-permute-done.10.rest_0_ = bf16[24,1920]{1,0:T(8,128)(2,1)S(1)} collective-permute-done((bf16[24,1920]{1,0:T(8,128)(2,1)S(1)}, bf16[24,1920]{1,0:T(8,128)(2,1)S(1)}, u32[]{:S(2)}, u32[]{:S(2)}) %collective-permute-start.10) | collective-permute-done | bytes 92192 | tf_op jit(solution)/shard_map/ppermute | solution.py:288
  43.0 1.3 %combine.3 = bf16[2,64,2560]{2,1,0:T(8,128)(2,1)} custom-call(f32[2,64,2560]{2,1,0:T(8,128)S(1)} %combine.2.base_ref, bf16[3,256,192]{2,1,0:T(8,128)(2,1)S(1)} %get-tuple-element.55.mix_ref, bf16[24,1920]{1,0:T(8,128)(2,1)S(1)} %collective-permute-done.10.rest_0_, bf16[24,1920]{1,0:T(8,128)(2,1)S(1)} %collective-permute-done.11.rest_1_, ...), custom_call_target="tpu_custom_call" | custom-call | flops 251658240 | bytes 2621440 | tf_op jit(solution)/shard_map/combine/pallas_call | solution.py:412
  (4 shorter events, 0.0 us)
Async XLA Ops:
  3.0 16.2 %collective-permute-start.4 = (bf16[24,1920]{1,0:T(8,128)(2,1)S(1)}, bf16[24,1920]{1,0:T(8,128)(2,1)S(1)}, u32[]{:S(2)}, u32[]{:S(2)}) collective-permute-start(bf16[24,1920]{1,0:T(8,128)(2,1)S(1)} %get-tuple-element.47), channel_id=1, source_target_pairs={{0,4},{1,5},{2,6},{3,7},{4,0},{5,1},{6,2},{7,3},{8,12},{9,13},{10,... | collective-permute-start | bytes 276488 | tf_op jit(solution)/shard_map/ppermute | solution.py:288
  7.1 12.2 %collective-permute-start.5 = (bf16[24,1920]{1,0:T(8,128)(2,1)S(1)}, bf16[24,1920]{1,0:T(8,128)(2,1)S(1)}, u32[]{:S(2)}, u32[]{:S(2)}) collective-permute-start(bf16[24,1920]{1,0:T(8,128)(2,1)S(1)} %get-tuple-element.48), channel_id=1, source_target_pairs={{0,5},{1,4},{2,7},{3,6},{4,1},{5,0},{6,3},{7,2},{8,13},{9,12},{10,... | collective-permute-start | bytes 276488 | tf_op jit(solution)/shard_map/ppermute | solution.py:288
  8.4 12.7 %collective-permute-start.6 = (bf16[24,1920]{1,0:T(8,128)(2,1)S(1)}, bf16[24,1920]{1,0:T(8,128)(2,1)S(1)}, u32[]{:S(2)}, u32[]{:S(2)}) collective-permute-start(bf16[24,1920]{1,0:T(8,128)(2,1)S(1)} %get-tuple-element.49), channel_id=1, source_target_pairs={{0,1},{1,0},{2,3},{3,2},{4,5},{5,4},{6,7},{7,6},{8,9},{9,8},{10,11... | collective-permute-start | bytes 276488 | tf_op jit(solution)/shard_map/ppermute | solution.py:288
  12.0 13.7 %collective-permute-start = (bf16[24,1920]{1,0:T(8,128)(2,1)S(1)}, bf16[24,1920]{1,0:T(8,128)(2,1)S(1)}, u32[]{:S(2)}, u32[]{:S(2)}) collective-permute-start(bf16[24,1920]{1,0:T(8,128)(2,1)S(1)} %get-tuple-element.37), channel_id=1, source_target_pairs={{0,6},{1,7},{2,4},{3,5},{4,2},{5,3},{6,0},{7,1},{8,14},{9,15},{10,... | collective-permute-start | bytes 276488 | tf_op jit(solution)/shard_map/ppermute | solution.py:288
  15.9 11.5 %collective-permute-start.1 = (bf16[24,1920]{1,0:T(8,128)(2,1)S(1)}, bf16[24,1920]{1,0:T(8,128)(2,1)S(1)}, u32[]{:S(2)}, u32[]{:S(2)}) collective-permute-start(bf16[24,1920]{1,0:T(8,128)(2,1)S(1)} %get-tuple-element.39), channel_id=1, source_target_pairs={{0,7},{1,6},{2,5},{3,4},{4,3},{5,2},{6,1},{7,0},{8,15},{9,14},{10,... | collective-permute-start | bytes 276488 | tf_op jit(solution)/shard_map/ppermute | solution.py:288
  19.2 8.5 %collective-permute-start.2 = (bf16[24,1920]{1,0:T(8,128)(2,1)S(1)}, bf16[24,1920]{1,0:T(8,128)(2,1)S(1)}, u32[]{:S(2)}, u32[]{:S(2)}) collective-permute-start(bf16[24,1920]{1,0:T(8,128)(2,1)S(1)} %get-tuple-element.41), channel_id=1, source_target_pairs={{0,2},{1,3},{2,0},{3,1},{4,6},{5,7},{6,4},{7,5},{8,10},{9,11},{10,... | collective-permute-start | bytes 276488 | tf_op jit(solution)/shard_map/ppermute | solution.py:288
  19.3 8.4 %collective-permute-start.3 = (bf16[24,1920]{1,0:T(8,128)(2,1)S(1)}, bf16[24,1920]{1,0:T(8,128)(2,1)S(1)}, u32[]{:S(2)}, u32[]{:S(2)}) collective-permute-start(bf16[24,1920]{1,0:T(8,128)(2,1)S(1)} %get-tuple-element.43), channel_id=1, source_target_pairs={{0,3},{1,2},{2,1},{3,0},{4,7},{5,6},{6,5},{7,4},{8,11},{9,10},{10,... | collective-permute-start | bytes 276488 | tf_op jit(solution)/shard_map/ppermute | solution.py:288
  23.3 11.4 %collective-permute-start.7 = (bf16[24,1920]{1,0:T(8,128)(2,1)S(1)}, bf16[24,1920]{1,0:T(8,128)(2,1)S(1)}, u32[]{:S(2)}, u32[]{:S(2)}) collective-permute-start(bf16[24,1920]{1,0:T(8,128)(2,1)S(1)} %get-tuple-element.51), channel_id=1, source_target_pairs={{0,4},{1,5},{2,6},{3,7},{4,0},{5,1},{6,2},{7,3},{8,12},{9,13},{10,... | collective-permute-start | bytes 276488 | tf_op jit(solution)/shard_map/ppermute | solution.py:288
  25.7 10.9 %collective-permute-start.8 = (bf16[24,1920]{1,0:T(8,128)(2,1)S(1)}, bf16[24,1920]{1,0:T(8,128)(2,1)S(1)}, u32[]{:S(2)}, u32[]{:S(2)}) collective-permute-start(bf16[24,1920]{1,0:T(8,128)(2,1)S(1)} %get-tuple-element.52), channel_id=1, source_target_pairs={{0,5},{1,4},{2,7},{3,6},{4,1},{5,0},{6,3},{7,2},{8,13},{9,12},{10,... | collective-permute-start | bytes 276488 | tf_op jit(solution)/shard_map/ppermute | solution.py:288
  27.4 13.1 %collective-permute-start.9 = (bf16[24,1920]{1,0:T(8,128)(2,1)S(1)}, bf16[24,1920]{1,0:T(8,128)(2,1)S(1)}, u32[]{:S(2)}, u32[]{:S(2)}) collective-permute-start(bf16[24,1920]{1,0:T(8,128)(2,1)S(1)} %get-tuple-element.53), channel_id=1, source_target_pairs={{0,1},{1,0},{2,3},{3,2},{4,5},{5,4},{6,7},{7,6},{8,9},{9,8},{10,11... | collective-permute-start | bytes 276488 | tf_op jit(solution)/shard_map/ppermute | solution.py:288
  29.9 11.0 %collective-permute-start.11 = (bf16[24,1920]{1,0:T(8,128)(2,1)S(1)}, bf16[24,1920]{1,0:T(8,128)(2,1)S(1)}, u32[]{:S(2)}, u32[]{:S(2)}) collective-permute-start(bf16[24,1920]{1,0:T(8,128)(2,1)S(1)} %get-tuple-element.56), channel_id=1, source_target_pairs={{0,7},{1,6},{2,5},{3,4},{4,3},{5,2},{6,1},{7,0},{8,15},{9,14},{10,... | collective-permute-start | bytes 276488 | tf_op jit(solution)/shard_map/ppermute | solution.py:288
  34.6 6.3 %collective-permute-start.12 = (bf16[24,1920]{1,0:T(8,128)(2,1)S(1)}, bf16[24,1920]{1,0:T(8,128)(2,1)S(1)}, u32[]{:S(2)}, u32[]{:S(2)}) collective-permute-start(bf16[24,1920]{1,0:T(8,128)(2,1)S(1)} %get-tuple-element.57), channel_id=1, source_target_pairs={{0,2},{1,3},{2,0},{3,1},{4,6},{5,7},{6,4},{7,5},{8,10},{9,11},{10,... | collective-permute-start | bytes 276488 | tf_op jit(solution)/shard_map/ppermute | solution.py:288
  34.7 6.5 %collective-permute-start.13 = (bf16[24,1920]{1,0:T(8,128)(2,1)S(1)}, bf16[24,1920]{1,0:T(8,128)(2,1)S(1)}, u32[]{:S(2)}, u32[]{:S(2)}) collective-permute-start(bf16[24,1920]{1,0:T(8,128)(2,1)S(1)} %get-tuple-element.58), channel_id=1, source_target_pairs={{0,3},{1,2},{2,1},{3,0},{4,7},{5,6},{6,5},{7,4},{8,11},{9,10},{10,... | collective-permute-start | bytes 276488 | tf_op jit(solution)/shard_map/ppermute | solution.py:288
  36.6 6.3 %collective-permute-start.10 = (bf16[24,1920]{1,0:T(8,128)(2,1)S(1)}, bf16[24,1920]{1,0:T(8,128)(2,1)S(1)}, u32[]{:S(2)}, u32[]{:S(2)}) collective-permute-start(bf16[24,1920]{1,0:T(8,128)(2,1)S(1)} %get-tuple-element.44), channel_id=1, source_target_pairs={{0,6},{1,7},{2,4},{3,5},{4,2},{5,3},{6,0},{7,1},{8,14},{9,15},{10,... | collective-permute-start | bytes 276488 | tf_op jit(solution)/shard_map/ppermute | solution.py:288

commit v4 on v3

--- a/solution.py
+++ b/solution.py
@@ -14,6 +14,7 @@
 SPLIT = CAP // (PACK - CAP)
 GROUPS = 3
 PERMUTED_WIDTH = 8
+PEER_GROUPS = [[4, 7, 1, 0], [5, 6, 2, 3]]
 MIB = 1024 * 1024
 
 F32 = jnp.float32
@@ -129,27 +130,37 @@
     value_ref,
     routes_ref,
     gain_ref,
-    attn_ref,
     *rest,
 ):
-    *send_refs, normed_ref = rest
+    if relative:
+        gate_hbm, gate_ref, attn_ref, *send_refs, normed_ref, sem = rest
+        load = pltpu.make_async_copy(gate_hbm, gate_ref, sem)
+        load.start()
+    else:
+        attn_ref, *send_refs, normed_ref = rest
     batches, tokens, features = query_ref.shape
     piece, cols = send_refs[0].shape
     step = cols // SPLIT
-    for b in range(batches):
-        scale = attend(query_ref, key_ref, value_ref, lengths_ref, b, attn_ref)
-        normed_ref[b * tokens : (b + 1) * tokens, :] = (
-            attn_ref[b] * scale * gain_ref[...][None, :]
-        ).astype(BF16)
-    lead, trail, _ = slot_picks(order, relative, holds_ref, dup_ref, routes_ref)
-    tail = normed_ref[:, cols:features]
-    for j in range(SPLIT):
-        at = slice(j * step, (j + 1) * step)
-        picks = jnp.concatenate([lead, trail[j]], axis=1).astype(BF16)
-        source = jnp.concatenate([normed_ref[:, at], tail], axis=0)
-        packed = dot(picks, source)
-        for i, send_ref in enumerate(send_refs):
-            send_ref[:, at] = packed[i * piece : (i + 1) * piece].astype(BF16)
+
+    @pl.when(holds_ref[0] >= 0)
+    def _():
+        for b in range(batches):
+            scale = attend(query_ref, key_ref, value_ref, lengths_ref, b, attn_ref)
+            normed_ref[b * tokens : (b + 1) * tokens, :] = (
+                attn_ref[b] * scale * gain_ref[...][None, :]
+            ).astype(BF16)
+        lead, trail, _ = slot_picks(order, relative, holds_ref, dup_ref, routes_ref)
+        tail = normed_ref[:, cols:features]
+        for j in range(SPLIT):
+            at = slice(j * step, (j + 1) * step)
+            picks = jnp.concatenate([lead, trail[j]], axis=1).astype(BF16)
+            source = jnp.concatenate([normed_ref[:, at], tail], axis=0)
+            packed = dot(picks, source)
+            for i, send_ref in enumerate(send_refs):
+                send_ref[:, at] = packed[i * piece : (i + 1) * piece].astype(BF16)
+
+    if relative:
+        load.wait()
 
 
 def load_kernel(*refs):
@@ -275,12 +286,6 @@
     return [pl.BlockSpec(memory_space=pltpu.SMEM)] * count
 
 
-def peer_groups(width):
-    half = width // 2
-    far, near = list(range(half, width)), [1, 0] + list(range(2, half))
-    return [far[: half // 2] + near[: half // 2], far[half // 2 :] + near[half // 2 :]]
-
-
 def swap(value, peer):
     if peer == 0:
         return value
@@ -331,7 +336,7 @@
     cols = features * CAP // PACK
     hidden = w_gate.shape[2]
     relative = width == PERMUTED_WIDTH
-    groups = peer_groups(width) if relative else [list(range(width))]
+    groups = PEER_GROUPS if relative else [list(range(width))]
     order = [peer for group in groups for peer in group]
     block = GROUPS * PACK
     piece = block if relative else block * width
@@ -340,30 +345,38 @@
     routes = jnp.transpose(routes, (2, 0, 1))
     gates = jnp.transpose(gates, (2, 0, 1))
 
-    attn, *send = pl.pallas_call(
+    hbm = [pl.BlockSpec(memory_space=pltpu.HBM)] if relative else []
+    one = [pltpu.SemaphoreType.DMA(())] if relative else []
+    weight = [(w_gate.shape, w_gate.dtype)] if relative else []
+    front = pl.pallas_call(
         functools.partial(front_kernel, order, relative),
         name="attend_and_pack",
         out_shape=results(
-            relative, ((batches, tokens, features), F32), *[((piece, cols), BF16)] * sum(counts)
+            relative,
+            *weight,
+            ((batches, tokens, features), F32),
+            *[((piece, cols), BF16)] * sum(counts),
         ),
-        in_specs=in_smem(3) + in_vmem(5),
-        out_specs=in_vmem(1 + sum(counts)),
-        scratch_shapes=[pltpu.VMEM((lanes, features), BF16)],
+        in_specs=in_smem(3) + in_vmem(5) + hbm,
+        out_specs=in_vmem(len(weight) + 1 + sum(counts)),
+        scratch_shapes=[pltpu.VMEM((lanes, features), BF16)] + one,
         compiler_params=params,
-    )(*from_hbm(lengths, old_holds, dup_experts, query, keys, values, routes, norm_gain))
-
+    )(
+        *from_hbm(lengths, old_holds, dup_experts, query, keys, values, routes, norm_gain),
+        *from_hbm(*[w_gate] * len(weight)),
+    )
+    gate_mat, attn, *send = front if relative else (w_gate, *front)
     sent = dict(zip(order, send))
     arrived = {}
-    gate_mat, up_mat, down_mat = w_gate, w_up, w_down
+    up_mat, down_mat = w_up, w_down
     if relative:
         half = width // 2
         for peer in groups[0]:
             arrived[peer] = swap(sent[peer], peer)
-        gate_mat, up_mat = load_weights(params, w_gate, w_up)
+        up_mat, down_mat = load_weights(params, *[after(w, sent[0]) for w in (w_up, w_down)])
         for peer in groups[1]:
             if peer >= half:
-                arrived[peer] = swap(after(sent[peer], up_mat), peer)
-        (down_mat,) = load_weights(params, after(w_down, up_mat))
+                arrived[peer] = swap(after(sent[peer], down_mat), peer)
         for peer in groups[1]:
             if peer < half:
                 arrived[peer] = swap(after(sent[peer], down_mat), peer)

time: 44.5 us -> 42.7 us (0.960)
  Pallas kernels: 15.8 us -> 14 us
    pallas_call x2 -> x1, Pallas kernels: 5.45 us -> 3.33 us  [load_weights(): pl.pallas_call(load_kernel, name='load_weights', out_shape=results(True,...]
  transfers between devices with their start and end apart: 14 -> 14, of which waited for: 2 -> 3; matrix products, arithmetic and copies ran while one was open for 0% -> 0% of each run, Pallas kernels for 26% -> 22%
where the time goes in v4:
time: 42.7 us; the launch traced here: 42.5 us
  starting transfers between devices  26.1 us (61%)
  Pallas kernels  14 us (33%)
  waiting for transfers between devices  2.32 us (5%)
    ppermute x14, starting transfers between devices, swap(): return lax.ppermute(value, 'expert', pairs)  26.1 us
    pallas_call x2, Pallas kernels, shards(): pl.pallas_call(functools.partial(expert_kernel, count), name='expert_ffn'...  4.29 us
    pallas_call x1, Pallas kernels, load_weights(): pl.pallas_call(load_kernel, name='load_weights', out_shape=results(True,...  3.33 us
    pallas_call x1, Pallas kernels, shards(): pl.pallas_call(functools.partial(front_kernel, order, relative), name='at...  3.32 us
    ppermute x14, waiting for transfers between devices, swap(): return lax.ppermute(value, 'expert', pairs)  2.32 us
    pallas_call x2, Pallas kernels, shards(): pl.pallas_call(combine_kernel, name='combine', out_shape=jax.ShapeDtypeSt...  1.78 us
    pallas_call x1, Pallas kernels, shards(): pl.pallas_call(functools.partial(weights_kernel, order, relative), name='...  1.3 us
  transfers between devices with their start and end apart: 14, of which 3 were waited for; matrix products, arithmetic and copies ran while one was open for 0% of the time, Pallas kernels for 22%

profile of v4, /device:TPU:0, one launch (start us, length us, event | category | flops | bytes accessed | tf_op | source)
XLA Modules:
  0.0 42.5 jit_solution(1502211140789135497)
XLA Ops:
  0.0 3.3 %attend_and_pack.1 = (bf16[1,2560,768]{2,1,0:T(8,128)(2,1)S(1)}, f32[2,64,2560]{2,1,0:T(8,128)S(1)}, bf16[24,1920]{1,0:T(8,128)(2,1)S(1)}, bf16[24,1920]{1,0:T(8...) custom-call(s32[2,1,4]{2,1,0:T(1,128)} %lengths_ref.1, ...), custom_call_target="tpu_custom_call" | custom-call | tf_op jit(solution)/shard_map/attend_and_pack/pallas_call | solution.py:351
  3.3 4.1 %collective-permute-start.4 = (bf16[24,1920]{1,0:T(8,128)(2,1)S(1)}, bf16[24,1920]{1,0:T(8,128)(2,1)S(1)}, u32[]{:S(2)}, u32[]{:S(2)}) collective-permute-start(bf16[24,1920]{1,0:T(8,128)(2,1)S(1)} %get-tuple-element.52), channel_id=1, source_target_pairs={{0,4},{1,5},{2,6},{3,7},{4,0},{5,1},{6,2},{7,3},{8,12},{9,13},{10,... | collective-permute-start | bytes 276488 | tf_op jit(solution)/shard_map/ppermute | solution.py:293
  7.4 2.3 %collective-permute-start.5 = (bf16[24,1920]{1,0:T(8,128)(2,1)S(1)}, bf16[24,1920]{1,0:T(8,128)(2,1)S(1)}, u32[]{:S(2)}, u32[]{:S(2)}) collective-permute-start(bf16[24,1920]{1,0:T(8,128)(2,1)S(1)} %get-tuple-element.53), channel_id=1, source_target_pairs={{0,7},{1,6},{2,5},{3,4},{4,3},{5,2},{6,1},{7,0},{8,15},{9,14},{10,... | collective-permute-start | bytes 276488 | tf_op jit(solution)/shard_map/ppermute | solution.py:293
  9.7 0.5 %collective-permute-start.6 = (bf16[24,1920]{1,0:T(8,128)(2,1)S(1)}, bf16[24,1920]{1,0:T(8,128)(2,1)S(1)}, u32[]{:S(2)}, u32[]{:S(2)}) collective-permute-start(bf16[24,1920]{1,0:T(8,128)(2,1)S(1)} %get-tuple-element.54), channel_id=1, source_target_pairs={{0,1},{1,0},{2,3},{3,2},{4,5},{5,4},{6,7},{7,6},{8,9},{9,8},{10,11... | collective-permute-start | bytes 276488 | tf_op jit(solution)/shard_map/ppermute | solution.py:293
  10.2 3.3 %load_weights.1 = (bf16[1,2560,768]{2,1,0:T(8,128)(2,1)S(1)}, bf16[1,768,2560]{2,1,0:T(8,128)(2,1)S(1)}) custom-call(bf16[1,2560,768]{2,1,0:T(8,128)(2,1)} %refs_0_, bf16[1,768,2560]{2,1,0:T(8,128)(2,1)} %refs_1_), custom_call_target="tpu_custom_call" | custom-call | bytes 15728640 | tf_op jit(solution)/shard_map/load_weights/pallas_call | solution.py:301
  13.6 2.7 %collective-permute-start = (bf16[24,1920]{1,0:T(8,128)(2,1)S(1)}, bf16[24,1920]{1,0:T(8,128)(2,1)S(1)}, u32[]{:S(2)}, u32[]{:S(2)}) collective-permute-start(bf16[24,1920]{1,0:T(8,128)(2,1)S(1)} %get-tuple-element.42), channel_id=1, source_target_pairs={{0,5},{1,4},{2,7},{3,6},{4,1},{5,0},{6,3},{7,2},{8,13},{9,12},{10,... | collective-permute-start | bytes 276488 | tf_op jit(solution)/shard_map/ppermute | solution.py:293
  16.3 0.2 collective-permute-start.1
  16.5 0.0 collective-permute-done.4.rest_0_
  16.5 1.6 %collective-permute-start.2 = (bf16[24,1920]{1,0:T(8,128)(2,1)S(1)}, bf16[24,1920]{1,0:T(8,128)(2,1)S(1)}, u32[]{:S(2)}, u32[]{:S(2)}) collective-permute-start(bf16[24,1920]{1,0:T(8,128)(2,1)S(1)} %get-tuple-element.46), channel_id=1, source_target_pairs={{0,2},{1,3},{2,0},{3,1},{4,6},{5,7},{6,4},{7,5},{8,10},{9,11},{10,... | collective-permute-start | bytes 276488 | tf_op jit(solution)/shard_map/ppermute | solution.py:293
  18.1 0.0 collective-permute-done.5.rest_1_
  18.1 2.3 %collective-permute-start.3 = (bf16[24,1920]{1,0:T(8,128)(2,1)S(1)}, bf16[24,1920]{1,0:T(8,128)(2,1)S(1)}, u32[]{:S(2)}, u32[]{:S(2)}) collective-permute-start(bf16[24,1920]{1,0:T(8,128)(2,1)S(1)} %get-tuple-element.48), channel_id=1, source_target_pairs={{0,3},{1,2},{2,1},{3,0},{4,7},{5,6},{6,5},{7,4},{8,11},{9,10},{10,... | collective-permute-start | bytes 276488 | tf_op jit(solution)/shard_map/ppermute | solution.py:293
  20.4 0.0 collective-permute-done.6.rest_2_
  20.4 2.1 %expert_ffn.3 = (bf16[24,1920]{1,0:T(8,128)(2,1)S(1)}, bf16[24,1920]{1,0:T(8,128)(2,1)S(1)}, bf16[24,1920]{1,0:T(8,128)(2,1)S(1)}, bf16[24,1920]{1,0:T(8,128)(2,1)S(1)}) custom-call(bf16[1,2560,768]{2,1,0:T(8,128)(2,1)S(1)} %get-tuple-element.35.gate_ref, bf16[1,2560,768]{2,1,0:T(8,128)(2,1)S(1)} %get-tuple-element.39.up_ref, ...), custom_call_target="tpu_custom_call" | custom-call | flops 1132462080 | bytes 11796480 | tf_op jit(solution)/shard_map/expert_ffn/pallas_call | solution.py:390
  22.5 2.3 %collective-permute-start.7 = (bf16[24,1920]{1,0:T(8,128)(2,1)S(1)}, bf16[24,1920]{1,0:T(8,128)(2,1)S(1)}, u32[]{:S(2)}, u32[]{:S(2)}) collective-permute-start(bf16[24,1920]{1,0:T(8,128)(2,1)S(1)} %get-tuple-element.55), channel_id=1, source_target_pairs={{0,4},{1,5},{2,6},{3,7},{4,0},{5,1},{6,2},{7,3},{8,12},{9,13},{10,... | collective-permute-start | bytes 276488 | tf_op jit(solution)/shard_map/ppermute | solution.py:293
  24.8 0.0 collective-permute-done.rest_0_
  24.8 2.4 %collective-permute-start.8 = (bf16[24,1920]{1,0:T(8,128)(2,1)S(1)}, bf16[24,1920]{1,0:T(8,128)(2,1)S(1)}, u32[]{:S(2)}, u32[]{:S(2)}) collective-permute-start(bf16[24,1920]{1,0:T(8,128)(2,1)S(1)} %get-tuple-element.56), channel_id=1, source_target_pairs={{0,7},{1,6},{2,5},{3,4},{4,3},{5,2},{6,1},{7,0},{8,15},{9,14},{10,... | collective-permute-start | bytes 276488 | tf_op jit(solution)/shard_map/ppermute | solution.py:293
  27.3 0.0 collective-permute-done.1.rest_1_
  27.3 0.8 %collective-permute-start.9 = (bf16[24,1920]{1,0:T(8,128)(2,1)S(1)}, bf16[24,1920]{1,0:T(8,128)(2,1)S(1)}, u32[]{:S(2)}, u32[]{:S(2)}) collective-permute-start(bf16[24,1920]{1,0:T(8,128)(2,1)S(1)} %get-tuple-element.57), channel_id=1, source_target_pairs={{0,1},{1,0},{2,3},{3,2},{4,5},{5,4},{6,7},{7,6},{8,9},{9,8},{10,11... | collective-permute-start | bytes 276488 | tf_op jit(solution)/shard_map/ppermute | solution.py:293
  28.0 0.0 collective-permute-done.3.rest_3_
  28.0 2.1 %expert_ffn.2 = (bf16[24,1920]{1,0:T(8,128)(2,1)S(1)}, bf16[24,1920]{1,0:T(8,128)(2,1)S(1)}, bf16[24,1920]{1,0:T(8,128)(2,1)S(1)}, bf16[24,1920]{1,0:T(8,128)(2,1)S(1)}) custom-call(bf16[1,2560,768]{2,1,0:T(8,128)(2,1)S(1)} %get-tuple-element.35.gate_ref, bf16[1,2560,768]{2,1,0:T(8,128)(2,1)S(1)} %get-tuple-element.39.up_ref, ...), custom_call_target="tpu_custom_call" | custom-call | flops 1132462080 | bytes 11796480 | tf_op jit(solution)/shard_map/expert_ffn/pallas_call | solution.py:390
  30.2 2.1 %collective-permute-start.11 = (bf16[24,1920]{1,0:T(8,128)(2,1)S(1)}, bf16[24,1920]{1,0:T(8,128)(2,1)S(1)}, u32[]{:S(2)}, u32[]{:S(2)}) collective-permute-start(bf16[24,1920]{1,0:T(8,128)(2,1)S(1)} %get-tuple-element.60), channel_id=1, source_target_pairs={{0,6},{1,7},{2,4},{3,5},{4,2},{5,3},{6,0},{7,1},{8,14},{9,15},{10,... | collective-permute-start | bytes 276488 | tf_op jit(solution)/shard_map/ppermute | solution.py:293
  32.3 0.0 collective-permute-start.12
  32.3 2.3 %collective-permute-start.13 = (bf16[24,1920]{1,0:T(8,128)(2,1)S(1)}, bf16[24,1920]{1,0:T(8,128)(2,1)S(1)}, u32[]{:S(2)}, u32[]{:S(2)}) collective-permute-start(bf16[24,1920]{1,0:T(8,128)(2,1)S(1)} %get-tuple-element.62), channel_id=1, source_target_pairs={{0,3},{1,2},{2,1},{3,0},{4,7},{5,6},{6,5},{7,4},{8,11},{9,10},{10,... | collective-permute-start | bytes 276488 | tf_op jit(solution)/shard_map/ppermute | solution.py:293
  34.7 0.0 collective-permute-done.8.rest_1_
  34.7 2.4 %collective-permute-start.10 = (bf16[24,1920]{1,0:T(8,128)(2,1)S(1)}, bf16[24,1920]{1,0:T(8,128)(2,1)S(1)}, u32[]{:S(2)}, u32[]{:S(2)}) collective-permute-start(bf16[24,1920]{1,0:T(8,128)(2,1)S(1)} %get-tuple-element.49), channel_id=1, source_target_pairs={{0,5},{1,4},{2,7},{3,6},{4,1},{5,0},{6,3},{7,2},{8,13},{9,12},{10,... | collective-permute-start | bytes 276488 | tf_op jit(solution)/shard_map/ppermute | solution.py:293
  37.1 1.3 %gate_weights.1 = (bf16[3,256,192]{2,1,0:T(8,128)(2,1)S(1)}, bf16[3,256,192]{2,1,0:T(8,128)(2,1)S(1)}) custom-call(s32[8]{0:T(128)} %holds_ref.3, s32[4]{0:T(128)} %dup_ref.3, s32[6,2,64]{2,1,0:T(2,128)} %bitcast.3, f32[6,2,64]{2,1,0:T(2,128)} %bitcast.4), custom_call_target="tpu_custom_call" | custom-call | bytes 4194304 | tf_op jit(solution)/shard_map/gate_weights/pallas_call | solution.py:409
  38.4 0.5 %combine.2.base_ref = f32[2,64,2560]{2,1,0:T(8,128)S(1)} custom-call(f32[2,64,2560]{2,1,0:T(8,128)S(1)} %get-tuple-element.34.base_ref, bf16[3,256,192]{2,1,0:T(8,128)(2,1)S(1)} %get-tuple-element.51.mix_ref, bf16[24,1920]{1,0:T(8,128)(2,1)S(1)} %collective-permute-done.7.rest_0_, bf16[24,1920]{1,0:T(8,128)(2,1)S(1)} %collective-permute-done.8.rest_1_, ...), custom_call_target="tpu_custom_call" | custom-call | flops 251658240 | bytes 2621440 | tf_op jit(solution)/shard_map/combine/pallas_call | solution.py:425
  38.9 0.0 collective-permute-done.11.rest_1_
  38.9 0.6 %collective-permute-done.12.rest_2_ = bf16[24,1920]{1,0:T(8,128)(2,1)S(1)} collective-permute-done((bf16[24,1920]{1,0:T(8,128)(2,1)S(1)}, bf16[24,1920]{1,0:T(8,128)(2,1)S(1)}, u32[]{:S(2)}, u32[]{:S(2)}) %collective-permute-start.12) | collective-permute-done | bytes 92192 | tf_op jit(solution)/shard_map/ppermute | solution.py:293
  39.5 0.8 %collective-permute-done.13.rest_3_ = bf16[24,1920]{1,0:T(8,128)(2,1)S(1)} collective-permute-done((bf16[24,1920]{1,0:T(8,128)(2,1)S(1)}, bf16[24,1920]{1,0:T(8,128)(2,1)S(1)}, u32[]{:S(2)}, u32[]{:S(2)}) %collective-permute-start.13) | collective-permute-done | bytes 92192 | tf_op jit(solution)/shard_map/ppermute | solution.py:293
  40.3 0.9 %collective-permute-done.10.rest_0_ = bf16[24,1920]{1,0:T(8,128)(2,1)S(1)} collective-permute-done((bf16[24,1920]{1,0:T(8,128)(2,1)S(1)}, bf16[24,1920]{1,0:T(8,128)(2,1)S(1)}, u32[]{:S(2)}, u32[]{:S(2)}) %collective-permute-start.10) | collective-permute-done | bytes 92192 | tf_op jit(solution)/shard_map/ppermute | solution.py:293
  41.2 1.3 %combine.3 = bf16[2,64,2560]{2,1,0:T(8,128)(2,1)} custom-call(f32[2,64,2560]{2,1,0:T(8,128)S(1)} %combine.2.base_ref, bf16[3,256,192]{2,1,0:T(8,128)(2,1)S(1)} %get-tuple-element.59.mix_ref, bf16[24,1920]{1,0:T(8,128)(2,1)S(1)} %collective-permute-done.10.rest_0_, bf16[24,1920]{1,0:T(8,128)(2,1)S(1)} %collective-permute-done.11.rest_1_, ...), custom_call_target="tpu_custom_call" | custom-call | flops 251658240 | bytes 2621440 | tf_op jit(solution)/shard_map/combine/pallas_call | solution.py:425
  (3 shorter events, 0.0 us)
Async XLA Ops:
  3.3 13.2 %collective-permute-start.4 = (bf16[24,1920]{1,0:T(8,128)(2,1)S(1)}, bf16[24,1920]{1,0:T(8,128)(2,1)S(1)}, u32[]{:S(2)}, u32[]{:S(2)}) collective-permute-start(bf16[24,1920]{1,0:T(8,128)(2,1)S(1)} %get-tuple-element.52), channel_id=1, source_target_pairs={{0,4},{1,5},{2,6},{3,7},{4,0},{5,1},{6,2},{7,3},{8,12},{9,13},{10,... | collective-permute-start | bytes 276488 | tf_op jit(solution)/shard_map/ppermute | solution.py:293
  7.4 10.7 %collective-permute-start.5 = (bf16[24,1920]{1,0:T(8,128)(2,1)S(1)}, bf16[24,1920]{1,0:T(8,128)(2,1)S(1)}, u32[]{:S(2)}, u32[]{:S(2)}) collective-permute-start(bf16[24,1920]{1,0:T(8,128)(2,1)S(1)} %get-tuple-element.53), channel_id=1, source_target_pairs={{0,7},{1,6},{2,5},{3,4},{4,3},{5,2},{6,1},{7,0},{8,15},{9,14},{10,... | collective-permute-start | bytes 276488 | tf_op jit(solution)/shard_map/ppermute | solution.py:293
  9.7 10.6 %collective-permute-start.6 = (bf16[24,1920]{1,0:T(8,128)(2,1)S(1)}, bf16[24,1920]{1,0:T(8,128)(2,1)S(1)}, u32[]{:S(2)}, u32[]{:S(2)}) collective-permute-start(bf16[24,1920]{1,0:T(8,128)(2,1)S(1)} %get-tuple-element.54), channel_id=1, source_target_pairs={{0,1},{1,0},{2,3},{3,2},{4,5},{5,4},{6,7},{7,6},{8,9},{9,8},{10,11... | collective-permute-start | bytes 276488 | tf_op jit(solution)/shard_map/ppermute | solution.py:293
  13.6 11.2 %collective-permute-start = (bf16[24,1920]{1,0:T(8,128)(2,1)S(1)}, bf16[24,1920]{1,0:T(8,128)(2,1)S(1)}, u32[]{:S(2)}, u32[]{:S(2)}) collective-permute-start(bf16[24,1920]{1,0:T(8,128)(2,1)S(1)} %get-tuple-element.42), channel_id=1, source_target_pairs={{0,5},{1,4},{2,7},{3,6},{4,1},{5,0},{6,3},{7,2},{8,13},{9,12},{10,... | collective-permute-start | bytes 276488 | tf_op jit(solution)/shard_map/ppermute | solution.py:293
  16.3 11.0 %collective-permute-start.1 = (bf16[24,1920]{1,0:T(8,128)(2,1)S(1)}, bf16[24,1920]{1,0:T(8,128)(2,1)S(1)}, u32[]{:S(2)}, u32[]{:S(2)}) collective-permute-start(bf16[24,1920]{1,0:T(8,128)(2,1)S(1)} %get-tuple-element.44), channel_id=1, source_target_pairs={{0,6},{1,7},{2,4},{3,5},{4,2},{5,3},{6,0},{7,1},{8,14},{9,15},{10,... | collective-permute-start | bytes 276488 | tf_op jit(solution)/shard_map/ppermute | solution.py:293
  16.5 11.5 %collective-permute-start.2 = (bf16[24,1920]{1,0:T(8,128)(2,1)S(1)}, bf16[24,1920]{1,0:T(8,128)(2,1)S(1)}, u32[]{:S(2)}, u32[]{:S(2)}) collective-permute-start(bf16[24,1920]{1,0:T(8,128)(2,1)S(1)} %get-tuple-element.46), channel_id=1, source_target_pairs={{0,2},{1,3},{2,0},{3,1},{4,6},{5,7},{6,4},{7,5},{8,10},{9,11},{10,... | collective-permute-start | bytes 276488 | tf_op jit(solution)/shard_map/ppermute | solution.py:293
  18.1 10.0 %collective-permute-start.3 = (bf16[24,1920]{1,0:T(8,128)(2,1)S(1)}, bf16[24,1920]{1,0:T(8,128)(2,1)S(1)}, u32[]{:S(2)}, u32[]{:S(2)}) collective-permute-start(bf16[24,1920]{1,0:T(8,128)(2,1)S(1)} %get-tuple-element.48), channel_id=1, source_target_pairs={{0,3},{1,2},{2,1},{3,0},{4,7},{5,6},{6,5},{7,4},{8,11},{9,10},{10,... | collective-permute-start | bytes 276488 | tf_op jit(solution)/shard_map/ppermute | solution.py:293
  22.5 9.8 %collective-permute-start.7 = (bf16[24,1920]{1,0:T(8,128)(2,1)S(1)}, bf16[24,1920]{1,0:T(8,128)(2,1)S(1)}, u32[]{:S(2)}, u32[]{:S(2)}) collective-permute-start(bf16[24,1920]{1,0:T(8,128)(2,1)S(1)} %get-tuple-element.55), channel_id=1, source_target_pairs={{0,4},{1,5},{2,6},{3,7},{4,0},{5,1},{6,2},{7,3},{8,12},{9,13},{10,... | collective-permute-start | bytes 276488 | tf_op jit(solution)/shard_map/ppermute | solution.py:293
  24.8 9.9 %collective-permute-start.8 = (bf16[24,1920]{1,0:T(8,128)(2,1)S(1)}, bf16[24,1920]{1,0:T(8,128)(2,1)S(1)}, u32[]{:S(2)}, u32[]{:S(2)}) collective-permute-start(bf16[24,1920]{1,0:T(8,128)(2,1)S(1)} %get-tuple-element.56), channel_id=1, source_target_pairs={{0,7},{1,6},{2,5},{3,4},{4,3},{5,2},{6,1},{7,0},{8,15},{9,14},{10,... | collective-permute-start | bytes 276488 | tf_op jit(solution)/shard_map/ppermute | solution.py:293
  27.3 11.1 %collective-permute-start.9 = (bf16[24,1920]{1,0:T(8,128)(2,1)S(1)}, bf16[24,1920]{1,0:T(8,128)(2,1)S(1)}, u32[]{:S(2)}, u32[]{:S(2)}) collective-permute-start(bf16[24,1920]{1,0:T(8,128)(2,1)S(1)} %get-tuple-element.57), channel_id=1, source_target_pairs={{0,1},{1,0},{2,3},{3,2},{4,5},{5,4},{6,7},{7,6},{8,9},{9,8},{10,11... | collective-permute-start | bytes 276488 | tf_op jit(solution)/shard_map/ppermute | solution.py:293
  30.2 8.7 %collective-permute-start.11 = (bf16[24,1920]{1,0:T(8,128)(2,1)S(1)}, bf16[24,1920]{1,0:T(8,128)(2,1)S(1)}, u32[]{:S(2)}, u32[]{:S(2)}) collective-permute-start(bf16[24,1920]{1,0:T(8,128)(2,1)S(1)} %get-tuple-element.60), channel_id=1, source_target_pairs={{0,6},{1,7},{2,4},{3,5},{4,2},{5,3},{6,0},{7,1},{8,14},{9,15},{10,... | collective-permute-start | bytes 276488 | tf_op jit(solution)/shard_map/ppermute | solution.py:293
  32.3 7.1 %collective-permute-start.12 = (bf16[24,1920]{1,0:T(8,128)(2,1)S(1)}, bf16[24,1920]{1,0:T(8,128)(2,1)S(1)}, u32[]{:S(2)}, u32[]{:S(2)}) collective-permute-start(bf16[24,1920]{1,0:T(8,128)(2,1)S(1)} %get-tuple-element.61), channel_id=1, source_target_pairs={{0,2},{1,3},{2,0},{3,1},{4,6},{5,7},{6,4},{7,5},{8,10},{9,11},{10,... | collective-permute-start | bytes 276488 | tf_op jit(solution)/shard_map/ppermute | solution.py:293
  32.3 8.0 %collective-permute-start.13 = (bf16[24,1920]{1,0:T(8,128)(2,1)S(1)}, bf16[24,1920]{1,0:T(8,128)(2,1)S(1)}, u32[]{:S(2)}, u32[]{:S(2)}) collective-permute-start(bf16[24,1920]{1,0:T(8,128)(2,1)S(1)} %get-tuple-element.62), channel_id=1, source_target_pairs={{0,3},{1,2},{2,1},{3,0},{4,7},{5,6},{6,5},{7,4},{8,11},{9,10},{10,... | collective-permute-start | bytes 276488 | tf_op jit(solution)/shard_map/ppermute | solution.py:293
  34.7 6.5 %collective-permute-start.10 = (bf16[24,1920]{1,0:T(8,128)(2,1)S(1)}, bf16[24,1920]{1,0:T(8,128)(2,1)S(1)}, u32[]{:S(2)}, u32[]{:S(2)}) collective-permute-start(bf16[24,1920]{1,0:T(8,128)(2,1)S(1)} %get-tuple-element.49), channel_id=1, source_target_pairs={{0,5},{1,4},{2,7},{3,6},{4,1},{5,0},{6,3},{7,2},{8,13},{9,12},{10,... | collective-permute-start | bytes 276488 | tf_op jit(solution)/shard_map/ppermute | solution.py:293

commit v5 on v4

--- a/solution.py
+++ b/solution.py
@@ -119,37 +119,46 @@
     return lax.rsqrt(meansq + 1e-05)
 
 
-def front_kernel(
-    order,
-    relative,
-    lengths_ref,
-    holds_ref,
-    dup_ref,
-    query_ref,
-    key_ref,
-    value_ref,
-    routes_ref,
-    gain_ref,
-    *rest,
-):
+def front_kernel(order, relative, *refs):
+    sources, refs = refs[:8], refs[8:]
     if relative:
-        gate_hbm, gate_ref, attn_ref, *send_refs, normed_ref, sem = rest
-        load = pltpu.make_async_copy(gate_hbm, gate_ref, sem)
-        load.start()
+        gate_hbm, gate_ref, attn_ref, *refs = refs
     else:
-        attn_ref, *send_refs, normed_ref = rest
+        attn_ref, *refs = refs
+    send_refs, refs = refs[: -(len(sources) + 2)], refs[-(len(sources) + 2) :]
+    *targets, normed_ref, sems = refs
+    lengths_ref, holds_ref, dup_ref, routes_ref, gain_ref, query_ref, key_ref, value_ref = targets
     batches, tokens, features = query_ref.shape
     piece, cols = send_refs[0].shape
     step = cols // SPLIT
 
+    small = [pltpu.make_async_copy(sources[i], targets[i], sems.at[0, i]) for i in range(5)]
+    large = [
+        [
+            pltpu.make_async_copy(sources[i].at[b], targets[i].at[b], sems.at[1 + b, i])
+            for i in range(5, 8)
+        ]
+        for b in range(batches)
+    ]
+    for copy in small + [copy for copies in large for copy in copies]:
+        copy.start()
+    if relative:
+        load = pltpu.make_async_copy(gate_hbm, gate_ref, sems.at[1, 0])
+        load.start()
+    for copy in small:
+        copy.wait()
+
     @pl.when(holds_ref[0] >= 0)
     def _():
+        lead, trail, _ = slot_picks(order, relative, holds_ref, dup_ref, routes_ref)
+        for b in range(batches):
+            for copy in large[b]:
+                copy.wait()
         for b in range(batches):
             scale = attend(query_ref, key_ref, value_ref, lengths_ref, b, attn_ref)
             normed_ref[b * tokens : (b + 1) * tokens, :] = (
                 attn_ref[b] * scale * gain_ref[...][None, :]
             ).astype(BF16)
-        lead, trail, _ = slot_picks(order, relative, holds_ref, dup_ref, routes_ref)
         tail = normed_ref[:, cols:features]
         for j in range(SPLIT):
             at = slice(j * step, (j + 1) * step)
@@ -246,27 +255,43 @@
                 back_refs[i][theirs, at] = result[mine].astype(BF16)
 
 
-def combine_kernel(base_ref, mix_ref, *rest):
-    *back_refs, out_ref = rest
+def combine_kernel(last, base_ref, mix_ref, *rest):
+    if last:
+        *back_refs, out_hbm, out_ref, sems = rest
+    else:
+        *back_refs, out_ref = rest
     batches, tokens, features = base_ref.shape
     lanes = batches * tokens
     piece, cols = back_refs[0].shape
     step = cols // SPLIT
     tail = jnp.zeros((lanes, features - cols), F32)
 
-    def put(part, at):
+    def write(index, at):
+        return pltpu.make_async_copy(out_ref.at[:, :, at], out_hbm.at[:, :, at], sems.at[index])
+
+    def put(part, index, at):
         for b in range(batches):
             out_ref[b, :, at] = (base_ref[b, :, at] + part[b * tokens : (b + 1) * tokens]).astype(
                 out_ref.dtype
             )
+        if last:
+            write(index, at).start()
+
+    def columns(j):
+        return pl.ds(j * step, step)
 
     for j in range(SPLIT):
-        at = slice(j * step, (j + 1) * step)
+        at = columns(j)
         back = jnp.concatenate([back_ref[:, at] for back_ref in back_refs] * 2, axis=0)
         mixed = dot(mix_ref[j], back)
-        put(mixed[:lanes], at)
+        put(mixed[:lanes], j, at)
         tail = tail + mixed[lanes:]
-    put(tail, slice(cols, features))
+    rest_at = pl.ds(cols, features - cols)
+    put(tail, SPLIT, rest_at)
+    if last:
+        for j in range(SPLIT):
+            write(j, columns(j)).wait()
+        write(SPLIT, rest_at).wait()
 
 
 def results(in_vmem, *shapes):
@@ -345,9 +370,11 @@
     routes = jnp.transpose(routes, (2, 0, 1))
     gates = jnp.transpose(gates, (2, 0, 1))
 
-    hbm = [pl.BlockSpec(memory_space=pltpu.HBM)] if relative else []
-    one = [pltpu.SemaphoreType.DMA(())] if relative else []
     weight = [(w_gate.shape, w_gate.dtype)] if relative else []
+    front_args = from_hbm(
+        lengths, old_holds, dup_experts, routes, norm_gain, query, keys, values,
+        *[w_gate] * len(weight),
+    )
     front = pl.pallas_call(
         functools.partial(front_kernel, order, relative),
         name="attend_and_pack",
@@ -357,14 +384,13 @@
             ((batches, tokens, features), F32),
             *[((piece, cols), BF16)] * sum(counts),
         ),
-        in_specs=in_smem(3) + in_vmem(5) + hbm,
+        in_specs=[pl.BlockSpec(memory_space=pltpu.HBM)] * len(front_args),
         out_specs=in_vmem(len(weight) + 1 + sum(counts)),
-        scratch_shapes=[pltpu.VMEM((lanes, features), BF16)] + one,
+        scratch_shapes=[pltpu.SMEM(x.shape, x.dtype) for x in front_args[:3]]
+        + [pltpu.VMEM(x.shape, x.dtype) for x in front_args[3:8]]
+        + [pltpu.VMEM((lanes, features), BF16), pltpu.SemaphoreType.DMA((1 + batches, 8))],
         compiler_params=params,
-    )(
-        *from_hbm(lengths, old_holds, dup_experts, query, keys, values, routes, norm_gain),
-        *from_hbm(*[w_gate] * len(weight)),
-    )
+    )(*front_args)
     gate_mat, attn, *send = front if relative else (w_gate, *front)
     sent = dict(zip(order, send))
     arrived = {}
@@ -422,12 +448,15 @@
     base = attn
     for at, (mix, back) in enumerate(zip(mixes, returned)):
         last = at == len(groups) - 1
+        out = (attn.shape, BF16 if last else F32)
         base = pl.pallas_call(
-            combine_kernel,
+            functools.partial(combine_kernel, last),
             name="combine",
-            out_shape=jax.ShapeDtypeStruct(attn.shape, BF16 if last else F32),
+            out_shape=results(relative and not last, out)[0],
             in_specs=in_vmem(2 + len(back)),
-            out_specs=in_vmem(1)[0],
+            out_specs=pl.BlockSpec(memory_space=pltpu.HBM) if last else in_vmem(1)[0],
+            scratch_shapes=[pltpu.VMEM(*out)] * last
+            + [pltpu.SemaphoreType.DMA((SPLIT + 1,))] * last,
             cost_estimate=pl.CostEstimate(
                 flops=2 * mix.size * features // SPLIT,
                 bytes_accessed=attn.size * 8,

time: 42.7 us -> 42.3 us (level)
  no operation moved by 1% of the time
where the time goes in v5:
time: 42.3 us; the launch traced here: 42.1 us
  starting transfers between devices  26.1 us (62%)
  Pallas kernels  13.6 us (32%)
  waiting for transfers between devices  2.32 us (5%)
    ppermute x14, starting transfers between devices, swap(): return lax.ppermute(value, 'expert', pairs)  26.1 us
    pallas_call x2, Pallas kernels, shards(): pl.pallas_call(functools.partial(expert_kernel, count), name='expert_ffn'...  4.29 us
    pallas_call x1, Pallas kernels, load_weights(): pl.pallas_call(load_kernel, name='load_weights', out_shape=results(True,...  3.33 us
    pallas_call x1, Pallas kernels, shards(): pl.pallas_call(functools.partial(front_kernel, order, relative), name='at...  3.04 us
    ppermute x14, waiting for transfers between devices, swap(): return lax.ppermute(value, 'expert', pairs)  2.32 us
    pallas_call x2, Pallas kernels, shards(): pl.pallas_call(functools.partial(combine_kernel, last), name='combine', o...  1.68 us
    pallas_call x1, Pallas kernels, shards(): pl.pallas_call(functools.partial(weights_kernel, order, relative), name='...  1.3 us
  transfers between devices with their start and end apart: 14, of which 3 were waited for; matrix products, arithmetic and copies ran while one was open for 0% of the time, Pallas kernels for 22%

profile of v5, /device:TPU:0, one launch (start us, length us, event | category | flops | bytes accessed | tf_op | source)
XLA Modules:
  0.0 42.1 jit_solution(15389196115310760158)
XLA Ops:
  0.0 3.0 %attend_and_pack.1 = (bf16[1,2560,768]{2,1,0:T(8,128)(2,1)S(1)}, f32[2,64,2560]{2,1,0:T(8,128)S(1)}, bf16[24,1920]{1,0:T(8,128)(2,1)S(1)}, bf16[24,1920]{1,0:T(8...) custom-call(s32[2,1,4]{2,1,0:T(1,128)} %refs_0_.1, ...), custom_call_target="tpu_custom_call" | custom-call | tf_op jit(solution)/shard_map/attend_and_pack/pallas_call | solution.py:378
  3.0 4.1 %collective-permute-start.4 = (bf16[24,1920]{1,0:T(8,128)(2,1)S(1)}, bf16[24,1920]{1,0:T(8,128)(2,1)S(1)}, u32[]{:S(2)}, u32[]{:S(2)}) collective-permute-start(bf16[24,1920]{1,0:T(8,128)(2,1)S(1)} %get-tuple-element.52), channel_id=1, source_target_pairs={{0,4},{1,5},{2,6},{3,7},{4,0},{5,1},{6,2},{7,3},{8,12},{9,13},{10,... | collective-permute-start | bytes 276488 | tf_op jit(solution)/shard_map/ppermute | solution.py:318
  7.1 2.3 %collective-permute-start.5 = (bf16[24,1920]{1,0:T(8,128)(2,1)S(1)}, bf16[24,1920]{1,0:T(8,128)(2,1)S(1)}, u32[]{:S(2)}, u32[]{:S(2)}) collective-permute-start(bf16[24,1920]{1,0:T(8,128)(2,1)S(1)} %get-tuple-element.53), channel_id=1, source_target_pairs={{0,7},{1,6},{2,5},{3,4},{4,3},{5,2},{6,1},{7,0},{8,15},{9,14},{10,... | collective-permute-start | bytes 276488 | tf_op jit(solution)/shard_map/ppermute | solution.py:318
  9.4 0.5 %collective-permute-start.6 = (bf16[24,1920]{1,0:T(8,128)(2,1)S(1)}, bf16[24,1920]{1,0:T(8,128)(2,1)S(1)}, u32[]{:S(2)}, u32[]{:S(2)}) collective-permute-start(bf16[24,1920]{1,0:T(8,128)(2,1)S(1)} %get-tuple-element.54), channel_id=1, source_target_pairs={{0,1},{1,0},{2,3},{3,2},{4,5},{5,4},{6,7},{7,6},{8,9},{9,8},{10,11... | collective-permute-start | bytes 276488 | tf_op jit(solution)/shard_map/ppermute | solution.py:318
  9.9 3.3 %load_weights.1 = (bf16[1,2560,768]{2,1,0:T(8,128)(2,1)S(1)}, bf16[1,768,2560]{2,1,0:T(8,128)(2,1)S(1)}) custom-call(bf16[1,2560,768]{2,1,0:T(8,128)(2,1)} %refs_0_.2, bf16[1,768,2560]{2,1,0:T(8,128)(2,1)} %refs_1_.2), custom_call_target="tpu_custom_call" | custom-call | bytes 15728640 | tf_op jit(solution)/shard_map/load_weights/pallas_call | solution.py:326
  13.3 2.7 %collective-permute-start = (bf16[24,1920]{1,0:T(8,128)(2,1)S(1)}, bf16[24,1920]{1,0:T(8,128)(2,1)S(1)}, u32[]{:S(2)}, u32[]{:S(2)}) collective-permute-start(bf16[24,1920]{1,0:T(8,128)(2,1)S(1)} %get-tuple-element.42), channel_id=1, source_target_pairs={{0,5},{1,4},{2,7},{3,6},{4,1},{5,0},{6,3},{7,2},{8,13},{9,12},{10,... | collective-permute-start | bytes 276488 | tf_op jit(solution)/shard_map/ppermute | solution.py:318
  16.0 0.2 collective-permute-start.1
  16.2 0.0 collective-permute-done.4.rest_0_
  16.2 1.6 %collective-permute-start.2 = (bf16[24,1920]{1,0:T(8,128)(2,1)S(1)}, bf16[24,1920]{1,0:T(8,128)(2,1)S(1)}, u32[]{:S(2)}, u32[]{:S(2)}) collective-permute-start(bf16[24,1920]{1,0:T(8,128)(2,1)S(1)} %get-tuple-element.46), channel_id=1, source_target_pairs={{0,2},{1,3},{2,0},{3,1},{4,6},{5,7},{6,4},{7,5},{8,10},{9,11},{10,... | collective-permute-start | bytes 276488 | tf_op jit(solution)/shard_map/ppermute | solution.py:318
  17.8 0.0 collective-permute-done.5.rest_1_
  17.8 2.3 %collective-permute-start.3 = (bf16[24,1920]{1,0:T(8,128)(2,1)S(1)}, bf16[24,1920]{1,0:T(8,128)(2,1)S(1)}, u32[]{:S(2)}, u32[]{:S(2)}) collective-permute-start(bf16[24,1920]{1,0:T(8,128)(2,1)S(1)} %get-tuple-element.48), channel_id=1, source_target_pairs={{0,3},{1,2},{2,1},{3,0},{4,7},{5,6},{6,5},{7,4},{8,11},{9,10},{10,... | collective-permute-start | bytes 276488 | tf_op jit(solution)/shard_map/ppermute | solution.py:318
  20.1 0.0 collective-permute-done.6.rest_2_
  20.1 2.1 %expert_ffn.3 = (bf16[24,1920]{1,0:T(8,128)(2,1)S(1)}, bf16[24,1920]{1,0:T(8,128)(2,1)S(1)}, bf16[24,1920]{1,0:T(8,128)(2,1)S(1)}, bf16[24,1920]{1,0:T(8,128)(2,1)S(1)}) custom-call(bf16[1,2560,768]{2,1,0:T(8,128)(2,1)S(1)} %get-tuple-element.35.gate_ref, bf16[1,2560,768]{2,1,0:T(8,128)(2,1)S(1)} %get-tuple-element.39.up_ref, ...), custom_call_target="tpu_custom_call" | custom-call | flops 1132462080 | bytes 11796480 | tf_op jit(solution)/shard_map/expert_ffn/pallas_call | solution.py:416
  22.2 2.3 %collective-permute-start.7 = (bf16[24,1920]{1,0:T(8,128)(2,1)S(1)}, bf16[24,1920]{1,0:T(8,128)(2,1)S(1)}, u32[]{:S(2)}, u32[]{:S(2)}) collective-permute-start(bf16[24,1920]{1,0:T(8,128)(2,1)S(1)} %get-tuple-element.55), channel_id=1, source_target_pairs={{0,4},{1,5},{2,6},{3,7},{4,0},{5,1},{6,2},{7,3},{8,12},{9,13},{10,... | collective-permute-start | bytes 276488 | tf_op jit(solution)/shard_map/ppermute | solution.py:318
  24.5 0.0 collective-permute-done.rest_0_
  24.5 2.4 %collective-permute-start.8 = (bf16[24,1920]{1,0:T(8,128)(2,1)S(1)}, bf16[24,1920]{1,0:T(8,128)(2,1)S(1)}, u32[]{:S(2)}, u32[]{:S(2)}) collective-permute-start(bf16[24,1920]{1,0:T(8,128)(2,1)S(1)} %get-tuple-element.56), channel_id=1, source_target_pairs={{0,7},{1,6},{2,5},{3,4},{4,3},{5,2},{6,1},{7,0},{8,15},{9,14},{10,... | collective-permute-start | bytes 276488 | tf_op jit(solution)/shard_map/ppermute | solution.py:318
  27.0 0.0 collective-permute-done.1.rest_1_
  27.0 0.8 %collective-permute-start.9 = (bf16[24,1920]{1,0:T(8,128)(2,1)S(1)}, bf16[24,1920]{1,0:T(8,128)(2,1)S(1)}, u32[]{:S(2)}, u32[]{:S(2)}) collective-permute-start(bf16[24,1920]{1,0:T(8,128)(2,1)S(1)} %get-tuple-element.57), channel_id=1, source_target_pairs={{0,1},{1,0},{2,3},{3,2},{4,5},{5,4},{6,7},{7,6},{8,9},{9,8},{10,11... | collective-permute-start | bytes 276488 | tf_op jit(solution)/shard_map/ppermute | solution.py:318
  27.7 0.0 collective-permute-done.2.rest_2_
  27.8 2.1 %expert_ffn.2 = (bf16[24,1920]{1,0:T(8,128)(2,1)S(1)}, bf16[24,1920]{1,0:T(8,128)(2,1)S(1)}, bf16[24,1920]{1,0:T(8,128)(2,1)S(1)}, bf16[24,1920]{1,0:T(8,128)(2,1)S(1)}) custom-call(bf16[1,2560,768]{2,1,0:T(8,128)(2,1)S(1)} %get-tuple-element.35.gate_ref, bf16[1,2560,768]{2,1,0:T(8,128)(2,1)S(1)} %get-tuple-element.39.up_ref, ...), custom_call_target="tpu_custom_call" | custom-call | flops 1132462080 | bytes 11796480 | tf_op jit(solution)/shard_map/expert_ffn/pallas_call | solution.py:416
  29.9 2.1 %collective-permute-start.11 = (bf16[24,1920]{1,0:T(8,128)(2,1)S(1)}, bf16[24,1920]{1,0:T(8,128)(2,1)S(1)}, u32[]{:S(2)}, u32[]{:S(2)}) collective-permute-start(bf16[24,1920]{1,0:T(8,128)(2,1)S(1)} %get-tuple-element.60), channel_id=1, source_target_pairs={{0,6},{1,7},{2,4},{3,5},{4,2},{5,3},{6,0},{7,1},{8,14},{9,15},{10,... | collective-permute-start | bytes 276488 | tf_op jit(solution)/shard_map/ppermute | solution.py:318
  32.1 0.0 collective-permute-start.12
  32.1 2.3 %collective-permute-start.13 = (bf16[24,1920]{1,0:T(8,128)(2,1)S(1)}, bf16[24,1920]{1,0:T(8,128)(2,1)S(1)}, u32[]{:S(2)}, u32[]{:S(2)}) collective-permute-start(bf16[24,1920]{1,0:T(8,128)(2,1)S(1)} %get-tuple-element.62), channel_id=1, source_target_pairs={{0,3},{1,2},{2,1},{3,0},{4,7},{5,6},{6,5},{7,4},{8,11},{9,10},{10,... | collective-permute-start | bytes 276488 | tf_op jit(solution)/shard_map/ppermute | solution.py:318
  34.4 0.0 collective-permute-done.8.rest_1_
  34.4 2.4 %collective-permute-start.10 = (bf16[24,1920]{1,0:T(8,128)(2,1)S(1)}, bf16[24,1920]{1,0:T(8,128)(2,1)S(1)}, u32[]{:S(2)}, u32[]{:S(2)}) collective-permute-start(bf16[24,1920]{1,0:T(8,128)(2,1)S(1)} %get-tuple-element.49), channel_id=1, source_target_pairs={{0,5},{1,4},{2,7},{3,6},{4,1},{5,0},{6,3},{7,2},{8,13},{9,12},{10,... | collective-permute-start | bytes 276488 | tf_op jit(solution)/shard_map/ppermute | solution.py:318
  36.8 1.3 %gate_weights.1 = (bf16[3,256,192]{2,1,0:T(8,128)(2,1)S(1)}, bf16[3,256,192]{2,1,0:T(8,128)(2,1)S(1)}) custom-call(s32[8]{0:T(128)} %holds_ref.1, s32[4]{0:T(128)} %dup_ref.1, s32[6,2,64]{2,1,0:T(2,128)} %bitcast.3, f32[6,2,64]{2,1,0:T(2,128)} %bitcast.4), custom_call_target="tpu_custom_call" | custom-call | bytes 4194304 | tf_op jit(solution)/shard_map/gate_weights/pallas_call | solution.py:435
  38.1 0.5 %combine.2.base_ref = f32[2,64,2560]{2,1,0:T(8,128)S(1)} custom-call(f32[2,64,2560]{2,1,0:T(8,128)S(1)} %get-tuple-element.34.base_ref, bf16[3,256,192]{2,1,0:T(8,128)(2,1)S(1)} %get-tuple-element.51.mix_ref, bf16[24,1920]{1,0:T(8,128)(2,1)S(1)} %collective-permute-done.7.rest_0_, bf16[24,1920]{1,0:T(8,128)(2,1)S(1)} %collective-permute-done.8.rest_1_, ...), custom_call_target="tpu_custom_call" | custom-call | flops 251658240 | bytes 2621440 | tf_op jit(solution)/shard_map/combine/pallas_call | solution.py:452
  38.6 0.0 collective-permute-done.11.rest_1_
  38.6 0.6 %collective-permute-done.12.rest_2_ = bf16[24,1920]{1,0:T(8,128)(2,1)S(1)} collective-permute-done((bf16[24,1920]{1,0:T(8,128)(2,1)S(1)}, bf16[24,1920]{1,0:T(8,128)(2,1)S(1)}, u32[]{:S(2)}, u32[]{:S(2)}) %collective-permute-start.12) | collective-permute-done | bytes 92192 | tf_op jit(solution)/shard_map/ppermute | solution.py:318
  39.2 0.9 %collective-permute-done.13.rest_3_ = bf16[24,1920]{1,0:T(8,128)(2,1)S(1)} collective-permute-done((bf16[24,1920]{1,0:T(8,128)(2,1)S(1)}, bf16[24,1920]{1,0:T(8,128)(2,1)S(1)}, u32[]{:S(2)}, u32[]{:S(2)}) %collective-permute-start.13) | collective-permute-done | bytes 92192 | tf_op jit(solution)/shard_map/ppermute | solution.py:318
  40.0 0.9 %collective-permute-done.10.rest_0_ = bf16[24,1920]{1,0:T(8,128)(2,1)S(1)} collective-permute-done((bf16[24,1920]{1,0:T(8,128)(2,1)S(1)}, bf16[24,1920]{1,0:T(8,128)(2,1)S(1)}, u32[]{:S(2)}, u32[]{:S(2)}) %collective-permute-start.10) | collective-permute-done | bytes 92192 | tf_op jit(solution)/shard_map/ppermute | solution.py:318
  40.9 1.2 %combine.3 = bf16[2,64,2560]{2,1,0:T(8,128)(2,1)} custom-call(f32[2,64,2560]{2,1,0:T(8,128)S(1)} %combine.2.base_ref, bf16[3,256,192]{2,1,0:T(8,128)(2,1)S(1)} %get-tuple-element.59.mix_ref, bf16[24,1920]{1,0:T(8,128)(2,1)S(1)} %collective-permute-done.10.rest_0_, bf16[24,1920]{1,0:T(8,128)(2,1)S(1)} %collective-permute-done.11.rest_1_, ...), custom_call_target="tpu_custom_call" | custom-call | flops 251658240 | bytes 2621440 | tf_op jit(solution)/shard_map/combine/pallas_call | solution.py:452
  (3 shorter events, 0.0 us)
Async XLA Ops:
  3.0 13.2 %collective-permute-start.4 = (bf16[24,1920]{1,0:T(8,128)(2,1)S(1)}, bf16[24,1920]{1,0:T(8,128)(2,1)S(1)}, u32[]{:S(2)}, u32[]{:S(2)}) collective-permute-start(bf16[24,1920]{1,0:T(8,128)(2,1)S(1)} %get-tuple-element.52), channel_id=1, source_target_pairs={{0,4},{1,5},{2,6},{3,7},{4,0},{5,1},{6,2},{7,3},{8,12},{9,13},{10,... | collective-permute-start | bytes 276488 | tf_op jit(solution)/shard_map/ppermute | solution.py:318
  7.1 10.7 %collective-permute-start.5 = (bf16[24,1920]{1,0:T(8,128)(2,1)S(1)}, bf16[24,1920]{1,0:T(8,128)(2,1)S(1)}, u32[]{:S(2)}, u32[]{:S(2)}) collective-permute-start(bf16[24,1920]{1,0:T(8,128)(2,1)S(1)} %get-tuple-element.53), channel_id=1, source_target_pairs={{0,7},{1,6},{2,5},{3,4},{4,3},{5,2},{6,1},{7,0},{8,15},{9,14},{10,... | collective-permute-start | bytes 276488 | tf_op jit(solution)/shard_map/ppermute | solution.py:318
  9.4 10.6 %collective-permute-start.6 = (bf16[24,1920]{1,0:T(8,128)(2,1)S(1)}, bf16[24,1920]{1,0:T(8,128)(2,1)S(1)}, u32[]{:S(2)}, u32[]{:S(2)}) collective-permute-start(bf16[24,1920]{1,0:T(8,128)(2,1)S(1)} %get-tuple-element.54), channel_id=1, source_target_pairs={{0,1},{1,0},{2,3},{3,2},{4,5},{5,4},{6,7},{7,6},{8,9},{9,8},{10,11... | collective-permute-start | bytes 276488 | tf_op jit(solution)/shard_map/ppermute | solution.py:318
  13.3 11.2 %collective-permute-start = (bf16[24,1920]{1,0:T(8,128)(2,1)S(1)}, bf16[24,1920]{1,0:T(8,128)(2,1)S(1)}, u32[]{:S(2)}, u32[]{:S(2)}) collective-permute-start(bf16[24,1920]{1,0:T(8,128)(2,1)S(1)} %get-tuple-element.42), channel_id=1, source_target_pairs={{0,5},{1,4},{2,7},{3,6},{4,1},{5,0},{6,3},{7,2},{8,13},{9,12},{10,... | collective-permute-start | bytes 276488 | tf_op jit(solution)/shard_map/ppermute | solution.py:318
  16.0 11.0 %collective-permute-start.1 = (bf16[24,1920]{1,0:T(8,128)(2,1)S(1)}, bf16[24,1920]{1,0:T(8,128)(2,1)S(1)}, u32[]{:S(2)}, u32[]{:S(2)}) collective-permute-start(bf16[24,1920]{1,0:T(8,128)(2,1)S(1)} %get-tuple-element.44), channel_id=1, source_target_pairs={{0,6},{1,7},{2,4},{3,5},{4,2},{5,3},{6,0},{7,1},{8,14},{9,15},{10,... | collective-permute-start | bytes 276488 | tf_op jit(solution)/shard_map/ppermute | solution.py:318
  16.2 11.5 %collective-permute-start.2 = (bf16[24,1920]{1,0:T(8,128)(2,1)S(1)}, bf16[24,1920]{1,0:T(8,128)(2,1)S(1)}, u32[]{:S(2)}, u32[]{:S(2)}) collective-permute-start(bf16[24,1920]{1,0:T(8,128)(2,1)S(1)} %get-tuple-element.46), channel_id=1, source_target_pairs={{0,2},{1,3},{2,0},{3,1},{4,6},{5,7},{6,4},{7,5},{8,10},{9,11},{10,... | collective-permute-start | bytes 276488 | tf_op jit(solution)/shard_map/ppermute | solution.py:318
  17.8 10.0 %collective-permute-start.3 = (bf16[24,1920]{1,0:T(8,128)(2,1)S(1)}, bf16[24,1920]{1,0:T(8,128)(2,1)S(1)}, u32[]{:S(2)}, u32[]{:S(2)}) collective-permute-start(bf16[24,1920]{1,0:T(8,128)(2,1)S(1)} %get-tuple-element.48), channel_id=1, source_target_pairs={{0,3},{1,2},{2,1},{3,0},{4,7},{5,6},{6,5},{7,4},{8,11},{9,10},{10,... | collective-permute-start | bytes 276488 | tf_op jit(solution)/shard_map/ppermute | solution.py:318
  22.2 9.8 %collective-permute-start.7 = (bf16[24,1920]{1,0:T(8,128)(2,1)S(1)}, bf16[24,1920]{1,0:T(8,128)(2,1)S(1)}, u32[]{:S(2)}, u32[]{:S(2)}) collective-permute-start(bf16[24,1920]{1,0:T(8,128)(2,1)S(1)} %get-tuple-element.55), channel_id=1, source_target_pairs={{0,4},{1,5},{2,6},{3,7},{4,0},{5,1},{6,2},{7,3},{8,12},{9,13},{10,... | collective-permute-start | bytes 276488 | tf_op jit(solution)/shard_map/ppermute | solution.py:318
  24.5 9.9 %collective-permute-start.8 = (bf16[24,1920]{1,0:T(8,128)(2,1)S(1)}, bf16[24,1920]{1,0:T(8,128)(2,1)S(1)}, u32[]{:S(2)}, u32[]{:S(2)}) collective-permute-start(bf16[24,1920]{1,0:T(8,128)(2,1)S(1)} %get-tuple-element.56), channel_id=1, source_target_pairs={{0,7},{1,6},{2,5},{3,4},{4,3},{5,2},{6,1},{7,0},{8,15},{9,14},{10,... | collective-permute-start | bytes 276488 | tf_op jit(solution)/shard_map/ppermute | solution.py:318
  27.0 11.1 %collective-permute-start.9 = (bf16[24,1920]{1,0:T(8,128)(2,1)S(1)}, bf16[24,1920]{1,0:T(8,128)(2,1)S(1)}, u32[]{:S(2)}, u32[]{:S(2)}) collective-permute-start(bf16[24,1920]{1,0:T(8,128)(2,1)S(1)} %get-tuple-element.57), channel_id=1, source_target_pairs={{0,1},{1,0},{2,3},{3,2},{4,5},{5,4},{6,7},{7,6},{8,9},{9,8},{10,11... | collective-permute-start | bytes 276488 | tf_op jit(solution)/shard_map/ppermute | solution.py:318
  29.9 8.7 %collective-permute-start.11 = (bf16[24,1920]{1,0:T(8,128)(2,1)S(1)}, bf16[24,1920]{1,0:T(8,128)(2,1)S(1)}, u32[]{:S(2)}, u32[]{:S(2)}) collective-permute-start(bf16[24,1920]{1,0:T(8,128)(2,1)S(1)} %get-tuple-element.60), channel_id=1, source_target_pairs={{0,6},{1,7},{2,4},{3,5},{4,2},{5,3},{6,0},{7,1},{8,14},{9,15},{10,... | collective-permute-start | bytes 276488 | tf_op jit(solution)/shard_map/ppermute | solution.py:318
  32.1 7.1 %collective-permute-start.12 = (bf16[24,1920]{1,0:T(8,128)(2,1)S(1)}, bf16[24,1920]{1,0:T(8,128)(2,1)S(1)}, u32[]{:S(2)}, u32[]{:S(2)}) collective-permute-start(bf16[24,1920]{1,0:T(8,128)(2,1)S(1)} %get-tuple-element.61), channel_id=1, source_target_pairs={{0,2},{1,3},{2,0},{3,1},{4,6},{5,7},{6,4},{7,5},{8,10},{9,11},{10,... | collective-permute-start | bytes 276488 | tf_op jit(solution)/shard_map/ppermute | solution.py:318
  32.1 8.0 %collective-permute-start.13 = (bf16[24,1920]{1,0:T(8,128)(2,1)S(1)}, bf16[24,1920]{1,0:T(8,128)(2,1)S(1)}, u32[]{:S(2)}, u32[]{:S(2)}) collective-permute-start(bf16[24,1920]{1,0:T(8,128)(2,1)S(1)} %get-tuple-element.62), channel_id=1, source_target_pairs={{0,3},{1,2},{2,1},{3,0},{4,7},{5,6},{6,5},{7,4},{8,11},{9,10},{10,... | collective-permute-start | bytes 276488 | tf_op jit(solution)/shard_map/ppermute | solution.py:318
  34.4 6.5 %collective-permute-start.10 = (bf16[24,1920]{1,0:T(8,128)(2,1)S(1)}, bf16[24,1920]{1,0:T(8,128)(2,1)S(1)}, u32[]{:S(2)}, u32[]{:S(2)}) collective-permute-start(bf16[24,1920]{1,0:T(8,128)(2,1)S(1)} %get-tuple-element.49), channel_id=1, source_target_pairs={{0,5},{1,4},{2,7},{3,6},{4,1},{5,0},{6,3},{7,2},{8,13},{9,12},{10,... | collective-permute-start | bytes 276488 | tf_op jit(solution)/shard_map/ppermute | solution.py:318

commit v6 on v5

--- a/solution.py
+++ b/solution.py
@@ -400,9 +400,11 @@
         for peer in groups[0]:
             arrived[peer] = swap(sent[peer], peer)
         up_mat, down_mat = load_weights(params, *[after(w, sent[0]) for w in (w_up, w_down)])
+        wait = down_mat
         for peer in groups[1]:
             if peer >= half:
-                arrived[peer] = swap(after(sent[peer], down_mat), peer)
+                arrived[peer] = swap(after(sent[peer], wait), peer)
+                wait = (down_mat, arrived[groups[0][0]])
         for peer in groups[1]:
             if peer < half:
                 arrived[peer] = swap(after(sent[peer], down_mat), peer)

time: 42.3 us -> 41.9 us (level)
  waiting for transfers between devices: 2.32 us -> 0.73 us
  starting transfers between devices: 26.1 us -> 27.3 us
    ppermute x14, waiting for transfers between devices: 2.32 us -> 0.73 us  [swap(): return lax.ppermute(value, 'expert', pairs)]
    ppermute x14, starting transfers between devices: 26.1 us -> 27.3 us  [swap(): return lax.ppermute(value, 'expert', pairs)]
  transfers between devices with their start and end apart: 14 -> 14, of which waited for: 3 -> 1; matrix products, arithmetic and copies ran while one was open for 0% -> 0% of each run, Pallas kernels for 22% -> 22%
where the time goes in v6:
time: 41.9 us; the launch traced here: 41.8 us
  starting transfers between devices  27.3 us (65%)
  Pallas kernels  13.6 us (32%)
  waiting for transfers between devices  0.73 us (2%)
    ppermute x14, starting transfers between devices, swap(): return lax.ppermute(value, 'expert', pairs)  27.3 us
    pallas_call x2, Pallas kernels, shards(): pl.pallas_call(functools.partial(expert_kernel, count), name='expert_ffn'...  4.29 us
    pallas_call x1, Pallas kernels, load_weights(): pl.pallas_call(load_kernel, name='load_weights', out_shape=results(True,...  3.33 us
    pallas_call x1, Pallas kernels, shards(): pl.pallas_call(functools.partial(front_kernel, order, relative), name='at...  3.04 us
    pallas_call x2, Pallas kernels, shards(): pl.pallas_call(functools.partial(combine_kernel, last), name='combine', o...  1.67 us
    pallas_call x1, Pallas kernels, shards(): pl.pallas_call(functools.partial(weights_kernel, order, relative), name='...  1.3 us
  transfers between devices with their start and end apart: 14, of which 1 were waited for; matrix products, arithmetic and copies ran while one was open for 0% of the time, Pallas kernels for 22%

profile of v6, /device:TPU:0, one launch (start us, length us, event | category | flops | bytes accessed | tf_op | source)
XLA Modules:
  0.0 41.8 jit_solution(1152681627309704647)
XLA Ops:
  0.0 3.0 %attend_and_pack.1 = (bf16[1,2560,768]{2,1,0:T(8,128)(2,1)S(1)}, f32[2,64,2560]{2,1,0:T(8,128)S(1)}, bf16[24,1920]{1,0:T(8,128)(2,1)S(1)}, bf16[24,1920]{1,0:T(8...) custom-call(s32[2,1,4]{2,1,0:T(1,128)} %refs_0_.1, ...), custom_call_target="tpu_custom_call" | custom-call | tf_op jit(solution)/shard_map/attend_and_pack/pallas_call | solution.py:378
  3.0 4.1 %collective-permute-start.1 = (bf16[24,1920]{1,0:T(8,128)(2,1)S(1)}, bf16[24,1920]{1,0:T(8,128)(2,1)S(1)}, u32[]{:S(2)}, u32[]{:S(2)}) collective-permute-start(bf16[24,1920]{1,0:T(8,128)(2,1)S(1)} %get-tuple-element.44), channel_id=1, source_target_pairs={{0,4},{1,5},{2,6},{3,7},{4,0},{5,1},{6,2},{7,3},{8,12},{9,13},{10,... | collective-permute-start | bytes 276488 | tf_op jit(solution)/shard_map/ppermute | solution.py:318
  7.1 2.3 %collective-permute-start.5 = (bf16[24,1920]{1,0:T(8,128)(2,1)S(1)}, bf16[24,1920]{1,0:T(8,128)(2,1)S(1)}, u32[]{:S(2)}, u32[]{:S(2)}) collective-permute-start(bf16[24,1920]{1,0:T(8,128)(2,1)S(1)} %get-tuple-element.53), channel_id=1, source_target_pairs={{0,7},{1,6},{2,5},{3,4},{4,3},{5,2},{6,1},{7,0},{8,15},{9,14},{10,... | collective-permute-start | bytes 276488 | tf_op jit(solution)/shard_map/ppermute | solution.py:318
  9.4 0.5 %collective-permute-start.6 = (bf16[24,1920]{1,0:T(8,128)(2,1)S(1)}, bf16[24,1920]{1,0:T(8,128)(2,1)S(1)}, u32[]{:S(2)}, u32[]{:S(2)}) collective-permute-start(bf16[24,1920]{1,0:T(8,128)(2,1)S(1)} %get-tuple-element.54), channel_id=1, source_target_pairs={{0,1},{1,0},{2,3},{3,2},{4,5},{5,4},{6,7},{7,6},{8,9},{9,8},{10,11... | collective-permute-start | bytes 276488 | tf_op jit(solution)/shard_map/ppermute | solution.py:318
  9.9 3.3 %load_weights.1 = (bf16[1,2560,768]{2,1,0:T(8,128)(2,1)S(1)}, bf16[1,768,2560]{2,1,0:T(8,128)(2,1)S(1)}) custom-call(bf16[1,2560,768]{2,1,0:T(8,128)(2,1)} %refs_0_.2, bf16[1,768,2560]{2,1,0:T(8,128)(2,1)} %refs_1_.2), custom_call_target="tpu_custom_call" | custom-call | bytes 15728640 | tf_op jit(solution)/shard_map/load_weights/pallas_call | solution.py:326
  13.3 2.7 %collective-permute-start = (bf16[24,1920]{1,0:T(8,128)(2,1)S(1)}, bf16[24,1920]{1,0:T(8,128)(2,1)S(1)}, u32[]{:S(2)}, u32[]{:S(2)}) collective-permute-start(bf16[24,1920]{1,0:T(8,128)(2,1)S(1)} %get-tuple-element.42), channel_id=1, source_target_pairs={{0,5},{1,4},{2,7},{3,6},{4,1},{5,0},{6,3},{7,2},{8,13},{9,12},{10,... | collective-permute-start | bytes 276488 | tf_op jit(solution)/shard_map/ppermute | solution.py:318
  16.0 1.3 %collective-permute-start.3 = (bf16[24,1920]{1,0:T(8,128)(2,1)S(1)}, bf16[24,1920]{1,0:T(8,128)(2,1)S(1)}, u32[]{:S(2)}, u32[]{:S(2)}) collective-permute-start(bf16[24,1920]{1,0:T(8,128)(2,1)S(1)} %get-tuple-element.47), channel_id=1, source_target_pairs={{0,2},{1,3},{2,0},{3,1},{4,6},{5,7},{6,4},{7,5},{8,10},{9,11},{10,... | collective-permute-start | bytes 276488 | tf_op jit(solution)/shard_map/ppermute | solution.py:318
  17.3 0.0 collective-permute-done.1.rest_0_
  17.3 0.6 %collective-permute-start.4 = (bf16[24,1920]{1,0:T(8,128)(2,1)S(1)}, bf16[24,1920]{1,0:T(8,128)(2,1)S(1)}, u32[]{:S(2)}, u32[]{:S(2)}) collective-permute-start(bf16[24,1920]{1,0:T(8,128)(2,1)S(1)} %get-tuple-element.49), channel_id=1, source_target_pairs={{0,3},{1,2},{2,1},{3,0},{4,7},{5,6},{6,5},{7,4},{8,11},{9,10},{10,... | collective-permute-start | bytes 276488 | tf_op jit(solution)/shard_map/ppermute | solution.py:318
  18.0 0.0 collective-permute-done.5.rest_1_
  18.0 1.0 %collective-permute-start.2 = (bf16[24,1920]{1,0:T(8,128)(2,1)S(1)}, bf16[24,1920]{1,0:T(8,128)(2,1)S(1)}, u32[]{:S(2)}, u32[]{:S(2)}) collective-permute-start(bf16[24,1920]{1,0:T(8,128)(2,1)S(1)} %get-tuple-element.45), channel_id=1, source_target_pairs={{0,6},{1,7},{2,4},{3,5},{4,2},{5,3},{6,0},{7,1},{8,14},{9,15},{10,... | collective-permute-start | bytes 276488 | tf_op jit(solution)/shard_map/ppermute | solution.py:318
  18.9 0.0 collective-permute-done.6.rest_2_
  18.9 2.1 %expert_ffn.3 = (bf16[24,1920]{1,0:T(8,128)(2,1)S(1)}, bf16[24,1920]{1,0:T(8,128)(2,1)S(1)}, bf16[24,1920]{1,0:T(8,128)(2,1)S(1)}, bf16[24,1920]{1,0:T(8,128)(2,1)S(1)}) custom-call(bf16[1,2560,768]{2,1,0:T(8,128)(2,1)S(1)} %get-tuple-element.35.gate_ref, bf16[1,2560,768]{2,1,0:T(8,128)(2,1)S(1)} %get-tuple-element.39.up_ref, ...), custom_call_target="tpu_custom_call" | custom-call | flops 1132462080 | bytes 11796480 | tf_op jit(solution)/shard_map/expert_ffn/pallas_call | solution.py:418
  21.1 1.9 %collective-permute-start.7 = (bf16[24,1920]{1,0:T(8,128)(2,1)S(1)}, bf16[24,1920]{1,0:T(8,128)(2,1)S(1)}, u32[]{:S(2)}, u32[]{:S(2)}) collective-permute-start(bf16[24,1920]{1,0:T(8,128)(2,1)S(1)} %get-tuple-element.55), channel_id=1, source_target_pairs={{0,4},{1,5},{2,6},{3,7},{4,0},{5,1},{6,2},{7,3},{8,12},{9,13},{10,... | collective-permute-start | bytes 276488 | tf_op jit(solution)/shard_map/ppermute | solution.py:318
  23.0 0.0 collective-permute-done.rest_0_
  23.0 2.3 %collective-permute-start.8 = (bf16[24,1920]{1,0:T(8,128)(2,1)S(1)}, bf16[24,1920]{1,0:T(8,128)(2,1)S(1)}, u32[]{:S(2)}, u32[]{:S(2)}) collective-permute-start(bf16[24,1920]{1,0:T(8,128)(2,1)S(1)} %get-tuple-element.56), channel_id=1, source_target_pairs={{0,7},{1,6},{2,5},{3,4},{4,3},{5,2},{6,1},{7,0},{8,15},{9,14},{10,... | collective-permute-start | bytes 276488 | tf_op jit(solution)/shard_map/ppermute | solution.py:318
  25.3 0.0 collective-permute-done.3.rest_2_
  25.3 1.8 %collective-permute-start.9 = (bf16[24,1920]{1,0:T(8,128)(2,1)S(1)}, bf16[24,1920]{1,0:T(8,128)(2,1)S(1)}, u32[]{:S(2)}, u32[]{:S(2)}) collective-permute-start(bf16[24,1920]{1,0:T(8,128)(2,1)S(1)} %get-tuple-element.57), channel_id=1, source_target_pairs={{0,1},{1,0},{2,3},{3,2},{4,5},{5,4},{6,7},{7,6},{8,9},{9,8},{10,11... | collective-permute-start | bytes 276488 | tf_op jit(solution)/shard_map/ppermute | solution.py:318
  27.1 0.0 collective-permute-done.4.rest_3_
  27.1 0.0 collective-permute-done.2.rest_1_
  27.1 2.1 %expert_ffn.2 = (bf16[24,1920]{1,0:T(8,128)(2,1)S(1)}, bf16[24,1920]{1,0:T(8,128)(2,1)S(1)}, bf16[24,1920]{1,0:T(8,128)(2,1)S(1)}, bf16[24,1920]{1,0:T(8,128)(2,1)S(1)}) custom-call(bf16[1,2560,768]{2,1,0:T(8,128)(2,1)S(1)} %get-tuple-element.35.gate_ref, bf16[1,2560,768]{2,1,0:T(8,128)(2,1)S(1)} %get-tuple-element.39.up_ref, ...), custom_call_target="tpu_custom_call" | custom-call | flops 1132462080 | bytes 11796480 | tf_op jit(solution)/shard_map/expert_ffn/pallas_call | solution.py:418
  29.2 1.3 %collective-permute-start.11 = (bf16[24,1920]{1,0:T(8,128)(2,1)S(1)}, bf16[24,1920]{1,0:T(8,128)(2,1)S(1)}, u32[]{:S(2)}, u32[]{:S(2)}) collective-permute-start(bf16[24,1920]{1,0:T(8,128)(2,1)S(1)} %get-tuple-element.60), channel_id=1, source_target_pairs={{0,6},{1,7},{2,4},{3,5},{4,2},{5,3},{6,0},{7,1},{8,14},{9,15},{10,... | collective-permute-start | bytes 276488 | tf_op jit(solution)/shard_map/ppermute | solution.py:318
  30.5 3.5 %collective-permute-start.12 = (bf16[24,1920]{1,0:T(8,128)(2,1)S(1)}, bf16[24,1920]{1,0:T(8,128)(2,1)S(1)}, u32[]{:S(2)}, u32[]{:S(2)}) collective-permute-start(bf16[24,1920]{1,0:T(8,128)(2,1)S(1)} %get-tuple-element.61), channel_id=1, source_target_pairs={{0,2},{1,3},{2,0},{3,1},{4,6},{5,7},{6,4},{7,5},{8,10},{9,11},{10,... | collective-permute-start | bytes 276488 | tf_op jit(solution)/shard_map/ppermute | solution.py:318
  34.0 0.0 collective-permute-done.7.rest_0_
  34.0 0.0 collective-permute-start.13
  34.0 0.0 collective-permute-done.8.rest_1_
  34.0 4.0 %collective-permute-start.10 = (bf16[24,1920]{1,0:T(8,128)(2,1)S(1)}, bf16[24,1920]{1,0:T(8,128)(2,1)S(1)}, u32[]{:S(2)}, u32[]{:S(2)}) collective-permute-start(bf16[24,1920]{1,0:T(8,128)(2,1)S(1)} %get-tuple-element.50), channel_id=1, source_target_pairs={{0,5},{1,4},{2,7},{3,6},{4,1},{5,0},{6,3},{7,2},{8,13},{9,12},{10,... | collective-permute-start | bytes 276488 | tf_op jit(solution)/shard_map/ppermute | solution.py:318
  38.1 1.3 %gate_weights.1 = (bf16[3,256,192]{2,1,0:T(8,128)(2,1)S(1)}, bf16[3,256,192]{2,1,0:T(8,128)(2,1)S(1)}) custom-call(s32[8]{0:T(128)} %holds_ref.1, s32[4]{0:T(128)} %dup_ref.1, s32[6,2,64]{2,1,0:T(2,128)} %bitcast.3, f32[6,2,64]{2,1,0:T(2,128)} %bitcast.4), custom_call_target="tpu_custom_call" | custom-call | bytes 4194304 | tf_op jit(solution)/shard_map/gate_weights/pallas_call | solution.py:437
  39.4 0.5 %combine.2.base_ref = f32[2,64,2560]{2,1,0:T(8,128)S(1)} custom-call(f32[2,64,2560]{2,1,0:T(8,128)S(1)} %get-tuple-element.34.base_ref, bf16[3,256,192]{2,1,0:T(8,128)(2,1)S(1)} %get-tuple-element.52.mix_ref, bf16[24,1920]{1,0:T(8,128)(2,1)S(1)} %collective-permute-done.7.rest_0_, bf16[24,1920]{1,0:T(8,128)(2,1)S(1)} %collective-permute-done.8.rest_1_, ...), custom_call_target="tpu_custom_call" | custom-call | flops 251658240 | bytes 2621440 | tf_op jit(solution)/shard_map/combine/pallas_call | solution.py:454
  39.9 0.0 collective-permute-done.13.rest_3_
  39.9 0.7 %collective-permute-done.10.rest_0_ = bf16[24,1920]{1,0:T(8,128)(2,1)S(1)} collective-permute-done((bf16[24,1920]{1,0:T(8,128)(2,1)S(1)}, bf16[24,1920]{1,0:T(8,128)(2,1)S(1)}, u32[]{:S(2)}, u32[]{:S(2)}) %collective-permute-start.10) | collective-permute-done | bytes 92192 | tf_op jit(solution)/shard_map/ppermute | solution.py:318
  40.6 1.2 %combine.3 = bf16[2,64,2560]{2,1,0:T(8,128)(2,1)} custom-call(f32[2,64,2560]{2,1,0:T(8,128)S(1)} %combine.2.base_ref, bf16[3,256,192]{2,1,0:T(8,128)(2,1)S(1)} %get-tuple-element.59.mix_ref, bf16[24,1920]{1,0:T(8,128)(2,1)S(1)} %collective-permute-done.10.rest_0_, bf16[24,1920]{1,0:T(8,128)(2,1)S(1)} %collective-permute-done.11.rest_1_, ...), custom_call_target="tpu_custom_call" | custom-call | flops 251658240 | bytes 2621440 | tf_op jit(solution)/shard_map/combine/pallas_call | solution.py:454
  (3 shorter events, 0.0 us)
Async XLA Ops:
  3.0 14.3 %collective-permute-start.1 = (bf16[24,1920]{1,0:T(8,128)(2,1)S(1)}, bf16[24,1920]{1,0:T(8,128)(2,1)S(1)}, u32[]{:S(2)}, u32[]{:S(2)}) collective-permute-start(bf16[24,1920]{1,0:T(8,128)(2,1)S(1)} %get-tuple-element.44), channel_id=1, source_target_pairs={{0,4},{1,5},{2,6},{3,7},{4,0},{5,1},{6,2},{7,3},{8,12},{9,13},{10,... | collective-permute-start | bytes 276488 | tf_op jit(solution)/shard_map/ppermute | solution.py:318
  7.1 10.8 %collective-permute-start.5 = (bf16[24,1920]{1,0:T(8,128)(2,1)S(1)}, bf16[24,1920]{1,0:T(8,128)(2,1)S(1)}, u32[]{:S(2)}, u32[]{:S(2)}) collective-permute-start(bf16[24,1920]{1,0:T(8,128)(2,1)S(1)} %get-tuple-element.53), channel_id=1, source_target_pairs={{0,7},{1,6},{2,5},{3,4},{4,3},{5,2},{6,1},{7,0},{8,15},{9,14},{10,... | collective-permute-start | bytes 276488 | tf_op jit(solution)/shard_map/ppermute | solution.py:318
  9.4 9.5 %collective-permute-start.6 = (bf16[24,1920]{1,0:T(8,128)(2,1)S(1)}, bf16[24,1920]{1,0:T(8,128)(2,1)S(1)}, u32[]{:S(2)}, u32[]{:S(2)}) collective-permute-start(bf16[24,1920]{1,0:T(8,128)(2,1)S(1)} %get-tuple-element.54), channel_id=1, source_target_pairs={{0,1},{1,0},{2,3},{3,2},{4,5},{5,4},{6,7},{7,6},{8,9},{9,8},{10,11... | collective-permute-start | bytes 276488 | tf_op jit(solution)/shard_map/ppermute | solution.py:318
  13.3 9.7 %collective-permute-start = (bf16[24,1920]{1,0:T(8,128)(2,1)S(1)}, bf16[24,1920]{1,0:T(8,128)(2,1)S(1)}, u32[]{:S(2)}, u32[]{:S(2)}) collective-permute-start(bf16[24,1920]{1,0:T(8,128)(2,1)S(1)} %get-tuple-element.42), channel_id=1, source_target_pairs={{0,5},{1,4},{2,7},{3,6},{4,1},{5,0},{6,3},{7,2},{8,13},{9,12},{10,... | collective-permute-start | bytes 276488 | tf_op jit(solution)/shard_map/ppermute | solution.py:318
  16.0 9.3 %collective-permute-start.3 = (bf16[24,1920]{1,0:T(8,128)(2,1)S(1)}, bf16[24,1920]{1,0:T(8,128)(2,1)S(1)}, u32[]{:S(2)}, u32[]{:S(2)}) collective-permute-start(bf16[24,1920]{1,0:T(8,128)(2,1)S(1)} %get-tuple-element.47), channel_id=1, source_target_pairs={{0,2},{1,3},{2,0},{3,1},{4,6},{5,7},{6,4},{7,5},{8,10},{9,11},{10,... | collective-permute-start | bytes 276488 | tf_op jit(solution)/shard_map/ppermute | solution.py:318
  17.3 9.7 %collective-permute-start.4 = (bf16[24,1920]{1,0:T(8,128)(2,1)S(1)}, bf16[24,1920]{1,0:T(8,128)(2,1)S(1)}, u32[]{:S(2)}, u32[]{:S(2)}) collective-permute-start(bf16[24,1920]{1,0:T(8,128)(2,1)S(1)} %get-tuple-element.49), channel_id=1, source_target_pairs={{0,3},{1,2},{2,1},{3,0},{4,7},{5,6},{6,5},{7,4},{8,11},{9,10},{10,... | collective-permute-start | bytes 276488 | tf_op jit(solution)/shard_map/ppermute | solution.py:318
  18.0 9.1 %collective-permute-start.2 = (bf16[24,1920]{1,0:T(8,128)(2,1)S(1)}, bf16[24,1920]{1,0:T(8,128)(2,1)S(1)}, u32[]{:S(2)}, u32[]{:S(2)}) collective-permute-start(bf16[24,1920]{1,0:T(8,128)(2,1)S(1)} %get-tuple-element.45), channel_id=1, source_target_pairs={{0,6},{1,7},{2,4},{3,5},{4,2},{5,3},{6,0},{7,1},{8,14},{9,15},{10,... | collective-permute-start | bytes 276488 | tf_op jit(solution)/shard_map/ppermute | solution.py:318
  21.1 12.9 %collective-permute-start.7 = (bf16[24,1920]{1,0:T(8,128)(2,1)S(1)}, bf16[24,1920]{1,0:T(8,128)(2,1)S(1)}, u32[]{:S(2)}, u32[]{:S(2)}) collective-permute-start(bf16[24,1920]{1,0:T(8,128)(2,1)S(1)} %get-tuple-element.55), channel_id=1, source_target_pairs={{0,4},{1,5},{2,6},{3,7},{4,0},{5,1},{6,2},{7,3},{8,12},{9,13},{10,... | collective-permute-start | bytes 276488 | tf_op jit(solution)/shard_map/ppermute | solution.py:318
  23.0 11.0 %collective-permute-start.8 = (bf16[24,1920]{1,0:T(8,128)(2,1)S(1)}, bf16[24,1920]{1,0:T(8,128)(2,1)S(1)}, u32[]{:S(2)}, u32[]{:S(2)}) collective-permute-start(bf16[24,1920]{1,0:T(8,128)(2,1)S(1)} %get-tuple-element.56), channel_id=1, source_target_pairs={{0,7},{1,6},{2,5},{3,4},{4,3},{5,2},{6,1},{7,0},{8,15},{9,14},{10,... | collective-permute-start | bytes 276488 | tf_op jit(solution)/shard_map/ppermute | solution.py:318
  25.3 14.0 %collective-permute-start.9 = (bf16[24,1920]{1,0:T(8,128)(2,1)S(1)}, bf16[24,1920]{1,0:T(8,128)(2,1)S(1)}, u32[]{:S(2)}, u32[]{:S(2)}) collective-permute-start(bf16[24,1920]{1,0:T(8,128)(2,1)S(1)} %get-tuple-element.57), channel_id=1, source_target_pairs={{0,1},{1,0},{2,3},{3,2},{4,5},{5,4},{6,7},{7,6},{8,9},{9,8},{10,11... | collective-permute-start | bytes 276488 | tf_op jit(solution)/shard_map/ppermute | solution.py:318
  29.2 10.6 %collective-permute-start.11 = (bf16[24,1920]{1,0:T(8,128)(2,1)S(1)}, bf16[24,1920]{1,0:T(8,128)(2,1)S(1)}, u32[]{:S(2)}, u32[]{:S(2)}) collective-permute-start(bf16[24,1920]{1,0:T(8,128)(2,1)S(1)} %get-tuple-element.60), channel_id=1, source_target_pairs={{0,6},{1,7},{2,4},{3,5},{4,2},{5,3},{6,0},{7,1},{8,14},{9,15},{10,... | collective-permute-start | bytes 276488 | tf_op jit(solution)/shard_map/ppermute | solution.py:318
  30.5 9.3 %collective-permute-start.12 = (bf16[24,1920]{1,0:T(8,128)(2,1)S(1)}, bf16[24,1920]{1,0:T(8,128)(2,1)S(1)}, u32[]{:S(2)}, u32[]{:S(2)}) collective-permute-start(bf16[24,1920]{1,0:T(8,128)(2,1)S(1)} %get-tuple-element.61), channel_id=1, source_target_pairs={{0,2},{1,3},{2,0},{3,1},{4,6},{5,7},{6,4},{7,5},{8,10},{9,11},{10,... | collective-permute-start | bytes 276488 | tf_op jit(solution)/shard_map/ppermute | solution.py:318
  34.0 5.9 %collective-permute-start.13 = (bf16[24,1920]{1,0:T(8,128)(2,1)S(1)}, bf16[24,1920]{1,0:T(8,128)(2,1)S(1)}, u32[]{:S(2)}, u32[]{:S(2)}) collective-permute-start(bf16[24,1920]{1,0:T(8,128)(2,1)S(1)} %get-tuple-element.62), channel_id=1, source_target_pairs={{0,3},{1,2},{2,1},{3,0},{4,7},{5,6},{6,5},{7,4},{8,11},{9,10},{10,... | collective-permute-start | bytes 276488 | tf_op jit(solution)/shard_map/ppermute | solution.py:318
  34.0 6.6 %collective-permute-start.10 = (bf16[24,1920]{1,0:T(8,128)(2,1)S(1)}, bf16[24,1920]{1,0:T(8,128)(2,1)S(1)}, u32[]{:S(2)}, u32[]{:S(2)}) collective-permute-start(bf16[24,1920]{1,0:T(8,128)(2,1)S(1)} %get-tuple-element.50), channel_id=1, source_target_pairs={{0,5},{1,4},{2,7},{3,6},{4,1},{5,0},{6,3},{7,2},{8,13},{9,12},{10,... | collective-permute-start | bytes 276488 | tf_op jit(solution)/shard_map/ppermute | solution.py:318

commit v7 on v6

--- a/solution.py
+++ b/solution.py
@@ -430,6 +430,8 @@
             compiler_params=params,
         )(gate_mat, up_mat, down_mat, *got)
         if relative:
+            if returned:
+                back = [after(back[0], returned[0][0]), *back[1:]]
             returned.append([swap(part, peer) for part, peer in zip(back, group)])
         else:
             returned.append([exchange_all(part) for part in back])

time: 41.9 us -> 44.9 us (1.072)
  waiting for transfers between devices: 0.73 us -> 7.45 us
  starting transfers between devices: 27.3 us -> 23.6 us
    ppermute x14, waiting for transfers between devices: 0.73 us -> 7.45 us  [swap(): return lax.ppermute(value, 'expert', pairs)]
    ppermute x14, starting transfers between devices: 27.3 us -> 23.6 us  [swap(): return lax.ppermute(value, 'expert', pairs)]
  transfers between devices with their start and end apart: 14 -> 14, of which waited for: 1 -> 4; matrix products, arithmetic and copies ran while one was open for 0% -> 0% of each run, Pallas kernels for 22% -> 21%
where the time goes in v7:
time: 44.9 us; the launch traced here: 44.7 us
  starting transfers between devices  23.6 us (53%)
  Pallas kernels  13.6 us (30%)
  waiting for transfers between devices  7.45 us (17%)
    ppermute x14, starting transfers between devices, swap(): return lax.ppermute(value, 'expert', pairs)  23.6 us
    ppermute x14, waiting for transfers between devices, swap(): return lax.ppermute(value, 'expert', pairs)  7.45 us
    pallas_call x2, Pallas kernels, shards(): pl.pallas_call(functools.partial(expert_kernel, count), name='expert_ffn'...  4.29 us
    pallas_call x1, Pallas kernels, load_weights(): pl.pallas_call(load_kernel, name='load_weights', out_shape=results(True,...  3.33 us
    pallas_call x1, Pallas kernels, shards(): pl.pallas_call(functools.partial(front_kernel, order, relative), name='at...  3.04 us
    pallas_call x2, Pallas kernels, shards(): pl.pallas_call(functools.partial(combine_kernel, last), name='combine', o...  1.66 us
    pallas_call x1, Pallas kernels, shards(): pl.pallas_call(functools.partial(weights_kernel, order, relative), name='...  1.3 us
  transfers between devices with their start and end apart: 14, of which 4 were waited for; matrix products, arithmetic and copies ran while one was open for 0% of the time, Pallas kernels for 21%

profile of v7, /device:TPU:0, one launch (start us, length us, event | category | flops | bytes accessed | tf_op | source)
XLA Modules:
  0.0 44.7 jit_solution(7613170460621535676)
XLA Ops:
  0.0 3.0 %attend_and_pack.1 = (bf16[1,2560,768]{2,1,0:T(8,128)(2,1)S(1)}, f32[2,64,2560]{2,1,0:T(8,128)S(1)}, bf16[24,1920]{1,0:T(8,128)(2,1)S(1)}, bf16[24,1920]{1,0:T(8...) custom-call(s32[2,1,4]{2,1,0:T(1,128)} %refs_0_.1, ...), custom_call_target="tpu_custom_call" | custom-call | tf_op jit(solution)/shard_map/attend_and_pack/pallas_call | solution.py:378
  3.0 4.1 %collective-permute-start.1 = (bf16[24,1920]{1,0:T(8,128)(2,1)S(1)}, bf16[24,1920]{1,0:T(8,128)(2,1)S(1)}, u32[]{:S(2)}, u32[]{:S(2)}) collective-permute-start(bf16[24,1920]{1,0:T(8,128)(2,1)S(1)} %get-tuple-element.45), channel_id=1, source_target_pairs={{0,4},{1,5},{2,6},{3,7},{4,0},{5,1},{6,2},{7,3},{8,12},{9,13},{10,... | collective-permute-start | bytes 276488 | tf_op jit(solution)/shard_map/ppermute | solution.py:318
  7.1 2.3 %collective-permute-start.5 = (bf16[24,1920]{1,0:T(8,128)(2,1)S(1)}, bf16[24,1920]{1,0:T(8,128)(2,1)S(1)}, u32[]{:S(2)}, u32[]{:S(2)}) collective-permute-start(bf16[24,1920]{1,0:T(8,128)(2,1)S(1)} %get-tuple-element.52), channel_id=1, source_target_pairs={{0,7},{1,6},{2,5},{3,4},{4,3},{5,2},{6,1},{7,0},{8,15},{9,14},{10,... | collective-permute-start | bytes 276488 | tf_op jit(solution)/shard_map/ppermute | solution.py:318
  9.4 0.5 %collective-permute-start.6 = (bf16[24,1920]{1,0:T(8,128)(2,1)S(1)}, bf16[24,1920]{1,0:T(8,128)(2,1)S(1)}, u32[]{:S(2)}, u32[]{:S(2)}) collective-permute-start(bf16[24,1920]{1,0:T(8,128)(2,1)S(1)} %get-tuple-element.53), channel_id=1, source_target_pairs={{0,1},{1,0},{2,3},{3,2},{4,5},{5,4},{6,7},{7,6},{8,9},{9,8},{10,11... | collective-permute-start | bytes 276488 | tf_op jit(solution)/shard_map/ppermute | solution.py:318
  9.9 3.3 %load_weights.1 = (bf16[1,2560,768]{2,1,0:T(8,128)(2,1)S(1)}, bf16[1,768,2560]{2,1,0:T(8,128)(2,1)S(1)}) custom-call(bf16[1,2560,768]{2,1,0:T(8,128)(2,1)} %refs_0_.2, bf16[1,768,2560]{2,1,0:T(8,128)(2,1)} %refs_1_.2), custom_call_target="tpu_custom_call" | custom-call | bytes 15728640 | tf_op jit(solution)/shard_map/load_weights/pallas_call | solution.py:326
  13.3 2.7 %collective-permute-start = (bf16[24,1920]{1,0:T(8,128)(2,1)S(1)}, bf16[24,1920]{1,0:T(8,128)(2,1)S(1)}, u32[]{:S(2)}, u32[]{:S(2)}) collective-permute-start(bf16[24,1920]{1,0:T(8,128)(2,1)S(1)} %get-tuple-element.43), channel_id=1, source_target_pairs={{0,5},{1,4},{2,7},{3,6},{4,1},{5,0},{6,3},{7,2},{8,13},{9,12},{10,... | collective-permute-start | bytes 276488 | tf_op jit(solution)/shard_map/ppermute | solution.py:318
  16.0 1.3 %collective-permute-start.3 = (bf16[24,1920]{1,0:T(8,128)(2,1)S(1)}, bf16[24,1920]{1,0:T(8,128)(2,1)S(1)}, u32[]{:S(2)}, u32[]{:S(2)}) collective-permute-start(bf16[24,1920]{1,0:T(8,128)(2,1)S(1)} %get-tuple-element.48), channel_id=1, source_target_pairs={{0,2},{1,3},{2,0},{3,1},{4,6},{5,7},{6,4},{7,5},{8,10},{9,11},{10,... | collective-permute-start | bytes 276488 | tf_op jit(solution)/shard_map/ppermute | solution.py:318
  17.3 0.0 collective-permute-done.1.rest_0_
  17.3 0.6 %collective-permute-start.4 = (bf16[24,1920]{1,0:T(8,128)(2,1)S(1)}, bf16[24,1920]{1,0:T(8,128)(2,1)S(1)}, u32[]{:S(2)}, u32[]{:S(2)}) collective-permute-start(bf16[24,1920]{1,0:T(8,128)(2,1)S(1)} %get-tuple-element.50), channel_id=1, source_target_pairs={{0,3},{1,2},{2,1},{3,0},{4,7},{5,6},{6,5},{7,4},{8,11},{9,10},{10,... | collective-permute-start | bytes 276488 | tf_op jit(solution)/shard_map/ppermute | solution.py:318
  18.0 0.0 collective-permute-done.5.rest_1_
  18.0 1.0 %collective-permute-start.2 = (bf16[24,1920]{1,0:T(8,128)(2,1)S(1)}, bf16[24,1920]{1,0:T(8,128)(2,1)S(1)}, u32[]{:S(2)}, u32[]{:S(2)}) collective-permute-start(bf16[24,1920]{1,0:T(8,128)(2,1)S(1)} %get-tuple-element.46), channel_id=1, source_target_pairs={{0,6},{1,7},{2,4},{3,5},{4,2},{5,3},{6,0},{7,1},{8,14},{9,15},{10,... | collective-permute-start | bytes 276488 | tf_op jit(solution)/shard_map/ppermute | solution.py:318
  18.9 0.0 collective-permute-done.6.rest_2_
  18.9 2.1 %expert_ffn.3 = (bf16[24,1920]{1,0:T(8,128)(2,1)S(1)}, bf16[24,1920]{1,0:T(8,128)(2,1)S(1)}, bf16[24,1920]{1,0:T(8,128)(2,1)S(1)}, bf16[24,1920]{1,0:T(8,128)(2,1)S(1)}) custom-call(bf16[1,2560,768]{2,1,0:T(8,128)(2,1)S(1)} %get-tuple-element.36.gate_ref, bf16[1,2560,768]{2,1,0:T(8,128)(2,1)S(1)} %get-tuple-element.40.up_ref, ...), custom_call_target="tpu_custom_call" | custom-call | flops 1132462080 | bytes 11796480 | tf_op jit(solution)/shard_map/expert_ffn/pallas_call | solution.py:418
  21.1 1.9 %collective-permute-start.7 = (bf16[24,1920]{1,0:T(8,128)(2,1)S(1)}, bf16[24,1920]{1,0:T(8,128)(2,1)S(1)}, u32[]{:S(2)}, u32[]{:S(2)}) collective-permute-start(bf16[24,1920]{1,0:T(8,128)(2,1)S(1)} %get-tuple-element.54), channel_id=1, source_target_pairs={{0,4},{1,5},{2,6},{3,7},{4,0},{5,1},{6,2},{7,3},{8,12},{9,13},{10,... | collective-permute-start | bytes 276488 | tf_op jit(solution)/shard_map/ppermute | solution.py:318
  23.0 2.3 %collective-permute-start.8 = (bf16[24,1920]{1,0:T(8,128)(2,1)S(1)}, bf16[24,1920]{1,0:T(8,128)(2,1)S(1)}, u32[]{:S(2)}, u32[]{:S(2)}) collective-permute-start(bf16[24,1920]{1,0:T(8,128)(2,1)S(1)} %get-tuple-element.58), channel_id=1, source_target_pairs={{0,7},{1,6},{2,5},{3,4},{4,3},{5,2},{6,1},{7,0},{8,15},{9,14},{10,... | collective-permute-start | bytes 276488 | tf_op jit(solution)/shard_map/ppermute | solution.py:318
  25.3 0.0 collective-permute-done.3.rest_2_
  25.3 1.8 %collective-permute-start.9 = (bf16[24,1920]{1,0:T(8,128)(2,1)S(1)}, bf16[24,1920]{1,0:T(8,128)(2,1)S(1)}, u32[]{:S(2)}, u32[]{:S(2)}) collective-permute-start(bf16[24,1920]{1,0:T(8,128)(2,1)S(1)} %get-tuple-element.59), channel_id=1, source_target_pairs={{0,1},{1,0},{2,3},{3,2},{4,5},{5,4},{6,7},{7,6},{8,9},{9,8},{10,11... | collective-permute-start | bytes 276488 | tf_op jit(solution)/shard_map/ppermute | solution.py:318
  27.1 0.0 collective-permute-done.4.rest_3_
  27.1 0.0 collective-permute-done.2.rest_1_
  27.1 2.1 %expert_ffn.2 = (bf16[24,1920]{1,0:T(8,128)(2,1)S(1)}, bf16[24,1920]{1,0:T(8,128)(2,1)S(1)}, bf16[24,1920]{1,0:T(8,128)(2,1)S(1)}, bf16[24,1920]{1,0:T(8,128)(2,1)S(1)}) custom-call(bf16[1,2560,768]{2,1,0:T(8,128)(2,1)S(1)} %get-tuple-element.36.gate_ref, bf16[1,2560,768]{2,1,0:T(8,128)(2,1)S(1)} %get-tuple-element.40.up_ref, ...), custom_call_target="tpu_custom_call" | custom-call | flops 1132462080 | bytes 11796480 | tf_op jit(solution)/shard_map/expert_ffn/pallas_call | solution.py:418
  29.2 2.4 %collective-permute-done.7.rest_0_ = bf16[24,1920]{1,0:T(8,128)(2,1)S(1)} collective-permute-done((bf16[24,1920]{1,0:T(8,128)(2,1)S(1)}, bf16[24,1920]{1,0:T(8,128)(2,1)S(1)}, u32[]{:S(2)}, u32[]{:S(2)}) %collective-permute-start.7) | collective-permute-done | bytes 92192 | tf_op jit(solution)/shard_map/ppermute | solution.py:318
  31.6 0.0 collective-permute-start.10
  31.6 2.5 %collective-permute-start.11 = (bf16[24,1920]{1,0:T(8,128)(2,1)S(1)}, bf16[24,1920]{1,0:T(8,128)(2,1)S(1)}, u32[]{:S(2)}, u32[]{:S(2)}) collective-permute-start(bf16[24,1920]{1,0:T(8,128)(2,1)S(1)} %get-tuple-element.62), channel_id=1, source_target_pairs={{0,6},{1,7},{2,4},{3,5},{4,2},{5,3},{6,0},{7,1},{8,14},{9,15},{10,... | collective-permute-start | bytes 276488 | tf_op jit(solution)/shard_map/ppermute | solution.py:318
  34.1 1.3 %collective-permute-start.12 = (bf16[24,1920]{1,0:T(8,128)(2,1)S(1)}, bf16[24,1920]{1,0:T(8,128)(2,1)S(1)}, u32[]{:S(2)}, u32[]{:S(2)}) collective-permute-start(bf16[24,1920]{1,0:T(8,128)(2,1)S(1)} %get-tuple-element.63), channel_id=1, source_target_pairs={{0,2},{1,3},{2,0},{3,1},{4,6},{5,7},{6,4},{7,5},{8,10},{9,11},{10,... | collective-permute-start | bytes 276488 | tf_op jit(solution)/shard_map/ppermute | solution.py:318
  35.4 0.0 collective-permute-done.8.rest_1_
  35.4 1.3 %collective-permute-start.13 = (bf16[24,1920]{1,0:T(8,128)(2,1)S(1)}, bf16[24,1920]{1,0:T(8,128)(2,1)S(1)}, u32[]{:S(2)}, u32[]{:S(2)}) collective-permute-start(bf16[24,1920]{1,0:T(8,128)(2,1)S(1)} %get-tuple-element.64), channel_id=1, source_target_pairs={{0,3},{1,2},{2,1},{3,0},{4,7},{5,6},{6,5},{7,4},{8,11},{9,10},{10,... | collective-permute-start | bytes 276488 | tf_op jit(solution)/shard_map/ppermute | solution.py:318
  36.7 1.3 %gate_weights.1 = (bf16[3,256,192]{2,1,0:T(8,128)(2,1)S(1)}, bf16[3,256,192]{2,1,0:T(8,128)(2,1)S(1)}) custom-call(s32[8]{0:T(128)} %holds_ref.1, s32[4]{0:T(128)} %dup_ref.1, s32[6,2,64]{2,1,0:T(2,128)} %bitcast.3, f32[6,2,64]{2,1,0:T(2,128)} %bitcast.4), custom_call_target="tpu_custom_call" | custom-call | bytes 4194304 | tf_op jit(solution)/shard_map/gate_weights/pallas_call | solution.py:439
  38.0 0.5 %combine.2.base_ref = f32[2,64,2560]{2,1,0:T(8,128)S(1)} custom-call(f32[2,64,2560]{2,1,0:T(8,128)S(1)} %get-tuple-element.35.base_ref, bf16[3,256,192]{2,1,0:T(8,128)(2,1)S(1)} %get-tuple-element.57.mix_ref, bf16[24,1920]{1,0:T(8,128)(2,1)S(1)} %collective-permute-done.7.rest_0_, bf16[24,1920]{1,0:T(8,128)(2,1)S(1)} %collective-permute-done.8.rest_1_, ...), custom_call_target="tpu_custom_call" | custom-call | flops 251658240 | bytes 2621440 | tf_op jit(solution)/shard_map/combine/pallas_call | solution.py:456
  38.5 1.2 %collective-permute-done.10.rest_0_ = bf16[24,1920]{1,0:T(8,128)(2,1)S(1)} collective-permute-done((bf16[24,1920]{1,0:T(8,128)(2,1)S(1)}, bf16[24,1920]{1,0:T(8,128)(2,1)S(1)}, u32[]{:S(2)}, u32[]{:S(2)}) %collective-permute-start.10) | collective-permute-done | bytes 92192 | tf_op jit(solution)/shard_map/ppermute | solution.py:318
  39.7 2.1 %collective-permute-done.12.rest_2_ = bf16[24,1920]{1,0:T(8,128)(2,1)S(1)} collective-permute-done((bf16[24,1920]{1,0:T(8,128)(2,1)S(1)}, bf16[24,1920]{1,0:T(8,128)(2,1)S(1)}, u32[]{:S(2)}, u32[]{:S(2)}) %collective-permute-start.12) | collective-permute-done | bytes 92192 | tf_op jit(solution)/shard_map/ppermute | solution.py:318
  41.8 1.7 %collective-permute-done.13.rest_3_ = bf16[24,1920]{1,0:T(8,128)(2,1)S(1)} collective-permute-done((bf16[24,1920]{1,0:T(8,128)(2,1)S(1)}, bf16[24,1920]{1,0:T(8,128)(2,1)S(1)}, u32[]{:S(2)}, u32[]{:S(2)}) %collective-permute-start.13) | collective-permute-done | bytes 92192 | tf_op jit(solution)/shard_map/ppermute | solution.py:318
  43.5 1.2 %combine.3 = bf16[2,64,2560]{2,1,0:T(8,128)(2,1)} custom-call(f32[2,64,2560]{2,1,0:T(8,128)S(1)} %combine.2.base_ref, bf16[3,256,192]{2,1,0:T(8,128)(2,1)S(1)} %get-tuple-element.61.mix_ref, bf16[24,1920]{1,0:T(8,128)(2,1)S(1)} %collective-permute-done.10.rest_0_, bf16[24,1920]{1,0:T(8,128)(2,1)S(1)} %collective-permute-done.11.rest_1_, ...), custom_call_target="tpu_custom_call" | custom-call | flops 251658240 | bytes 2621440 | tf_op jit(solution)/shard_map/combine/pallas_call | solution.py:456
  (3 shorter events, 0.0 us)
Async XLA Ops:
  3.0 14.3 %collective-permute-start.1 = (bf16[24,1920]{1,0:T(8,128)(2,1)S(1)}, bf16[24,1920]{1,0:T(8,128)(2,1)S(1)}, u32[]{:S(2)}, u32[]{:S(2)}) collective-permute-start(bf16[24,1920]{1,0:T(8,128)(2,1)S(1)} %get-tuple-element.45), channel_id=1, source_target_pairs={{0,4},{1,5},{2,6},{3,7},{4,0},{5,1},{6,2},{7,3},{8,12},{9,13},{10,... | collective-permute-start | bytes 276488 | tf_op jit(solution)/shard_map/ppermute | solution.py:318
  7.1 10.8 %collective-permute-start.5 = (bf16[24,1920]{1,0:T(8,128)(2,1)S(1)}, bf16[24,1920]{1,0:T(8,128)(2,1)S(1)}, u32[]{:S(2)}, u32[]{:S(2)}) collective-permute-start(bf16[24,1920]{1,0:T(8,128)(2,1)S(1)} %get-tuple-element.52), channel_id=1, source_target_pairs={{0,7},{1,6},{2,5},{3,4},{4,3},{5,2},{6,1},{7,0},{8,15},{9,14},{10,... | collective-permute-start | bytes 276488 | tf_op jit(solution)/shard_map/ppermute | solution.py:318
  9.4 9.5 %collective-permute-start.6 = (bf16[24,1920]{1,0:T(8,128)(2,1)S(1)}, bf16[24,1920]{1,0:T(8,128)(2,1)S(1)}, u32[]{:S(2)}, u32[]{:S(2)}) collective-permute-start(bf16[24,1920]{1,0:T(8,128)(2,1)S(1)} %get-tuple-element.53), channel_id=1, source_target_pairs={{0,1},{1,0},{2,3},{3,2},{4,5},{5,4},{6,7},{7,6},{8,9},{9,8},{10,11... | collective-permute-start | bytes 276488 | tf_op jit(solution)/shard_map/ppermute | solution.py:318
  13.3 9.7 %collective-permute-start = (bf16[24,1920]{1,0:T(8,128)(2,1)S(1)}, bf16[24,1920]{1,0:T(8,128)(2,1)S(1)}, u32[]{:S(2)}, u32[]{:S(2)}) collective-permute-start(bf16[24,1920]{1,0:T(8,128)(2,1)S(1)} %get-tuple-element.43), channel_id=1, source_target_pairs={{0,5},{1,4},{2,7},{3,6},{4,1},{5,0},{6,3},{7,2},{8,13},{9,12},{10,... | collective-permute-start | bytes 276488 | tf_op jit(solution)/shard_map/ppermute | solution.py:318
  16.0 9.3 %collective-permute-start.3 = (bf16[24,1920]{1,0:T(8,128)(2,1)S(1)}, bf16[24,1920]{1,0:T(8,128)(2,1)S(1)}, u32[]{:S(2)}, u32[]{:S(2)}) collective-permute-start(bf16[24,1920]{1,0:T(8,128)(2,1)S(1)} %get-tuple-element.48), channel_id=1, source_target_pairs={{0,2},{1,3},{2,0},{3,1},{4,6},{5,7},{6,4},{7,5},{8,10},{9,11},{10,... | collective-permute-start | bytes 276488 | tf_op jit(solution)/shard_map/ppermute | solution.py:318
  17.3 9.7 %collective-permute-start.4 = (bf16[24,1920]{1,0:T(8,128)(2,1)S(1)}, bf16[24,1920]{1,0:T(8,128)(2,1)S(1)}, u32[]{:S(2)}, u32[]{:S(2)}) collective-permute-start(bf16[24,1920]{1,0:T(8,128)(2,1)S(1)} %get-tuple-element.50), channel_id=1, source_target_pairs={{0,3},{1,2},{2,1},{3,0},{4,7},{5,6},{6,5},{7,4},{8,11},{9,10},{10,... | collective-permute-start | bytes 276488 | tf_op jit(solution)/shard_map/ppermute | solution.py:318
  18.0 9.1 %collective-permute-start.2 = (bf16[24,1920]{1,0:T(8,128)(2,1)S(1)}, bf16[24,1920]{1,0:T(8,128)(2,1)S(1)}, u32[]{:S(2)}, u32[]{:S(2)}) collective-permute-start(bf16[24,1920]{1,0:T(8,128)(2,1)S(1)} %get-tuple-element.46), channel_id=1, source_target_pairs={{0,6},{1,7},{2,4},{3,5},{4,2},{5,3},{6,0},{7,1},{8,14},{9,15},{10,... | collective-permute-start | bytes 276488 | tf_op jit(solution)/shard_map/ppermute | solution.py:318
  21.1 10.5 %collective-permute-start.7 = (bf16[24,1920]{1,0:T(8,128)(2,1)S(1)}, bf16[24,1920]{1,0:T(8,128)(2,1)S(1)}, u32[]{:S(2)}, u32[]{:S(2)}) collective-permute-start(bf16[24,1920]{1,0:T(8,128)(2,1)S(1)} %get-tuple-element.54), channel_id=1, source_target_pairs={{0,4},{1,5},{2,6},{3,7},{4,0},{5,1},{6,2},{7,3},{8,12},{9,13},{10,... | collective-permute-start | bytes 276488 | tf_op jit(solution)/shard_map/ppermute | solution.py:318
  23.0 12.4 %collective-permute-start.8 = (bf16[24,1920]{1,0:T(8,128)(2,1)S(1)}, bf16[24,1920]{1,0:T(8,128)(2,1)S(1)}, u32[]{:S(2)}, u32[]{:S(2)}) collective-permute-start(bf16[24,1920]{1,0:T(8,128)(2,1)S(1)} %get-tuple-element.58), channel_id=1, source_target_pairs={{0,7},{1,6},{2,5},{3,4},{4,3},{5,2},{6,1},{7,0},{8,15},{9,14},{10,... | collective-permute-start | bytes 276488 | tf_op jit(solution)/shard_map/ppermute | solution.py:318
  25.3 12.7 %collective-permute-start.9 = (bf16[24,1920]{1,0:T(8,128)(2,1)S(1)}, bf16[24,1920]{1,0:T(8,128)(2,1)S(1)}, u32[]{:S(2)}, u32[]{:S(2)}) collective-permute-start(bf16[24,1920]{1,0:T(8,128)(2,1)S(1)} %get-tuple-element.59), channel_id=1, source_target_pairs={{0,1},{1,0},{2,3},{3,2},{4,5},{5,4},{6,7},{7,6},{8,9},{9,8},{10,11... | collective-permute-start | bytes 276488 | tf_op jit(solution)/shard_map/ppermute | solution.py:318
  31.6 8.1 %collective-permute-start.10 = (bf16[24,1920]{1,0:T(8,128)(2,1)S(1)}, bf16[24,1920]{1,0:T(8,128)(2,1)S(1)}, u32[]{:S(2)}, u32[]{:S(2)}) collective-permute-start(bf16[24,1920]{1,0:T(8,128)(2,1)S(1)} %get-tuple-element.55), channel_id=1, source_target_pairs={{0,5},{1,4},{2,7},{3,6},{4,1},{5,0},{6,3},{7,2},{8,13},{9,12},{10,... | collective-permute-start | bytes 276488 | tf_op jit(solution)/shard_map/ppermute | solution.py:318
  31.6 8.1 %collective-permute-start.11 = (bf16[24,1920]{1,0:T(8,128)(2,1)S(1)}, bf16[24,1920]{1,0:T(8,128)(2,1)S(1)}, u32[]{:S(2)}, u32[]{:S(2)}) collective-permute-start(bf16[24,1920]{1,0:T(8,128)(2,1)S(1)} %get-tuple-element.62), channel_id=1, source_target_pairs={{0,6},{1,7},{2,4},{3,5},{4,2},{5,3},{6,0},{7,1},{8,14},{9,15},{10,... | collective-permute-start | bytes 276488 | tf_op jit(solution)/shard_map/ppermute | solution.py:318
  34.1 7.7 %collective-permute-start.12 = (bf16[24,1920]{1,0:T(8,128)(2,1)S(1)}, bf16[24,1920]{1,0:T(8,128)(2,1)S(1)}, u32[]{:S(2)}, u32[]{:S(2)}) collective-permute-start(bf16[24,1920]{1,0:T(8,128)(2,1)S(1)} %get-tuple-element.63), channel_id=1, source_target_pairs={{0,2},{1,3},{2,0},{3,1},{4,6},{5,7},{6,4},{7,5},{8,10},{9,11},{10,... | collective-permute-start | bytes 276488 | tf_op jit(solution)/shard_map/ppermute | solution.py:318
  35.4 8.1 %collective-permute-start.13 = (bf16[24,1920]{1,0:T(8,128)(2,1)S(1)}, bf16[24,1920]{1,0:T(8,128)(2,1)S(1)}, u32[]{:S(2)}, u32[]{:S(2)}) collective-permute-start(bf16[24,1920]{1,0:T(8,128)(2,1)S(1)} %get-tuple-element.64), channel_id=1, source_target_pairs={{0,3},{1,2},{2,1},{3,0},{4,7},{5,6},{6,5},{7,4},{8,11},{9,10},{10,... | collective-permute-start | bytes 276488 | tf_op jit(solution)/shard_map/ppermute | solution.py:318

commit v8 on v6

--- a/solution.py
+++ b/solution.py
@@ -445,7 +445,7 @@
         out_specs=in_vmem(len(groups)),
         cost_estimate=pl.CostEstimate(flops=0, bytes_accessed=4 * MIB, transcendentals=0),
         compiler_params=params,
-    )(*from_hbm(old_holds, dup_experts, after(routes, back[0]), gates))
+    )(*from_hbm(old_holds, dup_experts, after(routes, arrived[groups[0][0]]), gates))
 
     base = attn
     for at, (mix, back) in enumerate(zip(mixes, returned)):

time: 41.9 us -> 45.6 us (1.088)
  waiting for transfers between devices: 0.73 us -> 6.05 us
  starting transfers between devices: 27.3 us -> 25.6 us
    ppermute x14, waiting for transfers between devices: 0.73 us -> 6.05 us  [swap(): return lax.ppermute(value, 'expert', pairs)]
    ppermute x14, starting transfers between devices: 27.3 us -> 25.6 us  [swap(): return lax.ppermute(value, 'expert', pairs)]
  transfers between devices with their start and end apart: 14 -> 14, of which waited for: 1 -> 4; matrix products, arithmetic and copies ran while one was open for 0% -> 0% of each run, Pallas kernels for 22% -> 21%
where the time goes in v8:
time: 45.6 us; the launch traced here: 45.4 us
  starting transfers between devices  25.6 us (56%)
  Pallas kernels  13.6 us (30%)
  waiting for transfers between devices  6.05 us (13%)
    ppermute x14, starting transfers between devices, swap(): return lax.ppermute(value, 'expert', pairs)  25.6 us
    ppermute x14, waiting for transfers between devices, swap(): return lax.ppermute(value, 'expert', pairs)  6.05 us
    pallas_call x2, Pallas kernels, shards(): pl.pallas_call(functools.partial(expert_kernel, count), name='expert_ffn'...  4.29 us
    pallas_call x1, Pallas kernels, load_weights(): pl.pallas_call(load_kernel, name='load_weights', out_shape=results(True,...  3.33 us
    pallas_call x1, Pallas kernels, shards(): pl.pallas_call(functools.partial(front_kernel, order, relative), name='at...  3.04 us
    pallas_call x2, Pallas kernels, shards(): pl.pallas_call(functools.partial(combine_kernel, last), name='combine', o...  1.67 us
    pallas_call x1, Pallas kernels, shards(): pl.pallas_call(functools.partial(weights_kernel, order, relative), name='...  1.3 us
  transfers between devices with their start and end apart: 14, of which 4 were waited for; matrix products, arithmetic and copies ran while one was open for 0% of the time, Pallas kernels for 21%

profile of v8, /device:TPU:0, one launch (start us, length us, event | category | flops | bytes accessed | tf_op | source)
XLA Modules:
  0.0 45.4 jit_solution(8460952150766641147)
XLA Ops:
  0.0 3.0 %attend_and_pack.1 = (bf16[1,2560,768]{2,1,0:T(8,128)(2,1)S(1)}, f32[2,64,2560]{2,1,0:T(8,128)S(1)}, bf16[24,1920]{1,0:T(8,128)(2,1)S(1)}, bf16[24,1920]{1,0:T(8...) custom-call(s32[2,1,4]{2,1,0:T(1,128)} %refs_0_.1, ...), custom_call_target="tpu_custom_call" | custom-call | tf_op jit(solution)/shard_map/attend_and_pack/pallas_call | solution.py:378
  3.0 4.1 %collective-permute-start = (bf16[24,1920]{1,0:T(8,128)(2,1)S(1)}, bf16[24,1920]{1,0:T(8,128)(2,1)S(1)}, u32[]{:S(2)}, u32[]{:S(2)}) collective-permute-start(bf16[24,1920]{1,0:T(8,128)(2,1)S(1)} %get-tuple-element.35), channel_id=1, source_target_pairs={{0,4},{1,5},{2,6},{3,7},{4,0},{5,1},{6,2},{7,3},{8,12},{9,13},{10,... | collective-permute-start | bytes 276488 | tf_op jit(solution)/shard_map/ppermute | solution.py:318
  7.1 2.3 %collective-permute-start.1 = (bf16[24,1920]{1,0:T(8,128)(2,1)S(1)}, bf16[24,1920]{1,0:T(8,128)(2,1)S(1)}, u32[]{:S(2)}, u32[]{:S(2)}) collective-permute-start(bf16[24,1920]{1,0:T(8,128)(2,1)S(1)} %get-tuple-element.44), channel_id=1, source_target_pairs={{0,7},{1,6},{2,5},{3,4},{4,3},{5,2},{6,1},{7,0},{8,15},{9,14},{10,... | collective-permute-start | bytes 276488 | tf_op jit(solution)/shard_map/ppermute | solution.py:318
  9.4 0.5 %collective-permute-start.2 = (bf16[24,1920]{1,0:T(8,128)(2,1)S(1)}, bf16[24,1920]{1,0:T(8,128)(2,1)S(1)}, u32[]{:S(2)}, u32[]{:S(2)}) collective-permute-start(bf16[24,1920]{1,0:T(8,128)(2,1)S(1)} %get-tuple-element.45), channel_id=1, source_target_pairs={{0,1},{1,0},{2,3},{3,2},{4,5},{5,4},{6,7},{7,6},{8,9},{9,8},{10,11... | collective-permute-start | bytes 276488 | tf_op jit(solution)/shard_map/ppermute | solution.py:318
  9.9 3.3 %load_weights.1 = (bf16[1,2560,768]{2,1,0:T(8,128)(2,1)S(1)}, bf16[1,768,2560]{2,1,0:T(8,128)(2,1)S(1)}) custom-call(bf16[1,2560,768]{2,1,0:T(8,128)(2,1)} %refs_0_.2, bf16[1,768,2560]{2,1,0:T(8,128)(2,1)} %refs_1_.2), custom_call_target="tpu_custom_call" | custom-call | bytes 15728640 | tf_op jit(solution)/shard_map/load_weights/pallas_call | solution.py:326
  13.3 0.6 %collective-permute-start.9 = (bf16[24,1920]{1,0:T(8,128)(2,1)S(1)}, bf16[24,1920]{1,0:T(8,128)(2,1)S(1)}, u32[]{:S(2)}, u32[]{:S(2)}) collective-permute-start(bf16[24,1920]{1,0:T(8,128)(2,1)S(1)} %get-tuple-element.58), channel_id=1, source_target_pairs={{0,3},{1,2},{2,1},{3,0},{4,7},{5,6},{6,5},{7,4},{8,11},{9,10},{10,... | collective-permute-start | bytes 276488 | tf_op jit(solution)/shard_map/ppermute | solution.py:318
  13.9 2.5 %collective-permute-start.8 = (bf16[24,1920]{1,0:T(8,128)(2,1)S(1)}, bf16[24,1920]{1,0:T(8,128)(2,1)S(1)}, u32[]{:S(2)}, u32[]{:S(2)}) collective-permute-start(bf16[24,1920]{1,0:T(8,128)(2,1)S(1)} %get-tuple-element.56), channel_id=1, source_target_pairs={{0,2},{1,3},{2,0},{3,1},{4,6},{5,7},{6,4},{7,5},{8,10},{9,11},{10,... | collective-permute-start | bytes 276488 | tf_op jit(solution)/shard_map/ppermute | solution.py:318
  16.3 1.6 %collective-permute-start.6 = (bf16[24,1920]{1,0:T(8,128)(2,1)S(1)}, bf16[24,1920]{1,0:T(8,128)(2,1)S(1)}, u32[]{:S(2)}, u32[]{:S(2)}) collective-permute-start(bf16[24,1920]{1,0:T(8,128)(2,1)S(1)} %get-tuple-element.52), channel_id=1, source_target_pairs={{0,5},{1,4},{2,7},{3,6},{4,1},{5,0},{6,3},{7,2},{8,13},{9,12},{10,... | collective-permute-start | bytes 276488 | tf_op jit(solution)/shard_map/ppermute | solution.py:318
  18.0 0.0 collective-permute-done.1.rest_1_
  18.0 1.0 %collective-permute-start.7 = (bf16[24,1920]{1,0:T(8,128)(2,1)S(1)}, bf16[24,1920]{1,0:T(8,128)(2,1)S(1)}, u32[]{:S(2)}, u32[]{:S(2)}) collective-permute-start(bf16[24,1920]{1,0:T(8,128)(2,1)S(1)} %get-tuple-element.54), channel_id=1, source_target_pairs={{0,6},{1,7},{2,4},{3,5},{4,2},{5,3},{6,0},{7,1},{8,14},{9,15},{10,... | collective-permute-start | bytes 276488 | tf_op jit(solution)/shard_map/ppermute | solution.py:318
  18.9 0.0 collective-permute-done.2.rest_2_
  18.9 2.1 %expert_ffn.2 = (bf16[24,1920]{1,0:T(8,128)(2,1)S(1)}, bf16[24,1920]{1,0:T(8,128)(2,1)S(1)}, bf16[24,1920]{1,0:T(8,128)(2,1)S(1)}, bf16[24,1920]{1,0:T(8,128)(2,1)S(1)}) custom-call(bf16[1,2560,768]{2,1,0:T(8,128)(2,1)S(1)} %get-tuple-element.38.gate_ref, bf16[1,2560,768]{2,1,0:T(8,128)(2,1)S(1)} %get-tuple-element.42.up_ref, ...), custom_call_target="tpu_custom_call" | custom-call | flops 1132462080 | bytes 11796480 | tf_op jit(solution)/shard_map/expert_ffn/pallas_call | solution.py:418
  21.1 1.9 %collective-permute-start.3 = (bf16[24,1920]{1,0:T(8,128)(2,1)S(1)}, bf16[24,1920]{1,0:T(8,128)(2,1)S(1)}, u32[]{:S(2)}, u32[]{:S(2)}) collective-permute-start(bf16[24,1920]{1,0:T(8,128)(2,1)S(1)} %get-tuple-element.46), channel_id=1, source_target_pairs={{0,4},{1,5},{2,6},{3,7},{4,0},{5,1},{6,2},{7,3},{8,12},{9,13},{10,... | collective-permute-start | bytes 276488 | tf_op jit(solution)/shard_map/ppermute | solution.py:318
  23.0 0.0 collective-permute-done.9.rest_3_
  23.0 2.3 %collective-permute-start.4 = (bf16[24,1920]{1,0:T(8,128)(2,1)S(1)}, bf16[24,1920]{1,0:T(8,128)(2,1)S(1)}, u32[]{:S(2)}, u32[]{:S(2)}) collective-permute-start(bf16[24,1920]{1,0:T(8,128)(2,1)S(1)} %get-tuple-element.47), channel_id=1, source_target_pairs={{0,7},{1,6},{2,5},{3,4},{4,3},{5,2},{6,1},{7,0},{8,15},{9,14},{10,... | collective-permute-start | bytes 276488 | tf_op jit(solution)/shard_map/ppermute | solution.py:318
  25.3 0.0 collective-permute-done.8.rest_2_
  25.3 1.9 %collective-permute-start.5 = (bf16[24,1920]{1,0:T(8,128)(2,1)S(1)}, bf16[24,1920]{1,0:T(8,128)(2,1)S(1)}, u32[]{:S(2)}, u32[]{:S(2)}) collective-permute-start(bf16[24,1920]{1,0:T(8,128)(2,1)S(1)} %get-tuple-element.48), channel_id=1, source_target_pairs={{0,1},{1,0},{2,3},{3,2},{4,5},{5,4},{6,7},{7,6},{8,9},{9,8},{10,11... | collective-permute-start | bytes 276488 | tf_op jit(solution)/shard_map/ppermute | solution.py:318
  27.2 3.3 %collective-permute-done.6.rest_0_ = bf16[24,1920]{1,0:T(8,128)(2,1)S(1)} collective-permute-done((bf16[24,1920]{1,0:T(8,128)(2,1)S(1)}, bf16[24,1920]{1,0:T(8,128)(2,1)S(1)}, u32[]{:S(2)}, u32[]{:S(2)}) %collective-permute-start.6) | collective-permute-done | bytes 92192 | tf_op jit(solution)/shard_map/ppermute | solution.py:318
  30.6 2.1 %expert_ffn.3 = (bf16[24,1920]{1,0:T(8,128)(2,1)S(1)}, bf16[24,1920]{1,0:T(8,128)(2,1)S(1)}, bf16[24,1920]{1,0:T(8,128)(2,1)S(1)}, bf16[24,1920]{1,0:T(8,128)(2,1)S(1)}) custom-call(bf16[1,2560,768]{2,1,0:T(8,128)(2,1)S(1)} %get-tuple-element.38.gate_ref, bf16[1,2560,768]{2,1,0:T(8,128)(2,1)S(1)} %get-tuple-element.42.up_ref, ...), custom_call_target="tpu_custom_call" | custom-call | flops 1132462080 | bytes 11796480 | tf_op jit(solution)/shard_map/expert_ffn/pallas_call | solution.py:418
  32.7 3.2 %collective-permute-start.10 = (bf16[24,1920]{1,0:T(8,128)(2,1)S(1)}, bf16[24,1920]{1,0:T(8,128)(2,1)S(1)}, u32[]{:S(2)}, u32[]{:S(2)}) collective-permute-start(bf16[24,1920]{1,0:T(8,128)(2,1)S(1)} %get-tuple-element.59), channel_id=1, source_target_pairs={{0,5},{1,4},{2,7},{3,6},{4,1},{5,0},{6,3},{7,2},{8,13},{9,12},{10,... | collective-permute-start | bytes 276488 | tf_op jit(solution)/shard_map/ppermute | solution.py:318
  36.0 1.7 %collective-permute-start.11 = (bf16[24,1920]{1,0:T(8,128)(2,1)S(1)}, bf16[24,1920]{1,0:T(8,128)(2,1)S(1)}, u32[]{:S(2)}, u32[]{:S(2)}) collective-permute-start(bf16[24,1920]{1,0:T(8,128)(2,1)S(1)} %get-tuple-element.60), channel_id=1, source_target_pairs={{0,6},{1,7},{2,4},{3,5},{4,2},{5,3},{6,0},{7,1},{8,14},{9,15},{10,... | collective-permute-start | bytes 276488 | tf_op jit(solution)/shard_map/ppermute | solution.py:318
  37.7 0.0 collective-permute-start.12
  37.7 0.0 collective-permute-done.4.rest_1_
  37.7 2.0 %collective-permute-start.13 = (bf16[24,1920]{1,0:T(8,128)(2,1)S(1)}, bf16[24,1920]{1,0:T(8,128)(2,1)S(1)}, u32[]{:S(2)}, u32[]{:S(2)}) collective-permute-start(bf16[24,1920]{1,0:T(8,128)(2,1)S(1)} %get-tuple-element.62), channel_id=1, source_target_pairs={{0,3},{1,2},{2,1},{3,0},{4,7},{5,6},{6,5},{7,4},{8,11},{9,10},{10,... | collective-permute-start | bytes 276488 | tf_op jit(solution)/shard_map/ppermute | solution.py:318
  39.7 1.3 %gate_weights.1 = (bf16[3,256,192]{2,1,0:T(8,128)(2,1)S(1)}, bf16[3,256,192]{2,1,0:T(8,128)(2,1)S(1)}) custom-call(s32[8]{0:T(128)} %holds_ref.1, s32[4]{0:T(128)} %dup_ref.1, s32[6,2,64]{2,1,0:T(2,128)} %bitcast.3, f32[6,2,64]{2,1,0:T(2,128)} %bitcast.4), custom_call_target="tpu_custom_call" | custom-call | bytes 4194304 | tf_op jit(solution)/shard_map/gate_weights/pallas_call | solution.py:437
  41.0 0.0 collective-permute-done.5.rest_2_
  41.0 0.5 %combine.2.base_ref = f32[2,64,2560]{2,1,0:T(8,128)S(1)} custom-call(f32[2,64,2560]{2,1,0:T(8,128)S(1)} %get-tuple-element.34.base_ref, bf16[3,256,192]{2,1,0:T(8,128)(2,1)S(1)} %get-tuple-element.37.mix_ref, bf16[24,1920]{1,0:T(8,128)(2,1)S(1)} %collective-permute-done.3.rest_0_, bf16[24,1920]{1,0:T(8,128)(2,1)S(1)} %collective-permute-done.4.rest_1_, ...), custom_call_target="tpu_custom_call" | custom-call | flops 251658240 | bytes 2621440 | tf_op jit(solution)/shard_map/combine/pallas_call | solution.py:454
  41.5 0.0 collective-permute-done.10.rest_0_
  41.5 0.9 %collective-permute-done.11.rest_1_ = bf16[24,1920]{1,0:T(8,128)(2,1)S(1)} collective-permute-done((bf16[24,1920]{1,0:T(8,128)(2,1)S(1)}, bf16[24,1920]{1,0:T(8,128)(2,1)S(1)}, u32[]{:S(2)}, u32[]{:S(2)}) %collective-permute-start.11) | collective-permute-done | bytes 92192 | tf_op jit(solution)/shard_map/ppermute | solution.py:318
  42.5 0.8 %collective-permute-done.12.rest_2_ = bf16[24,1920]{1,0:T(8,128)(2,1)S(1)} collective-permute-done((bf16[24,1920]{1,0:T(8,128)(2,1)S(1)}, bf16[24,1920]{1,0:T(8,128)(2,1)S(1)}, u32[]{:S(2)}, u32[]{:S(2)}) %collective-permute-start.12) | collective-permute-done | bytes 92192 | tf_op jit(solution)/shard_map/ppermute | solution.py:318
  43.2 1.0 %collective-permute-done.13.rest_3_ = bf16[24,1920]{1,0:T(8,128)(2,1)S(1)} collective-permute-done((bf16[24,1920]{1,0:T(8,128)(2,1)S(1)}, bf16[24,1920]{1,0:T(8,128)(2,1)S(1)}, u32[]{:S(2)}, u32[]{:S(2)}) %collective-permute-start.13) | collective-permute-done | bytes 92192 | tf_op jit(solution)/shard_map/ppermute | solution.py:318
  44.2 1.2 %combine.3 = bf16[2,64,2560]{2,1,0:T(8,128)(2,1)} custom-call(f32[2,64,2560]{2,1,0:T(8,128)S(1)} %combine.2.base_ref, bf16[3,256,192]{2,1,0:T(8,128)(2,1)S(1)} %get-tuple-element.50.mix_ref, bf16[24,1920]{1,0:T(8,128)(2,1)S(1)} %collective-permute-done.10.rest_0_, bf16[24,1920]{1,0:T(8,128)(2,1)S(1)} %collective-permute-done.11.rest_1_, ...), custom_call_target="tpu_custom_call" | custom-call | flops 251658240 | bytes 2621440 | tf_op jit(solution)/shard_map/combine/pallas_call | solution.py:454
  (3 shorter events, 0.0 us)
Async XLA Ops:
  3.0 13.3 %collective-permute-start = (bf16[24,1920]{1,0:T(8,128)(2,1)S(1)}, bf16[24,1920]{1,0:T(8,128)(2,1)S(1)}, u32[]{:S(2)}, u32[]{:S(2)}) collective-permute-start(bf16[24,1920]{1,0:T(8,128)(2,1)S(1)} %get-tuple-element.35), channel_id=1, source_target_pairs={{0,4},{1,5},{2,6},{3,7},{4,0},{5,1},{6,2},{7,3},{8,12},{9,13},{10,... | collective-permute-start | bytes 276488 | tf_op jit(solution)/shard_map/ppermute | solution.py:318
  7.1 10.8 %collective-permute-start.1 = (bf16[24,1920]{1,0:T(8,128)(2,1)S(1)}, bf16[24,1920]{1,0:T(8,128)(2,1)S(1)}, u32[]{:S(2)}, u32[]{:S(2)}) collective-permute-start(bf16[24,1920]{1,0:T(8,128)(2,1)S(1)} %get-tuple-element.44), channel_id=1, source_target_pairs={{0,7},{1,6},{2,5},{3,4},{4,3},{5,2},{6,1},{7,0},{8,15},{9,14},{10,... | collective-permute-start | bytes 276488 | tf_op jit(solution)/shard_map/ppermute | solution.py:318
  9.4 9.5 %collective-permute-start.2 = (bf16[24,1920]{1,0:T(8,128)(2,1)S(1)}, bf16[24,1920]{1,0:T(8,128)(2,1)S(1)}, u32[]{:S(2)}, u32[]{:S(2)}) collective-permute-start(bf16[24,1920]{1,0:T(8,128)(2,1)S(1)} %get-tuple-element.45), channel_id=1, source_target_pairs={{0,1},{1,0},{2,3},{3,2},{4,5},{5,4},{6,7},{7,6},{8,9},{9,8},{10,11... | collective-permute-start | bytes 276488 | tf_op jit(solution)/shard_map/ppermute | solution.py:318
  13.3 9.7 %collective-permute-start.9 = (bf16[24,1920]{1,0:T(8,128)(2,1)S(1)}, bf16[24,1920]{1,0:T(8,128)(2,1)S(1)}, u32[]{:S(2)}, u32[]{:S(2)}) collective-permute-start(bf16[24,1920]{1,0:T(8,128)(2,1)S(1)} %get-tuple-element.58), channel_id=1, source_target_pairs={{0,3},{1,2},{2,1},{3,0},{4,7},{5,6},{6,5},{7,4},{8,11},{9,10},{10,... | collective-permute-start | bytes 276488 | tf_op jit(solution)/shard_map/ppermute | solution.py:318
  13.9 11.4 %collective-permute-start.8 = (bf16[24,1920]{1,0:T(8,128)(2,1)S(1)}, bf16[24,1920]{1,0:T(8,128)(2,1)S(1)}, u32[]{:S(2)}, u32[]{:S(2)}) collective-permute-start(bf16[24,1920]{1,0:T(8,128)(2,1)S(1)} %get-tuple-element.56), channel_id=1, source_target_pairs={{0,2},{1,3},{2,0},{3,1},{4,6},{5,7},{6,4},{7,5},{8,10},{9,11},{10,... | collective-permute-start | bytes 276488 | tf_op jit(solution)/shard_map/ppermute | solution.py:318
  16.3 14.2 %collective-permute-start.6 = (bf16[24,1920]{1,0:T(8,128)(2,1)S(1)}, bf16[24,1920]{1,0:T(8,128)(2,1)S(1)}, u32[]{:S(2)}, u32[]{:S(2)}) collective-permute-start(bf16[24,1920]{1,0:T(8,128)(2,1)S(1)} %get-tuple-element.52), channel_id=1, source_target_pairs={{0,5},{1,4},{2,7},{3,6},{4,1},{5,0},{6,3},{7,2},{8,13},{9,12},{10,... | collective-permute-start | bytes 276488 | tf_op jit(solution)/shard_map/ppermute | solution.py:318
  18.0 12.6 %collective-permute-start.7 = (bf16[24,1920]{1,0:T(8,128)(2,1)S(1)}, bf16[24,1920]{1,0:T(8,128)(2,1)S(1)}, u32[]{:S(2)}, u32[]{:S(2)}) collective-permute-start(bf16[24,1920]{1,0:T(8,128)(2,1)S(1)} %get-tuple-element.54), channel_id=1, source_target_pairs={{0,6},{1,7},{2,4},{3,5},{4,2},{5,3},{6,0},{7,1},{8,14},{9,15},{10,... | collective-permute-start | bytes 276488 | tf_op jit(solution)/shard_map/ppermute | solution.py:318
  21.1 16.6 %collective-permute-start.3 = (bf16[24,1920]{1,0:T(8,128)(2,1)S(1)}, bf16[24,1920]{1,0:T(8,128)(2,1)S(1)}, u32[]{:S(2)}, u32[]{:S(2)}) collective-permute-start(bf16[24,1920]{1,0:T(8,128)(2,1)S(1)} %get-tuple-element.46), channel_id=1, source_target_pairs={{0,4},{1,5},{2,6},{3,7},{4,0},{5,1},{6,2},{7,3},{8,12},{9,13},{10,... | collective-permute-start | bytes 276488 | tf_op jit(solution)/shard_map/ppermute | solution.py:318
  23.0 14.7 %collective-permute-start.4 = (bf16[24,1920]{1,0:T(8,128)(2,1)S(1)}, bf16[24,1920]{1,0:T(8,128)(2,1)S(1)}, u32[]{:S(2)}, u32[]{:S(2)}) collective-permute-start(bf16[24,1920]{1,0:T(8,128)(2,1)S(1)} %get-tuple-element.47), channel_id=1, source_target_pairs={{0,7},{1,6},{2,5},{3,4},{4,3},{5,2},{6,1},{7,0},{8,15},{9,14},{10,... | collective-permute-start | bytes 276488 | tf_op jit(solution)/shard_map/ppermute | solution.py:318
  25.3 15.7 %collective-permute-start.5 = (bf16[24,1920]{1,0:T(8,128)(2,1)S(1)}, bf16[24,1920]{1,0:T(8,128)(2,1)S(1)}, u32[]{:S(2)}, u32[]{:S(2)}) collective-permute-start(bf16[24,1920]{1,0:T(8,128)(2,1)S(1)} %get-tuple-element.48), channel_id=1, source_target_pairs={{0,1},{1,0},{2,3},{3,2},{4,5},{5,4},{6,7},{7,6},{8,9},{9,8},{10,11... | collective-permute-start | bytes 276488 | tf_op jit(solution)/shard_map/ppermute | solution.py:318
  32.7 8.8 %collective-permute-start.10 = (bf16[24,1920]{1,0:T(8,128)(2,1)S(1)}, bf16[24,1920]{1,0:T(8,128)(2,1)S(1)}, u32[]{:S(2)}, u32[]{:S(2)}) collective-permute-start(bf16[24,1920]{1,0:T(8,128)(2,1)S(1)} %get-tuple-element.59), channel_id=1, source_target_pairs={{0,5},{1,4},{2,7},{3,6},{4,1},{5,0},{6,3},{7,2},{8,13},{9,12},{10,... | collective-permute-start | bytes 276488 | tf_op jit(solution)/shard_map/ppermute | solution.py:318
  36.0 6.5 %collective-permute-start.11 = (bf16[24,1920]{1,0:T(8,128)(2,1)S(1)}, bf16[24,1920]{1,0:T(8,128)(2,1)S(1)}, u32[]{:S(2)}, u32[]{:S(2)}) collective-permute-start(bf16[24,1920]{1,0:T(8,128)(2,1)S(1)} %get-tuple-element.60), channel_id=1, source_target_pairs={{0,6},{1,7},{2,4},{3,5},{4,2},{5,3},{6,0},{7,1},{8,14},{9,15},{10,... | collective-permute-start | bytes 276488 | tf_op jit(solution)/shard_map/ppermute | solution.py:318
  37.7 5.5 %collective-permute-start.12 = (bf16[24,1920]{1,0:T(8,128)(2,1)S(1)}, bf16[24,1920]{1,0:T(8,128)(2,1)S(1)}, u32[]{:S(2)}, u32[]{:S(2)}) collective-permute-start(bf16[24,1920]{1,0:T(8,128)(2,1)S(1)} %get-tuple-element.61), channel_id=1, source_target_pairs={{0,2},{1,3},{2,0},{3,1},{4,6},{5,7},{6,4},{7,5},{8,10},{9,11},{10,... | collective-permute-start | bytes 276488 | tf_op jit(solution)/shard_map/ppermute | solution.py:318
  37.7 6.5 %collective-permute-start.13 = (bf16[24,1920]{1,0:T(8,128)(2,1)S(1)}, bf16[24,1920]{1,0:T(8,128)(2,1)S(1)}, u32[]{:S(2)}, u32[]{:S(2)}) collective-permute-start(bf16[24,1920]{1,0:T(8,128)(2,1)S(1)} %get-tuple-element.62), channel_id=1, source_target_pairs={{0,3},{1,2},{2,1},{3,0},{4,7},{5,6},{6,5},{7,4},{8,11},{9,10},{10,... | collective-permute-start | bytes 276488 | tf_op jit(solution)/shard_map/ppermute | solution.py:318
